TPU v7x, 128 devices: a whole 4x4x4 slice. The times are simulated.
128 devices in a mesh: row: 16 (over z, y_hi, core), col: 8 (over y_lo, x).
Axes of the slice: x: 4, y: 4 (y_hi: 2, y_lo: 2; y = y_hi * 2 + y_lo), z: 4, core: 2. Of those that a mesh axis runs over, the one named last changes fastest.
Arguments:
- tokens: bfloat16 [32, 1024, 768], P('row', 'col'), may hold values from -6 to 6
- grad_out: bfloat16 [32, 1024, 768], P('row', 'col'), may hold values from -6 to 6
- w_qkv: bfloat16 [768, 2304], replicated, may hold values from -0.21875 to 0.21875
- w_out: bfloat16 [768, 768], replicated, may hold values from -0.21875 to 0.21875
- gain: float32 [768], replicated, may hold values from 0.5 to 1.5
- log_decay_rows: bfloat16 [2, 12, 32, 1024], P(None, None, 'row', 'col'), may hold values from -1 to 0, as said below
- log_decay_cols: bfloat16 [2, 12, 1024, 32], P(None, None, ('col', 'row')), may hold values from -1 to 0, as said below
- border_cols: int32 [1024], replicated, may hold values 0 or 1
- border_rows: int32 [32], replicated, may hold values 0 or 1
Outputs:
- grad_tokens: bfloat16 [32, 1024, 768], P('row', 'col')
- grad_qkv_weight: float32 [768, 2304], P(('row', 'col'))
- grad_out_weight: float32 [768, 768], P(('row', 'col'))
- grad_gain: float32 [768], P(('row', 'col'))
- grad_decay_rows: bfloat16 [2, 12, 32, 1024], P(None, None, 'row', 'col')
- grad_decay_cols: bfloat16 [2, 12, 1024, 32], P(None, None, ('col', 'row'))
Inputs may be any that keep to these rules, and one draw needn't show every extreme that they name: `log_decay_rows`: negative log decay of one scan step. `log_decay_cols`: negative log decay of one scan step. `border_cols`: tile border flags. `border_rows`: tile border flags.
All inputs are finite; a program needn't handle non-finite values.
Results may differ from a plain program's by a relative error of at most 0.014.
Values may be sent and summed in bfloat16 or wider, within the bound.
No kernel may reach another device: no remote copies, remote signals or barrier semaphores. Data moves between devices by JAX's collectives and lax.ppermute only.
A program may use at most 192 MiB of HBM per device.

v0:
```python
import functools

import jax
import jax.numpy as jnp
from jax import lax
from jax.sharding import PartitionSpec as P

EPSILON = 1e-05
HIGHEST = lax.Precision.HIGHEST


def entering_2(value, axis, join, neutral, backward):
    count = lax.axis_size(axis)
    place = lax.axis_index(axis)
    ahead = count - 1 - place if backward else place
    gathered = jax.tree.map(
        lambda a, kind: lax.all_gather(a.astype(kind), axis),
        value,
        jax.tree.map(lambda a: jnp.bfloat16 if a.dtype == jnp.float32 else a.dtype, value),
    )
    state = jax.tree.map(lambda a, e: jnp.zeros_like(a) + jnp.asarray(e, a.dtype), value, neutral)

    def one(hop, state):
        source = count - 1 - hop if backward else hop
        return join(
            state,
            jax.tree.map(
                lambda a, own: lax.dynamic_index_in_dim(a, source, 0, False).astype(own.dtype),
                gathered,
                value,
            ),
        )

    return lax.fori_loop(0, ahead, one, state)


def heads_of(packed, head_count):
    leading = packed.shape[:-1]
    model_width = packed.shape[-1] // 3
    pieces = packed.reshape(leading + (3, head_count, model_width // head_count))
    return (pieces[..., 0, :, :], pieces[..., 1, :, :], pieces[..., 2, :, :])


def reversed_borders(borders):
    return jnp.concatenate([borders[1:], jnp.zeros((1,), jnp.int32)])


def decay_factors(decays, resets):
    log_sums = jnp.cumsum(decays.astype(jnp.float32), axis=-1)
    segment = jnp.cumsum(resets, dtype=jnp.int32)
    entries = jnp.where(segment == 0, jnp.exp(log_sums), 0.0)
    tail_weight = jnp.where(segment == segment[-1], jnp.exp(log_sums[..., -1:] - log_sums), 0.0)
    return (log_sums, segment, entries, tail_weight)


def carry_term(query_wide, entries, carry_in, scaling):
    product = jnp.einsum("lthd,lhde->lthe", query_wide, carry_in, precision=HIGHEST)
    return product * (jnp.swapaxes(entries, 1, 2)[..., None] * scaling)


def state_update(key_wide, value_wide, tail_weight):
    weighted = key_wide * jnp.swapaxes(tail_weight, 1, 2)[..., None]
    return jnp.einsum("lshd,lshe->lhde", weighted, value_wide, precision=HIGHEST)


def block_scan(queries, key_heads, values, decays, resets, carry_in):
    scaling = queries.shape[-1] ** (-0.5)
    log_sums, segment, entries, tail_weight = decay_factors(decays, resets)
    positions = jnp.arange(resets.shape[0], dtype=jnp.int32)
    same_part = (segment[:, None] == segment[None, :]) & (positions[:, None] >= positions[None, :])
    spread = log_sums[..., :, None] - log_sums[..., None, :]
    weights = jnp.where(same_part, jnp.exp(jnp.where(same_part, spread, 0.0)), 0.0)
    query_wide = queries.astype(jnp.float32)
    key_wide = key_heads.astype(jnp.float32)
    value_wide = values.astype(jnp.float32)
    scores = jnp.einsum("lthd,lshd->lhts", query_wide, key_wide, precision=HIGHEST)
    within_block = jnp.einsum(
        "lhts,lshd->lthd", scores * weights * scaling, value_wide, precision=HIGHEST
    )
    carried = carry_term(query_wide, entries, carry_in, scaling)
    leaving = entries[..., -1][..., None, None] * carry_in + state_update(
        key_wide, value_wide, tail_weight
    )
    return (within_block + carried, leaving)


def down_up(projected, planes, border_rows):
    head_count = planes.shape[1]
    queries, key_heads, values = heads_of(jnp.swapaxes(projected, 0, 1), head_count)
    head_dim = queries.shape[-1]
    zero_state = jnp.zeros((queries.shape[0], head_count, head_dim, head_dim), jnp.float32)
    downward, _ = block_scan(
        queries, key_heads, values, jnp.swapaxes(planes[0], 0, 1), border_rows, zero_state
    )
    upward, _ = block_scan(
        queries[:, ::-1],
        key_heads[:, ::-1],
        values[:, ::-1],
        jnp.swapaxes(planes[1], 0, 1)[..., ::-1],
        reversed_borders(border_rows)[::-1],
        zero_state,
    )
    combined = downward + upward[:, ::-1]
    combined = combined.reshape(combined.shape[0], combined.shape[1], -1)
    return jnp.swapaxes(combined, 0, 1).astype(jnp.bfloat16)


def norm_part(mixed, gain):
    power = jnp.mean(mixed * mixed, axis=-1, keepdims=True)
    return mixed * lax.rsqrt(power + EPSILON) * gain


def row_inputs(projected, plane_log, resets, backward):
    queries, key_heads, values = heads_of(projected, plane_log.shape[0])
    decays = jnp.swapaxes(plane_log, 0, 1)
    if backward:
        return (
            queries[:, ::-1],
            key_heads[:, ::-1],
            values[:, ::-1],
            decays[..., ::-1],
            resets[::-1],
        )
    return (queries, key_heads, values, decays, resets)


def row_block(projected, plane_log, carry_in, resets, backward):
    queries, key_heads, values, decays, scan_order = row_inputs(
        projected, plane_log, resets, backward
    )
    result, leaving = block_scan(queries, key_heads, values, decays, scan_order, carry_in)
    if backward:
        result = result[:, ::-1]
    return (result.reshape(result.shape[0], result.shape[1], -1), leaving)


def row_summary(projected, plane_log, resets, backward):
    queries, key_heads, values, decays, scan_order = row_inputs(
        projected, plane_log, resets, backward
    )
    _, _, entries, tail_weight = decay_factors(decays, scan_order)
    update = state_update(key_heads.astype(jnp.float32), values.astype(jnp.float32), tail_weight)
    return (entries[..., -1], update)


def row_adjoint(projected, plane_log, resets, backward, cotangent):
    queries, key_heads, values, decays, scan_order = row_inputs(
        projected, plane_log, resets, backward
    )
    _, _, entries, _ = decay_factors(decays, scan_order)
    cot_heads = cotangent.reshape(queries.shape)
    if backward:
        cot_heads = cot_heads[:, ::-1]
    scaling = queries.shape[-1] ** (-0.5)
    factor = jnp.swapaxes(entries, 1, 2)[..., None] * scaling
    return jnp.einsum(
        "lthd,lthe->lhde", queries.astype(jnp.float32), cot_heads * factor, precision=HIGHEST
    )


def merge_steps(earlier, later):
    return (earlier[0] * later[0], later[0][..., None, None] * earlier[1] + later[1])


def chain(through, update, backward):
    identity = (jnp.ones_like(through), jnp.zeros_like(update))
    combined = entering_2((through, update), "col", merge_steps, identity, backward)
    return combined[1]


def to_columns(tile_data):
    return lax.all_to_all(tile_data, "row", split_axis=1, concat_axis=0, tiled=True)


def from_columns(column_data):
    return lax.all_to_all(column_data, "row", split_axis=0, concat_axis=1, tiled=True)


def per_device(
    tokens, grad_out, w_qkv, w_out, gain, log_decay_rows, log_decay_cols, border_cols, border_rows
):
    row_count, col_count, model_width = tokens.shape
    token_total = row_count * col_count * lax.axis_size("row") * lax.axis_size("col")
    flat_tokens = tokens.reshape(row_count * col_count, model_width)
    projected = jnp.dot(flat_tokens, w_qkv, preferred_element_type=jnp.float32).astype(jnp.bfloat16)
    projected = projected.reshape(row_count, col_count, 3 * model_width)
    col_start = lax.axis_index("col") * col_count
    forward_borders = lax.dynamic_slice_in_dim(border_cols, col_start, col_count)
    backward_borders = lax.dynamic_slice_in_dim(reversed_borders(border_cols), col_start, col_count)
    border_pair = (forward_borders, backward_borders)
    pullbacks = []
    throughs = []
    mixed = jnp.zeros((row_count, col_count, model_width), jnp.float32)
    for direction in range(2):
        backward = direction == 1
        through, update = row_summary(
            projected, log_decay_rows[direction], border_pair[direction], backward
        )
        entering = chain(through, update, backward)
        scanner = functools.partial(row_block, resets=border_pair[direction], backward=backward)
        (row_result, _), pullback = jax.vjp(scanner, projected, log_decay_rows[direction], entering)
        mixed = mixed + row_result
        pullbacks.append(pullback)
        throughs.append(through)
    column_qkv = to_columns(projected)
    column_result, column_pull = jax.vjp(
        functools.partial(down_up, border_rows=border_rows), column_qkv, log_decay_cols
    )
    mixed = mixed + from_columns(column_result).astype(jnp.float32)
    normed_value, norm_pull = jax.vjp(norm_part, mixed, gain)
    normed = normed_value.astype(jnp.bfloat16)
    flat_grad = grad_out.reshape(row_count * col_count, model_width)
    d_normed = jnp.dot(flat_grad, w_out.T, preferred_element_type=jnp.float32).astype(jnp.bfloat16)
    d_normed = lax.optimization_barrier(d_normed).astype(jnp.float32)
    d_mixed, d_gain = norm_pull(d_normed.reshape(row_count, col_count, model_width))
    d_out_weight = jnp.dot(
        normed.reshape(-1, model_width).T, flat_grad, preferred_element_type=jnp.float32
    )
    row_grads = []
    plane_grads = []
    for direction in range(2):
        backward = direction == 1
        entry_part = row_adjoint(
            projected, log_decay_rows[direction], border_pair[direction], backward, d_mixed
        )
        leaving = chain(throughs[direction], entry_part, not backward)
        grad_qkv, grad_plane, _ = pullbacks[direction]((d_mixed, leaving))
        row_grads.append(grad_qkv)
        plane_grads.append(grad_plane)
    row_qkv = row_grads[0] + row_grads[1]
    grad_decay_rows = jnp.stack(plane_grads)
    column_grad = to_columns(d_mixed.astype(jnp.bfloat16))
    column_dqkv, grad_decay_cols = column_pull(column_grad)
    col_flat = from_columns(column_dqkv).reshape(-1, 3 * model_width)
    col_tokens = jnp.dot(col_flat, w_qkv.T, preferred_element_type=jnp.float32).astype(jnp.bfloat16)
    col_tokens = lax.optimization_barrier(col_tokens)
    col_weight = jnp.dot(flat_tokens.T, col_flat, preferred_element_type=jnp.float32)
    row_flat = row_qkv.reshape(-1, 3 * model_width)
    grad_tokens = jnp.dot(
        row_flat, w_qkv.T, preferred_element_type=jnp.float32
    ) + col_tokens.astype(jnp.float32)
    grad_tokens = grad_tokens.astype(jnp.bfloat16).reshape(row_count, col_count, model_width)
    d_qkv_weight = jnp.dot(flat_tokens.T, row_flat, preferred_element_type=jnp.float32) + col_weight
    weight_part, out_part, gain_part = (
        lax.psum_scatter(d_qkv_weight, ("row", "col"), scatter_dimension=0, tiled=True),
        lax.psum_scatter(d_out_weight, ("row", "col"), scatter_dimension=0, tiled=True),
        lax.psum_scatter(d_gain, ("row", "col"), scatter_dimension=0, tiled=True),
    )
    scaling = float(token_total) ** (-0.5)
    return (
        grad_tokens,
        weight_part * scaling,
        out_part * scaling,
        gain_part * scaling,
        grad_decay_rows,
        grad_decay_cols,
    )


def solution(mesh):
    in_specs = (
        P("row", "col", None),
        P("row", "col", None),
        P(),
        P(),
        P(),
        P(None, None, "row", "col"),
        P(None, None, ("col", "row"), None),
        P(),
        P(),
    )
    out_specs = (
        P("row", "col", None),
        P(("row", "col"), None),
        P(("row", "col"), None),
        P(("row", "col")),
        P(None, None, "row", "col"),
        P(None, None, ("col", "row"), None),
    )
    return jax.shard_map(
        per_device, mesh=mesh, in_specs=in_specs, out_specs=out_specs, check_vma=False
    )
```

profile of v0, /device:TPU:0, one launch (start us, length us, event | category | flops | bytes accessed | tf_op | source)
XLA Modules:
  0.0 1063.4 jit_solution(15337717268205216932)
XLA Ops:
  36.0 8.2 all-to-all-start
  92.2 4.7 reduce_window_sum.97
  96.9 4.7 reduce_window_sum.98
  111.5 4.6 reshape.374
  147.9 4.2 fusion.14
  157.9 7.3 all-to-all-start.1
  172.6 18.2 %all-gather.2 = bf16[16,12,1]{1,2,0:T(2,128)(2,1)S(1)} all-gather(bf16[2,12,1]{1,2,0:T(2,128)(2,1)} %copy.219), channel_id=4, replica_groups=mesh['row'=16,'col'=8] {'col'}, dimensions={0}, use_global_device_ids=true | all-gather | bytes 432 | tf_op jit(solution)/shard_map/all_gather | solution.py:17
  194.1 15.4 %all-gather = bf16[16,12,1]{1,2,0:T(2,128)(2,1)S(1)} all-gather(bf16[2,12,1]{1,2,0:T(2,128)(2,1)} %copy.209), channel_id=2, replica_groups=mesh['row'=16,'col'=8] {'col'}, dimensions={0}, use_global_device_ids=true | all-gather | bytes 432 | tf_op jit(solution)/shard_map/all_gather | solution.py:17
  232.2 20.6 %while.53 = (s32[]{:T(128)}, f32[2,12,64,64]{3,2,1,0:T(8,128)}, s32[]{:T(128)}, bf16[8,2,12]{2,1,0:T(2,128)(2,1)}, bf16[8,2,12,64,64]{4,3,2,1,0:T(8,128)(2,1)}, ...) while((s32[]{:T(128)}, f32[2,12,64,64]{3,2,1,0:T(8,128)}, s32[]{:T(128)}, bf16[8,2,12]{2,1,0:T(2,128)(2,1)}, ...), condition=%wide.region_7.8_spmd, body=%wide.region_6.7_spmd.sunk | while | flops 294942 | bytes 983435 | solution.py:34
  261.6 5.3 multiply_reduce_fusion.5
  281.3 7.8 all-to-all-start.2
  294.7 338.7 %fusion = f32[8,768]{1,0:T(8,128)} fusion(f32[768,768]{1,0:T(8,128)} %convolution_bitcast_fusion), kind=kCustom, calls=%all-reduce-scatter | all-reduce-scatter fusion | flops 786433 | bytes 2383872
  647.7 5.5 fusion.189
  657.5 5.0 fusion.193
  670.9 6.2 fusion.38
  695.7 4.5 fusion.43
  707.2 4.8 reshape.343
  714.9 4.4 all-to-all-start.3
  730.9 4.6 collective-permute-start.31
  735.4 4.6 fusion.187
  754.0 20.6 %while.54 = (s32[]{:T(128)}, f32[2,12,64,64]{3,2,1,0:T(8,128)}, s32[]{:T(128)}, bf16[8,2,12]{2,1,0:T(2,128)(2,1)}, bf16[8,2,12,64,64]{4,3,2,1,0:T(8,128)(2,1)}, ...) while((s32[]{:T(128)}, f32[2,12,64,64]{3,2,1,0:T(8,128)}, s32[]{:T(128)}, bf16[8,2,12]{2,1,0:T(2,128)(2,1)}, ...), condition=%wide.region_15.16_spmd, body=%wide.region_14.15_spmd.sunk | while | flops 294942 | bytes 983435 | solution.py:34
  793.6 5.0 collective-permute-start.26
  798.6 5.6 collective-permute-start.25
  809.8 8.3 collective-permute-start.22
  831.2 4.1 collective-permute-start.16
  837.4 4.1 fusion.1
  849.6 5.0 collective-permute-start.10
  871.2 62.5 %all-reduce.17 = f32[768]{0:T(1024)} all-reduce(f32[768]{0:T(1024)} %fusion.86), channel_id=10, replica_groups=mesh['row'=16,'col'=8] {'row','col'}, use_global_device_ids=true, to_apply=%region_21.22.clone | all-reduce | flops 768 | bytes 6144
  940.3 4.0 collective-permute-start.2
  951.0 47.1 %concatenate.8 = f32[262,768]{1,0:T(8,128)} concatenate(f32[6,768]{1,0:T(8,128)} %collective-permute-done.31, f32[8,768]{1,0:T(8,128)} %collective-permute-done.30, f32[8,768]{1,0:T(8,128)} %collective-permute-done.29, f32[8,768]{1,0:T(8,128)} %collective-permute-done.28, f32[8,768]{1,0:T(8,128)} %collective-permute-done.27, f32[8,768]{1,0:T(8,128)} %copy-done.82, ...), dimensions={0} | concatenate | bytes 1609728
  1002.7 4.9 reduce_window_sum.101
  1012.1 4.9 reduce_window_sum.102
  (487 shorter events, 434.1 us)
Async XLA Ops:
  7.2 220.1 %all-gather.11.cloned.1.call-start = ((), (), s32[]{:S(2)}) async-start(), calls=%async_computation.4 | async-start | bytes 3538944 | tf_op jit(solution)/shard_map/all_gather | solution.py:17
  36.0 72.9 %all-to-all-start = ((bf16[2,128,2304]{2,0,1:T(2,128)(2,1)}), bf16[2,128,2304]{2,0,1:T(2,128)(2,1)}, u32[]{:S(2)}, u32[]{:S(2)}) async-start(bf16[2,128,2304]{2,0,1:T(2,128)(2,1)} %copy.221), calls=%async_computation | async-start | bytes 2359296 | tf_op jit(solution)/shard_map/all_to_all | solution.py:172
  44.2 187.0 %all-gather.13.cloned.1.call-start = ((), (), s32[]{:S(2)}) async-start(), calls=%async_computation.5 | async-start | bytes 3538944 | tf_op jit(solution)/shard_map/all_gather | solution.py:17
  157.9 61.3 %all-to-all-start.1 = ((bf16[32,8,768]{2,1,0:T(8,128)(2,1)}), bf16[32,8,768]{2,1,0:T(8,128)(2,1)}, u32[]{:S(2)}, u32[]{:S(2)}) async-start(bf16[32,8,768]{2,1,0:T(8,128)(2,1)} %copy.233), calls=%async_computation.1 | async-start | bytes 786432 | tf_op jit(solution)/shard_map/all_to_all | solution.py:176
  165.2 581.1 %all-gather.17.cloned.1.call-start = ((), (), s32[]{:S(2)}) async-start(), calls=%async_computation.7 | async-start | bytes 3538944 | tf_op jit(solution)/shard_map/all_gather | solution.py:17
  281.3 371.8 %all-to-all-start.2 = ((bf16[2,128,768]{2,0,1:T(2,128)(2,1)}), bf16[2,128,768]{2,0,1:T(2,128)(2,1)}, u32[]{:S(2)}, u32[]{:S(2)}) async-start(bf16[2,128,768]{2,0,1:T(2,128)(2,1)} %copy.241), calls=%async_computation.2 | async-start | bytes 786432 | tf_op jit(solution)/shard_map/all_to_all | solution.py:172
  289.1 463.9 %all-gather.15.cloned.1.call-start = ((), (), s32[]{:S(2)}) async-start(), calls=%async_computation.6 | async-start | bytes 3538944 | tf_op jit(solution)/shard_map/all_gather | solution.py:17
  640.1 158.5 %collective-permute-start.30 = (f32[8,768]{1,0:T(8,128)}, f32[8,768]{1,0:T(8,128)}, u32[]{:S(2)}, u32[]{:S(2)}) collective-permute-start(f32[8,768]{1,0:T(8,128)} %fusion), channel_id=1, source_target_pairs={{0,31},{1,32},{2,33},{3,34},{4,35},{5,36},{6,37},{7,38},{8,39},{9,... | collective-permute-start | bytes 73736
  642.0 164.2 %collective-permute-start.29 = (f32[8,768]{1,0:T(8,128)}, f32[8,768]{1,0:T(8,128)}, u32[]{:S(2)}, u32[]{:S(2)}) collective-permute-start(f32[8,768]{1,0:T(8,128)} %fusion), channel_id=1, source_target_pairs={{0,30},{1,31},{2,32},{3,33},{4,34},{5,35},{6,36},{7,37},{8,38},{9,... | collective-permute-start | bytes 73736
  643.9 163.7 %collective-permute-start.28 = (f32[8,768]{1,0:T(8,128)}, f32[8,768]{1,0:T(8,128)}, u32[]{:S(2)}, u32[]{:S(2)}) collective-permute-start(f32[8,768]{1,0:T(8,128)} %fusion), channel_id=1, source_target_pairs={{0,29},{1,30},{2,31},{3,32},{4,33},{5,34},{6,35},{7,36},{8,37},{9,... | collective-permute-start | bytes 73736
  645.7 164.1 %collective-permute-start.27 = (f32[8,768]{1,0:T(8,128)}, f32[8,768]{1,0:T(8,128)}, u32[]{:S(2)}, u32[]{:S(2)}) collective-permute-start(f32[8,768]{1,0:T(8,128)} %fusion), channel_id=1, source_target_pairs={{0,28},{1,29},{2,30},{3,31},{4,32},{5,33},{6,34},{7,35},{8,36},{9,... | collective-permute-start | bytes 73736
  714.9 29.0 %all-to-all-start.3 = ((bf16[32,8,2304]{2,1,0:T(8,128)(2,1)}), bf16[32,8,2304]{2,1,0:T(8,128)(2,1)}, u32[]{:S(2)}, u32[]{:S(2)}) async-start(bf16[32,8,2304]{2,1,0:T(8,128)(2,1)} %copy.252), calls=%async_computation.3 | async-start | bytes 2359296 | tf_op jit(solution)/shard_map/all_to_all | solution.py:176
  719.3 331.7 %all-reduce.21.cloned.1.call-start = ((), (), s32[]{:S(2)}) async-start(), calls=%async_computation.8 | async-start | bytes 14155776
  730.9 62.8 %collective-permute-start.31 = (f32[6,768]{1,0:T(8,128)}, f32[6,768]{1,0:T(8,128)}, u32[]{:S(2)}, u32[]{:S(2)}) collective-permute-start(f32[6,768]{1,0:T(8,128)} %slice.105), channel_id=1, source_target_pairs={{0,32},{1,33},{2,34},{3,35},{4,36},{5,37},{6,38},{7,39},{8,40},{9,... | collective-permute-start | bytes 55304
  793.6 24.5 %collective-permute-start.26 = (f32[8,768]{1,0:T(8,128)}, f32[8,768]{1,0:T(8,128)S(1)}, u32[]{:S(2)}, u32[]{:S(2)}) collective-permute-start(f32[8,768]{1,0:T(8,128)} %fusion), channel_id=1, source_target_pairs={{0,27},{1,28},{2,29},{3,30},{4,31},{5,32},{6,33},{7,34},{8,35},{9,... | collective-permute-start | bytes 73736
  798.6 21.3 %collective-permute-start.25 = (f32[8,768]{1,0:T(8,128)}, f32[8,768]{1,0:T(8,128)S(1)}, u32[]{:S(2)}, u32[]{:S(2)}) collective-permute-start(f32[8,768]{1,0:T(8,128)} %fusion), channel_id=1, source_target_pairs={{0,26},{1,27},{2,28},{3,29},{4,30},{5,31},{6,32},{7,33},{8,34},{9,... | collective-permute-start | bytes 73736
  806.2 17.8 %collective-permute-start.24 = (f32[8,768]{1,0:T(8,128)}, f32[8,768]{1,0:T(8,128)S(1)}, u32[]{:S(2)}, u32[]{:S(2)}) collective-permute-start(f32[8,768]{1,0:T(8,128)} %fusion), channel_id=1, source_target_pairs={{0,25},{1,26},{2,27},{3,28},{4,29},{5,30},{6,31},{7,32},{8,33},{9,... | collective-permute-start | bytes 73736
  807.6 18.8 %collective-permute-start.23 = (f32[8,768]{1,0:T(8,128)}, f32[8,768]{1,0:T(8,128)}, u32[]{:S(2)}, u32[]{:S(2)}) collective-permute-start(f32[8,768]{1,0:T(8,128)} %fusion), channel_id=1, source_target_pairs={{0,24},{1,25},{2,26},{3,27},{4,28},{5,29},{6,30},{7,31},{8,32},{9,... | collective-permute-start | bytes 73736
  809.8 19.5 %collective-permute-start.22 = (f32[8,768]{1,0:T(8,128)}, f32[8,768]{1,0:T(8,128)}, u32[]{:S(2)}, u32[]{:S(2)}) collective-permute-start(f32[8,768]{1,0:T(8,128)} %fusion), channel_id=1, source_target_pairs={{0,23},{1,24},{2,25},{3,26},{4,27},{5,28},{6,29},{7,30},{8,31},{9,... | collective-permute-start | bytes 73736
  824.6 17.0 %collective-permute-start.19 = (f32[8,768]{1,0:T(8,128)}, f32[8,768]{1,0:T(8,128)}, u32[]{:S(2)}, u32[]{:S(2)}) collective-permute-start(f32[8,768]{1,0:T(8,128)} %fusion), channel_id=1, source_target_pairs={{0,20},{1,21},{2,22},{3,23},{4,24},{5,25},{6,26},{7,27},{8,28},{9,... | collective-permute-start | bytes 73736
  826.5 17.5 %collective-permute-start.18 = (f32[8,768]{1,0:T(8,128)}, f32[8,768]{1,0:T(8,128)}, u32[]{:S(2)}, u32[]{:S(2)}) collective-permute-start(f32[8,768]{1,0:T(8,128)} %fusion), channel_id=1, source_target_pairs={{0,19},{1,20},{2,21},{3,22},{4,23},{5,24},{6,25},{7,26},{8,27},{9,... | collective-permute-start | bytes 73736
  829.3 16.6 %collective-permute-start.17 = (f32[8,768]{1,0:T(8,128)}, f32[8,768]{1,0:T(8,128)}, u32[]{:S(2)}, u32[]{:S(2)}) collective-permute-start(f32[8,768]{1,0:T(8,128)} %fusion), channel_id=1, source_target_pairs={{0,18},{1,19},{2,20},{3,21},{4,22},{5,23},{6,24},{7,25},{8,26},{9,... | collective-permute-start | bytes 73736
  831.2 16.5 %collective-permute-start.16 = (f32[8,768]{1,0:T(8,128)}, f32[8,768]{1,0:T(8,128)}, u32[]{:S(2)}, u32[]{:S(2)}) collective-permute-start(f32[8,768]{1,0:T(8,128)} %fusion), channel_id=1, source_target_pairs={{0,17},{1,18},{2,19},{3,20},{4,21},{5,22},{6,23},{7,24},{8,25},{9,... | collective-permute-start | bytes 73736
  843.9 15.8 %collective-permute-start.13 = (f32[8,768]{1,0:T(8,128)}, f32[8,768]{1,0:T(8,128)}, u32[]{:S(2)}, u32[]{:S(2)}) collective-permute-start(f32[8,768]{1,0:T(8,128)} %fusion), channel_id=1, source_target_pairs={{0,14},{1,15},{2,16},{3,17},{4,18},{5,19},{6,20},{7,21},{8,22},{9,... | collective-permute-start | bytes 73736
  845.8 15.8 %collective-permute-start.12 = (f32[8,768]{1,0:T(8,128)}, f32[8,768]{1,0:T(8,128)}, u32[]{:S(2)}, u32[]{:S(2)}) collective-permute-start(f32[8,768]{1,0:T(8,128)} %fusion), channel_id=1, source_target_pairs={{0,13},{1,14},{2,15},{3,16},{4,17},{5,18},{6,19},{7,20},{8,21},{9,... | collective-permute-start | bytes 73736
  849.6 17.1 %collective-permute-start.10 = (f32[8,768]{1,0:T(8,128)}, f32[8,768]{1,0:T(8,128)}, u32[]{:S(2)}, u32[]{:S(2)}) collective-permute-start(f32[8,768]{1,0:T(8,128)} %fusion), channel_id=1, source_target_pairs={{0,11},{1,12},{2,13},{3,14},{4,15},{5,16},{6,17},{7,18},{8,19},{9,... | collective-permute-start | bytes 73736
  856.9 76.8 %collective-permute-start.9 = (f32[8,768]{1,0:T(8,128)}, f32[8,768]{1,0:T(8,128)}, u32[]{:S(2)}, u32[]{:S(2)}) collective-permute-start(f32[8,768]{1,0:T(8,128)} %fusion), channel_id=1, source_target_pairs={{0,10},{1,11},{2,12},{3,13},{4,14},{5,15},{6,16},{7,17},{8,18},{9,... | collective-permute-start | bytes 73736
  859.7 76.7 %collective-permute-start.8 = (f32[8,768]{1,0:T(8,128)}, f32[8,768]{1,0:T(8,128)}, u32[]{:S(2)}, u32[]{:S(2)}) collective-permute-start(f32[8,768]{1,0:T(8,128)} %fusion), channel_id=1, source_target_pairs={{0,9},{1,10},{2,11},{3,12},{4,13},{5,14},{6,15},{7,16},{8,17},{9,1... | collective-permute-start | bytes 73736
  861.6 78.7 %collective-permute-start.7 = (f32[8,768]{1,0:T(8,128)}, f32[8,768]{1,0:T(8,128)}, u32[]{:S(2)}, u32[]{:S(2)}) collective-permute-start(f32[8,768]{1,0:T(8,128)} %fusion), channel_id=1, source_target_pairs={{0,8},{1,9},{2,10},{3,11},{4,12},{5,13},{6,14},{7,15},{8,16},{9,17... | collective-permute-start | bytes 73736
  863.5 80.9 %collective-permute-start.6 = (f32[8,768]{1,0:T(8,128)}, f32[8,768]{1,0:T(8,128)}, u32[]{:S(2)}, u32[]{:S(2)}) collective-permute-start(f32[8,768]{1,0:T(8,128)} %fusion), channel_id=1, source_target_pairs={{0,7},{1,8},{2,9},{3,10},{4,11},{5,12},{6,13},{7,14},{8,15},{9,16}... | collective-permute-start | bytes 73736
  866.7 80.2 %collective-permute-start.5 = (f32[8,768]{1,0:T(8,128)}, f32[8,768]{1,0:T(8,128)}, u32[]{:S(2)}, u32[]{:S(2)}) collective-permute-start(f32[8,768]{1,0:T(8,128)} %fusion), channel_id=1, source_target_pairs={{0,6},{1,7},{2,8},{3,9},{4,10},{5,11},{6,12},{7,13},{8,14},{9,15},... | collective-permute-start | bytes 73736
  933.8 17.2 %collective-permute-start.4 = (f32[8,768]{1,0:T(8,128)}, f32[8,768]{1,0:T(8,128)}, u32[]{:S(2)}, u32[]{:S(2)}) collective-permute-start(f32[8,768]{1,0:T(8,128)} %fusion), channel_id=1, source_target_pairs={{0,5},{1,6},{2,7},{3,8},{4,9},{5,10},{6,11},{7,12},{8,13},{9,14},{... | collective-permute-start | bytes 73736
  (109 other events, 527.8 us)
Sparse Core Ops, SparseCore 0:
  32.6 46.9 all-gather.10
  81.2 43.7 all-gather.12
  274.3 45.9 all-gather.16
  647.8 42.5 all-gather.14
  841.7 154.5 all-reduce.20
where the time goes:
time: 1080 us; the launch traced here: 1060 us
  blocking collectives  435 us (40%)
  local copies, waits for them, and re-layouts  218 us (20%)
  other arithmetic  137 us (13%)
  matrix products  135 us (12%)
  starting transfers between devices  123 us (11%)
  between operations  15.3 us (1%)
    unnamed x2, blocking collectives  401 us
    unnamed x33, starting transfers between devices  94.7 us
    unnamed x210, local copies, waits for them, and re-layouts  64.7 us
    dot_general x12, matrix products, block_scan(): jnp.einsum('lhts,lshd->lthd', scores * weights * scaling, value_wide, pre...  50.7 us
    all_gather x2, blocking collectives, entering_2(): lax.all_gather(a.astype(kind), axis)  33.6 us
    add x14, other arithmetic, merge_steps(): later[0][..., None, None] * earlier[1] + later[1]  32 us
    another operation x8, other arithmetic, decay_factors(): log_sums = jnp.cumsum(decays.astype(jnp.float32), axis=-1)  29.2 us
    dot_general x12, matrix products, block_scan(): jnp.einsum('lthd,lshd->lhts', query_wide, key_wide, precision=HIGHEST)  26.1 us
  transfers between devices with their start and end apart: 41, of which 0 were waited for; matrix products, arithmetic and copies ran while one was open for 71% of the time, Pallas kernels for 0%

commit v1 on v0

v1 whole, which is shorter than its diff:
```python
import functools

import jax
import jax.numpy as jnp
from jax import lax
from jax.experimental import pallas as pl
from jax.experimental.pallas import tpu as pltpu
from jax.sharding import PartitionSpec as P

EPSILON = 1e-05
HEADS = 12
HEAD_DIM = 64
PAIRS = HEADS // 2
D = 768
F = 3 * D
ROWS = 2
COLS = 128
TOK = ROWS * COLS
GRID_H = 32
CD = 8
SCALE = HEAD_DIM ** (-0.5)
WIDE = F + D + 128
F32 = jnp.float32
BF = jnp.bfloat16
EVEN_ODD = [list(range(0, 16, 2)), list(range(1, 16, 2))]
CORE_SWAP = [(i, i ^ 1) for i in range(16)]


def call(body, outs, *args, smem=()):
    specs = [
        pl.BlockSpec(memory_space=pltpu.SMEM if n in smem else pltpu.VMEM) for n in range(len(args))
    ]
    return pl.pallas_call(
        body,
        out_shape=[jax.ShapeDtypeStruct(s, t) for s, t in outs],
        in_specs=specs,
        out_specs=[pl.BlockSpec(memory_space=pltpu.VMEM)] * len(outs),
        compiler_params=pltpu.CompilerParams(vmem_limit_bytes=56 * 1024 * 1024),
    )(*args)


def iota(shape, dim):
    return lax.broadcasted_iota(jnp.int32, shape, dim)


def nn(a, b):
    return lax.dot_general(a, b, (((1,), (0,)), ((), ())), preferred_element_type=F32)


def nt(a, b):
    return lax.dot_general(a, b, (((1,), (1,)), ((), ())), preferred_element_type=F32)


def tn(a, b):
    return lax.dot_general(a, b, (((0,), (0,)), ((), ())), preferred_element_type=F32)


def left_half(shape):
    return iota(shape, len(shape) - 1) < HEAD_DIM


def split_heads(x):
    mask = left_half(x.shape)
    zero = jnp.zeros_like(x)
    return jnp.concatenate([jnp.where(mask, x, zero), jnp.where(mask, zero, x)], axis=0)


def side(x):
    half = x.shape[0] // 2
    return jnp.concatenate([x[:half], x[half:]], axis=1)


def lanes_of(fac, p):
    shape = (fac.shape[0], 128)
    return jnp.where(left_half(shape), fac[:, 2 * p : 2 * p + 1], fac[:, 2 * p + 1 : 2 * p + 2])


def compact(m):
    return jnp.where(left_half((HEAD_DIM, 128)), m[:HEAD_DIM], m[HEAD_DIM:])


def block_of(ref, direction, r, p):
    n = direction * ROWS * PAIRS + r * PAIRS + p
    return n // 3, (n % 3) * HEAD_DIM


def weights(col_r, row_r, col_l, row_l, lower, mask):
    return jnp.exp(jnp.where(lower, col_r - row_r, col_l - row_l)) * mask


def prep_kernel(ldr_ref, ldc_ref, bc_ref, br_ref, wr_ref, wc_ref, fac_ref, th_ref):
    i0, i1 = iota((COLS, COLS), 0), iota((COLS, COLS), 1)
    le, ge = (i0 <= i1).astype(BF), (i0 >= i1).astype(BF)
    lower = i0 >= i1
    b = bc_ref[...].astype(F32)
    b8 = jnp.broadcast_to(b[0:1], (8, COLS)).astype(BF)
    seg_row = nn(b8, le)[0:1]
    seg_col = nt(ge, b8)[:, 0:1]
    first, last = seg_row[:, 0:1], seg_row[:, COLS - 1 : COLS]
    after = last + b[1:2, 0:1]
    mask = jnp.where(seg_col == seg_row, jnp.where(i0 == i1, 2.0 * SCALE, SCALE), 0.0)
    th_ref[...] = jnp.zeros_like(th_ref)
    for r in range(ROWS):
        lr, ll = ldr_ref[r, 0], ldr_ref[r, 1]
        row_r, row_l = nn(lr, le), nn(ll, ge)
        col_r, col_l = nt(ge, lr), nt(le, ll)
        for h in range(HEADS):
            w = weights(col_r[:, h : h + 1], row_r[h : h + 1], col_l[:, h : h + 1], row_l[h : h + 1], lower, mask)
            wr_ref[r * PAIRS + h // 2, (h % 2) * COLS : (h % 2 + 1) * COLS, :] = w
        fac_ref[0, r] = jnp.where(seg_col == 0.0, jnp.exp(col_r), 0.0) * SCALE
        fac_ref[1, r] = jnp.where(seg_col == after, jnp.exp(col_l), 0.0) * SCALE
        fac_ref[2, r] = jnp.where(seg_col == last, jnp.exp(col_r[COLS - 1 : COLS] - col_r), 0.0)
        fac_ref[3, r] = jnp.where(seg_col == first, jnp.exp(col_l[0:1] - col_l), 0.0)
        th_r = jnp.where(last == 0.0, jnp.exp(row_r[:, COLS - 1 : COLS]), 0.0)
        th_l = jnp.where(after == first, jnp.exp(row_l[:, 0:1]), 0.0)
        for direction, th in enumerate((th_r, th_l)):
            for p in range(PAIRS):
                n = direction * ROWS * PAIRS + r * PAIRS + p
                both = jnp.where(left_half((1, 128)), th[2 * p : 2 * p + 1], th[2 * p + 1 : 2 * p + 2])
                th_ref[n // 3, n % 3 : n % 3 + 1, :] = both
    j0, j1 = iota((TOK, TOK), 0), iota((TOK, TOK), 1)
    same = (j0 & 7) == (j1 & 7)
    below = (j0 >> 3) >= (j1 >> 3)
    cle = (same & ((j0 >> 3) <= (j1 >> 3))).astype(BF)
    cge = (same & below).astype(BF)
    r8 = jnp.broadcast_to(br_ref[...].astype(F32), (8, TOK)).astype(BF)
    seg_row = nn(r8, cle)[0:1]
    seg_col = nt(cge, r8)[:, 0:1]
    mask = jnp.where(same & (seg_col == seg_row), jnp.where(j0 == j1, 2.0 * SCALE, SCALE), 0.0)
    lr, ll = ldc_ref[0], ldc_ref[1]
    row_r, row_l = nn(lr, cle), nn(ll, cge)
    col_r, col_l = nt(cge, lr), nt(cle, ll)
    for h in range(HEADS):
        w = weights(col_r[:, h : h + 1], row_r[h : h + 1], col_l[:, h : h + 1], row_l[h : h + 1], below, mask)
        wc_ref[h // 2, (h % 2) * TOK : (h % 2 + 1) * TOK, :] = w


def project_kernel(x_ref, g_ref, w_ref, wo_ref, fac_ref, th_ref, qkv_ref, dn_ref, u_ref):
    qkv_ref[...] = nn(x_ref[...], w_ref[...]).astype(BF)
    for r in range(ROWS):
        rows = slice(r * COLS, (r + 1) * COLS)
        for p in range(PAIRS):
            k = qkv_ref[rows, D + p * 128 : D + (p + 1) * 128]
            v = qkv_ref[rows, 2 * D + p * 128 : 2 * D + (p + 1) * 128].astype(F32)
            for direction in range(2):
                tv = (lanes_of(fac_ref[2 + direction, r], p) * v).astype(BF)
                a, off = block_of(u_ref, direction, r, p)
                u_ref[a, off : off + HEAD_DIM, :] = compact(tn(k, tv)).astype(BF)
    u_ref[:, 192:208, :] = th_ref[...].astype(BF)
    dn_ref[...] = nt(g_ref[...], wo_ref[...]).astype(BF)


def chain_kernel(adjoint, rev_ref, th_ref, x_ref, out_ref):
    rev = rev_ref[0]
    state = jnp.zeros((192, 128), F32)
    for n in range(8):
        up, down = n, 7 - n
        if adjoint:
            up, down = down, up
        src = jnp.where(rev == 1, down, up)
        out_ref[src] = state.astype(BF)
        if n < 7:
            th = th_ref[src, 192:208, :].astype(F32)
            th = jnp.concatenate([jnp.broadcast_to(th[m : m + 1], (HEAD_DIM, 128)) for m in range(3)], axis=0)
            state = th * state + x_ref[src, 0:192, :].astype(F32)


def col_forward_kernel(rx_ref, w_ref, wo_ref, wc_ref, qkv_ref, dn_ref, out_ref):
    x = rx_ref[:, 0:16, :].reshape(TOK, D)
    g = rx_ref[:, 16:32, :].reshape(TOK, D)
    qkv_ref[...] = nn(x, w_ref[...]).astype(BF)
    for p in range(PAIRS):
        q = qkv_ref[:, p * 128 : (p + 1) * 128]
        k = qkv_ref[:, D + p * 128 : D + (p + 1) * 128]
        v = qkv_ref[:, 2 * D + p * 128 : 2 * D + (p + 1) * 128]
        probs = (nt(split_heads(q), k) * wc_ref[p]).astype(BF)
        out_ref[:, p * 128 : (p + 1) * 128] = nn(side(probs), split_heads(v)).astype(BF)
    dn_ref[...] = nt(g, wo_ref[...]).astype(BF)


def state_of(s_ref, direction, r, p):
    a, off = block_of(s_ref, direction, r, p)
    return s_ref[a, off : off + HEAD_DIM, :]


def both_states(s_ref, r, p):
    return jnp.concatenate([split_heads(state_of(s_ref, d, r, p)) for d in range(2)], axis=1)


def row_forward_kernel(qkv_ref, s_ref, wr_ref, fac_ref, col_ref, out_ref, xch_ref):
    for r in range(ROWS):
        rows = slice(r * COLS, (r + 1) * COLS)
        for p in range(PAIRS):
            q = qkv_ref[rows, p * 128 : (p + 1) * 128]
            k = qkv_ref[rows, D + p * 128 : D + (p + 1) * 128]
            v = qkv_ref[rows, 2 * D + p * 128 : 2 * D + (p + 1) * 128]
            probs = (nt(split_heads(q), k) * wr_ref[r * PAIRS + p]).astype(BF)
            carried = nn(q, both_states(s_ref, r, p))
            out = nn(side(probs), split_heads(v))
            out = out + lanes_of(fac_ref[0, r], p) * carried[:, :128]
            out = out + lanes_of(fac_ref[1, r], p) * carried[:, 128:]
            out_ref[rows, p * 128 : (p + 1) * 128] = out
    xch_ref[:, 0:16, :] = col_ref[...].reshape(16, 16, D)
    slab = out_ref[...].reshape(2, 16, 8, D).swapaxes(0, 1).reshape(16, 16, D)
    xch_ref[:, 16:32, :] = slab.astype(BF)


def norm_backward(mixed, dn, gain):
    inv = lax.rsqrt(jnp.mean(mixed * mixed, axis=-1, keepdims=True) + EPSILON)
    unit = mixed * inv
    scaled = dn * gain
    d_mixed = inv * (scaled - unit * jnp.mean(scaled * unit, axis=-1, keepdims=True))
    return unit, d_mixed


def from_slab(x):
    return x.astype(F32).reshape(16, 2, 8, D).swapaxes(0, 1).reshape(TOK, D)


def row_middle_kernel(rx_ref, row_ref, dn_ref, gain_ref, qkv_ref, fac_ref, dm_ref, normed_ref, gt_ref, g_ref):
    mixed = row_ref[...] + from_slab(rx_ref[:, 0:16, :])
    dn = dn_ref[...].astype(F32)
    gain = gain_ref[...]
    unit, d_mixed = norm_backward(mixed, dn, gain)
    dm_ref[...] = d_mixed.astype(BF)
    normed_ref[...] = (unit * gain).astype(BF)
    gt_ref[...] = (dn * unit).astype(BF)
    for r in range(ROWS):
        rows = slice(r * COLS, (r + 1) * COLS)
        for p in range(PAIRS):
            q = qkv_ref[rows, p * 128 : (p + 1) * 128]
            do = dm_ref[rows, p * 128 : (p + 1) * 128].astype(F32)
            for direction in range(2):
                eo = (lanes_of(fac_ref[direction, r], p) * do).astype(BF)
                a, off = block_of(g_ref, direction, r, p)
                g_ref[a, off : off + HEAD_DIM, :] = compact(tn(q, eo)).astype(BF)


def local_backward(q, k, v, do, w):
    q2, do2 = split_heads(q), split_heads(do)
    scores = nt(q2, k)
    dw = nt(do2, v) * w
    probs = (scores * w).astype(BF)
    both = (scores * dw).astype(BF)
    dw = dw.astype(BF)
    dq = nn(side(dw), split_heads(k))
    dk = tn(dw, q2)
    dv = tn(probs, do2)
    return dq, dk, dv, both


def col_backward_kernel(rx_ref, col_ref, dn_ref, gain_ref, qkv_ref, wc_ref, w_ref, dqkv_ref, gd_ref, tok_ref):
    mixed = rx_ref[:, 16:32, :].reshape(TOK, D).astype(F32) + col_ref[...].astype(F32)
    _, d_mixed = norm_backward(mixed, dn_ref[...].astype(F32), gain_ref[...])
    d_mixed = d_mixed.astype(BF)
    j0, j1 = iota((TOK, TOK), 0), iota((TOK, TOK), 1)
    same = (j0 & 7) == (j1 & 7)
    k0, k1 = j0 >> 3, j1 >> 3
    before, behind = (same & (k0 < k1)).astype(BF), (same & (k0 > k1)).astype(BF)
    table = jnp.concatenate([before, behind], axis=1)
    for p in range(PAIRS):
        lanes = slice(p * 128, (p + 1) * 128)
        q = qkv_ref[:, p * 128 : (p + 1) * 128]
        k = qkv_ref[:, D + p * 128 : D + (p + 1) * 128]
        v = qkv_ref[:, 2 * D + p * 128 : 2 * D + (p + 1) * 128]
        dq, dk, dv, both = local_backward(q, k, v, d_mixed[:, lanes], wc_ref[p])
        dqkv_ref[:, p * 128 : (p + 1) * 128] = dq.astype(BF)
        dqkv_ref[:, D + p * 128 : D + (p + 1) * 128] = dk.astype(BF)
        dqkv_ref[:, 2 * D + p * 128 : 2 * D + (p + 1) * 128] = dv.astype(BF)
        sums = nn(both, table)
        for half in range(2):
            part = sums[half * TOK : (half + 1) * TOK]
            h = 2 * p + half
            gd_ref[0, h : h + 1, :] = jnp.sum(jnp.where(k0 >= k1, part[:, :TOK], 0.0), axis=0, keepdims=True)
            gd_ref[1, h : h + 1, :] = jnp.sum(jnp.where(k0 <= k1, part[:, TOK:], 0.0), axis=0, keepdims=True)
    tok_ref[...] = nt(dqkv_ref[...], w_ref[...]).astype(BF)


def row_backward_kernel(qkv_ref, dm_ref, s_ref, a_ref, wr_ref, fac_ref, th_ref, dqkv_ref, gd_ref):
    i0, i1 = iota((COLS, COLS), 0), iota((COLS, COLS), 1)
    table = jnp.concatenate([(i0 < i1).astype(BF), (i0 > i1).astype(BF)], axis=1)
    left = left_half((COLS, 128))
    for r in range(ROWS):
        rows = slice(r * COLS, (r + 1) * COLS)
        for p in range(PAIRS):
            lanes = slice(p * 128, (p + 1) * 128)
            q = qkv_ref[rows, p * 128 : (p + 1) * 128]
            k = qkv_ref[rows, D + p * 128 : D + (p + 1) * 128]
            v = qkv_ref[rows, 2 * D + p * 128 : 2 * D + (p + 1) * 128]
            do = dm_ref[rows, lanes]
            dq, dk, dv, both = local_backward(q, k, v, do, wr_ref[r * PAIRS + p])
            states, adjoints = both_states(s_ref, r, p), both_states(a_ref, r, p)
            wide_do, wide_v = do.astype(F32), v.astype(F32)
            enter = [lanes_of(fac_ref[d, r], p) for d in range(2)]
            tail = [lanes_of(fac_ref[2 + d, r], p) for d in range(2)]
            eo = [e * wide_do for e in enter]
            tv = [t * wide_v for t in tail]
            dq = dq + nt(jnp.concatenate(eo, axis=1).astype(BF), states)
            dk = dk + nt(jnp.concatenate(tv, axis=1).astype(BF), adjoints)
            carried = nn(q, states)
            leaving = nn(k, adjoints)
            dv = dv + tail[0] * leaving[:, :128] + tail[1] * leaving[:, 128:]
            dqkv_ref[rows, p * 128 : (p + 1) * 128] = dq.astype(BF)
            dqkv_ref[rows, D + p * 128 : D + (p + 1) * 128] = dk.astype(BF)
            dqkv_ref[rows, 2 * D + p * 128 : 2 * D + (p + 1) * 128] = dv.astype(BF)
            sums = nn(both, table)
            for direction in range(2):
                e_all = carried[:, direction * 128 : (direction + 1) * 128] * eo[direction]
                g_all = leaving[:, direction * 128 : (direction + 1) * 128] * tv[direction]
                n = direction * ROWS * PAIRS + r * PAIRS + p
                through = th_ref[n // 3, n % 3 : n % 3 + 1, :]
                prod = state_of(s_ref, direction, r, p).astype(F32) * state_of(a_ref, direction, r, p).astype(F32)
                prod = through * jnp.sum(prod, axis=0, keepdims=True)
                keep = (i0 >= i1) if direction == 0 else (i0 <= i1)
                for half in range(2):
                    pick = left if half == 0 else ~left
                    e = jnp.sum(jnp.where(pick, e_all, 0.0), axis=1, keepdims=True)
                    g = jnp.sum(jnp.where(pick, g_all, 0.0), axis=1, keepdims=True)
                    c = jnp.sum(jnp.where(pick[0:1], prod, 0.0), axis=1, keepdims=True)
                    part = sums[half * COLS : (half + 1) * COLS, direction * COLS : (direction + 1) * COLS]
                    grad = jnp.sum(jnp.where(keep, part + e, g), axis=0, keepdims=True) + c
                    gd_ref[direction, 2 * p + half, r : r + 1, :] = grad


def weight_kernel(x_ref, rx_ref, dr_ref, dc_ref, normed_ref, g_ref, gt_ref, out_ref):
    x = jnp.concatenate([x_ref[...], rx_ref[:, 0:16, :].reshape(TOK, D)], axis=0)

    def put(value, start):
        width = value.shape[1]
        for c in range(2):
            for n in range(8):
                at = (2 * n + c) * 48
                out_ref[c, n, :, start : start + width] = value[at : at + 48].astype(BF)

    for start in range(0, F, 384):
        d = jnp.concatenate([dr_ref[:, start : start + 384], dc_ref[:, start : start + 384]], axis=0)
        put(tn(x, d), start)
    for start in range(0, D, 384):
        put(tn(normed_ref[...], g_ref[:, start : start + 384]), F + start)
    put(tn(gt_ref[...], jnp.ones((TOK, 128), BF)), F + D)


def token_kernel(dr_ref, w_ref, rx_ref, out_ref):
    out_ref[...] = (nt(dr_ref[...], w_ref[...]) + from_slab(rx_ref[...])).astype(BF)


def exchange(x, axis, groups=None):
    return lax.all_to_all(x, axis, 0, 0, tiled=True, axis_index_groups=groups)


def per_device(
    tokens, grad_out, w_qkv, w_out, gain, log_decay_rows, log_decay_cols, border_cols, border_rows
):
    place = lax.axis_index("col")
    core = lax.axis_index("row") % 2
    rev = (place >= 4).astype(jnp.int32).reshape(1)
    x = tokens.reshape(TOK, D)
    g = grad_out.reshape(TOK, D)
    gain = gain.reshape(1, D)

    def slab(a):
        return a.reshape(ROWS, 16, CD, D).swapaxes(0, 1).reshape(16, ROWS * CD, D)

    rx = exchange(jnp.concatenate([slab(tokens), slab(grad_out)], axis=1), "row")

    ldr = log_decay_rows.transpose(2, 0, 1, 3)
    ldc = log_decay_cols.swapaxes(2, 3).reshape(2, HEADS, TOK)
    tiles = jnp.concatenate([border_cols, jnp.zeros((COLS,), jnp.int32)]).reshape(9, COLS)
    bc = lax.dynamic_slice_in_dim(tiles, place, 2)
    br = jnp.broadcast_to(border_rows[:, None], (GRID_H, CD)).reshape(1, TOK)
    wr, wc, fac, th = call(
        prep_kernel,
        [
            ((ROWS * PAIRS, 2 * COLS, COLS), F32),
            ((PAIRS, 2 * TOK, TOK), F32),
            ((4, ROWS, COLS, HEADS), F32),
            ((8, 16, 128), F32),
        ],
        ldr, ldc, bc, br,
    )
    qkv, dn, update = call(
        project_kernel,
        [((TOK, F), BF), ((TOK, D), BF), ((8, 208, 128), BF)],
        x, g, w_qkv, w_out, fac, th,
    )
    update = exchange(update, "col")
    (entering,) = call(
        functools.partial(chain_kernel, False), [((8, 192, 128), BF)], rev, update, update, smem=(0,)
    )
    entering = exchange(entering, "col")
    qkv_c, dn_c, col_out = call(
        col_forward_kernel,
        [((TOK, F), BF), ((TOK, D), BF), ((TOK, D), BF)],
        rx, w_qkv, w_out, wc,
    )
    row_out, swap = call(
        row_forward_kernel,
        [((TOK, D), F32), ((16, 32, D), BF)],
        qkv, entering, wr, fac, col_out,
    )
    rx2 = exchange(swap, "row")
    dm, normed, gt, adj = call(
        row_middle_kernel,
        [((TOK, D), BF), ((TOK, D), BF), ((TOK, D), BF), ((8, 192, 128), BF)],
        rx2, row_out, dn, gain, qkv, fac,
    )
    adj = exchange(adj, "col")
    (leaving,) = call(
        functools.partial(chain_kernel, True), [((8, 192, 128), BF)], rev, update, adj, smem=(0,)
    )
    leaving = exchange(leaving, "col")
    dqkv_c, gdc, tok_c = call(
        col_backward_kernel,
        [((TOK, F), BF), ((2, HEADS, TOK), F32), ((TOK, D), BF)],
        rx2, col_out, dn_c, gain, qkv_c, wc, w_qkv,
    )
    rx3 = exchange(tok_c.reshape(16, 16, D), "row")
    dqkv, gdr = call(
        row_backward_kernel,
        [((TOK, F), BF), ((2, HEADS, ROWS, COLS), F32)],
        qkv, dm, entering, leaving, wr, fac, th,
    )
    (wg,) = call(
        weight_kernel, [((2, 8, 48, WIDE), BF)], x, rx, dqkv, dqkv_c, normed, g, gt
    )
    other = lax.ppermute(lax.dynamic_index_in_dim(wg, 1 - core, 0, False), "row", CORE_SWAP)
    mine = lax.dynamic_index_in_dim(wg, core, 0, False)
    wg = (mine.astype(F32) + other.astype(F32)).astype(BF)
    wg = exchange(wg, "row", EVEN_ODD)
    wg = jnp.sum(wg.astype(F32), axis=0).astype(BF).reshape(8, 6, WIDE)
    wg = exchange(wg, "col")
    wg = jnp.sum(wg.astype(F32), axis=0) * (32768.0 ** (-0.5))
    (grad_tokens,) = call(token_kernel, [((TOK, D), BF)], dqkv, w_qkv, rx3)
    return (
        grad_tokens.reshape(ROWS, COLS, D),
        wg[:, :F],
        wg[:, F : F + D],
        wg[:, F + D],
        gdr.astype(BF),
        gdc.astype(BF).reshape(2, HEADS, GRID_H, CD).swapaxes(2, 3),
    )


def solution(mesh):
    in_specs = (
        P("row", "col", None),
        P("row", "col", None),
        P(),
        P(),
        P(),
        P(None, None, "row", "col"),
        P(None, None, ("col", "row"), None),
        P(),
        P(),
    )
    out_specs = (
        P("row", "col", None),
        P(("row", "col"), None),
        P(("row", "col"), None),
        P(("row", "col")),
        P(None, None, "row", "col"),
        P(None, None, ("col", "row"), None),
    )
    return jax.shard_map(
        per_device, mesh=mesh, in_specs=in_specs, out_specs=out_specs, check_vma=False
    )
```

time: 1080 us -> 224 us (0.21); the launches traced: 1060 us -> 223 us
  blocking collectives: 435 us -> 48.5 us
  local copies, waits for them, and re-layouts: 218 us -> 14.4 us
  matrix products: 135 us -> 0 us
  other arithmetic: 137 us -> 5.07 us
  starting transfers between devices: 123 us -> 32.8 us
  Pallas kernels: 0 us -> 67.2 us
  waiting for transfers between devices: 0.18 us -> 54.3 us
  between operations: 15.3 us -> 0.84 us
    unnamed x2 -> x0, blocking collectives: 401 us -> none
    dot_general x47 -> x0, matrix products: 135 us -> none  [the longest x12 50.7 us: block_scan(): jnp.einsum('lhts,lshd->lthd', scores * weights * scaling, value_wide, pre...]
    unnamed x33 -> x0, starting transfers between devices: 94.7 us -> none
    pallas_call x0 -> x11, Pallas kernels: none -> 67.2 us  [call(): pl.pallas_call(body, out_shape=[jax.ShapeDtypeStruct(s, t) for s, t in ou...]
    unnamed x210 -> x24, local copies, waits for them, and re-layouts: 64.7 us -> 4.46 us
    all_to_all x4 -> x7, waiting for transfers between devices: 0.01 us -> 49.5 us  [exchange(): return lax.all_to_all(x, axis, 0, 0, tiled=True, axis_index_groups=groups)]
    rev x22 -> x0, local copies, waits for them, and re-layouts: 49.1 us -> none  [the longest x2 6.98 us: down_up(): combined = downward + upward[:, ::-1]]
    all_to_all x0 -> x2, blocking collectives: none -> 48.5 us  [exchange(): return lax.all_to_all(x, axis, 0, 0, tiled=True, axis_index_groups=groups)]
  transfers between devices with their start and end apart: 41 -> 8, of which waited for: 0 -> 7; matrix products, arithmetic and copies ran while one was open for 71% -> 2% of each run, Pallas kernels for 0% -> 10%
where the time goes in v1:
time: 224 us; the launch traced here: 223 us
  Pallas kernels  67.2 us (30%)
  waiting for transfers between devices  54.3 us (24%)
  blocking collectives  48.5 us (22%)
  starting transfers between devices  32.8 us (15%)
  local copies, waits for them, and re-layouts  14.4 us (6%)
  other arithmetic  5.07 us (2%)
    pallas_call x11, Pallas kernels, call(): pl.pallas_call(body, out_shape=[jax.ShapeDtypeStruct(s, t) for s, t in ou...  67.2 us
    all_to_all x7, waiting for transfers between devices, exchange(): return lax.all_to_all(x, axis, 0, 0, tiled=True, axis_index_groups=groups)  49.5 us
    all_to_all x2, blocking collectives, exchange(): return lax.all_to_all(x, axis, 0, 0, tiled=True, axis_index_groups=groups)  48.5 us
    all_to_all x7, starting transfers between devices, exchange(): return lax.all_to_all(x, axis, 0, 0, tiled=True, axis_index_groups=groups)  32.7 us
    ppermute x1, waiting for transfers between devices, per_device(): lax.ppermute(lax.dynamic_index_in_dim(wg, 1 - core, 0, False), 'row', COR...  4.79 us
  transfers between devices with their start and end apart: 8, of which 7 were waited for; matrix products, arithmetic and copies ran while one was open for 2% of the time, Pallas kernels for 10%

profile of v1, /device:TPU:0, one launch (start us, length us, event | category | flops | bytes accessed | tf_op | source)
XLA Modules:
  0.0 223.1 jit_solution(16198406037688477823)
XLA Ops:
  0.6 1.3 copy.32
  2.0 0.9 copy.27
  6.4 6.0 %shard_map.136 = (f32[12,256,128]{2,1,0:T(8,128)}, f32[6,512,256]{2,1,0:T(8,128)}, f32[4,2,128,12]{3,2,1,0:T(8,128)}, f32[8,16,128]{2,1,0:T(8,128)}) custom-call(bf16[2,2,12,128]{3,2,1,0:T(8,128)(2,1)} %bitcast.41, bf16[2,12,256]{2,1,0:T(8,128)(2,1)} %reshape.81.ldc_ref, s32[2,128]{1,0:T(2,128)} %constant_dynamic-slice_fusion.bc_ref, s32[1,256]{1,0:T(1,128)} %reshape.66.br_ref), custom_call_target="tpu_custom_call" | custom-call | tf_op jit(solution)/shard_map/pallas_call | solution.py:33
  12.4 5.5 %shard_map.137 = (bf16[256,2304]{1,0:T(8,128)(2,1)}, bf16[256,768]{1,0:T(8,128)(2,1)}, bf16[8,208,128]{2,1,0:T(8,128)(2,1)}) custom-call(bf16[256,768]{1,0:T(8,128)(2,1)} %bitcast.35, bf16[256,768]{1,0:T(8,128)(2,1)} %bitcast.37, bf16[768,2304]{1,0:T(8,128)(2,1)} %w_ref.7, bf16[768,768]{1,0:T(8,128)(2,1)} %wo_ref.3, ...), custom_call_target="tpu_custom_call" | custom-call | tf_op jit(solution)/shard_map/pallas_call | solution.py:33
  17.9 5.4 %all-to-all-start = ((bf16[8,208,128]{2,1,0:T(8,128)(2,1)}), bf16[8,208,128]{2,1,0:T(8,128)(2,1)S(1)}, u32[]{:S(2)}, u32[]{:S(2)}) async-start(bf16[8,208,128]{2,1,0:T(8,128)(2,1)} %get-tuple-element.30), calls=%async_computation | async-start | bytes 851968 | tf_op jit(solution)/shard_map/all_to_all | solution.py:348
  23.3 1.0 pad_maximum_fusion
  24.3 8.0 %all-to-all-done.th_ref.x_ref = bf16[8,208,128]{2,1,0:T(8,128)(2,1)S(1)} async-done(((bf16[8,208,128]{2,1,0:T(8,128)(2,1)}), bf16[8,208,128]{2,1,0:T(8,128)(2,1)S(1)}, u32[]{:S(2)}, u32[]{:S(2)}) %all-to-all-start) | async-done | bytes 426016 | tf_op jit(solution)/shard_map/all_to_all | solution.py:348
  32.3 7.8 %all-to-all-start.2 = ((bf16[16,32,768]{2,1,0:T(8,128)(2,1)}), bf16[16,32,768]{2,1,0:T(8,128)(2,1)S(1)}, u32[]{:S(2)}, u32[]{:S(2)}) async-start(bf16[16,32,768]{2,1,0:T(8,128)(2,1)} %pad_maximum_fusion), calls=%async_computation.2 | async-start | bytes 1572864 | tf_op jit(solution)/shard_map/all_to_all | solution.py:348
  40.1 2.0 shard_map.138
  42.0 13.2 %all-to-all-done.2.rx_ref = bf16[16,32,768]{2,1,0:T(8,128)(2,1)S(1)} async-done(((bf16[16,32,768]{2,1,0:T(8,128)(2,1)}), bf16[16,32,768]{2,1,0:T(8,128)(2,1)S(1)}, u32[]{:S(2)}, u32[]{:S(2)}) %all-to-all-start.2) | async-done | bytes 786464 | tf_op jit(solution)/shard_map/all_to_all | solution.py:348
  55.2 3.5 %all-to-all-start.1 = ((bf16[8,192,128]{2,1,0:T(8,128)(2,1)}), bf16[8,192,128]{2,1,0:T(8,128)(2,1)S(1)}, u32[]{:S(2)}, u32[]{:S(2)}) async-start(bf16[8,192,128]{2,1,0:T(8,128)(2,1)} %shard_map.138), calls=%async_computation.1 | async-start | bytes 786432 | tf_op jit(solution)/shard_map/all_to_all | solution.py:348
  58.7 7.0 %shard_map.139 = (bf16[256,2304]{1,0:T(8,128)(2,1)}, bf16[256,768]{1,0:T(8,128)(2,1)}, bf16[256,768]{1,0:T(8,128)(2,1)}) custom-call(bf16[16,32,768]{2,1,0:T(8,128)(2,1)} %copy-done, bf16[768,2304]{1,0:T(8,128)(2,1)} %w_ref.7, bf16[768,768]{1,0:T(8,128)(2,1)} %wo_ref.3, f32[6,512,256]{2,1,0:T(8,128)} %get-tuple-element.32.wc_ref), custom_call_target="tpu_custom_call" | custom-call | tf_op jit(solution)/shard_map/pallas_call | solution.py:33
  65.7 1.7 all-to-all-done.1.s_ref
  68.1 4.8 %shard_map.140 = (f32[256,768]{1,0:T(8,128)}, bf16[16,32,768]{2,1,0:T(8,128)(2,1)}) custom-call(bf16[256,2304]{1,0:T(8,128)(2,1)} %get-tuple-element.29.qkv_ref, bf16[8,192,128]{2,1,0:T(8,128)(2,1)} %copy-done.5, f32[12,256,128]{2,1,0:T(8,128)} %get-tuple-element.31.wr_ref, f32[4,2,128,12]{3,2,1,0:T(8,128)} %get-tuple-element.27.fac_ref, ...), custom_call_target="tpu_custom_call" | custom-call | tf_op jit(solution)/shard_map/pallas_call | solution.py:33
  72.9 3.6 %all-to-all-start.3 = ((bf16[16,32,768]{2,1,0:T(8,128)(2,1)}), bf16[16,32,768]{2,1,0:T(8,128)(2,1)S(1)}, u32[]{:S(2)}, u32[]{:S(2)}) async-start(bf16[16,32,768]{2,1,0:T(8,128)(2,1)} %get-tuple-element.34), calls=%async_computation.3 | async-start | bytes 1572864 | tf_op jit(solution)/shard_map/all_to_all | solution.py:348
  77.1 14.5 %all-to-all-done.3.rx_ref = bf16[16,32,768]{2,1,0:T(8,128)(2,1)S(1)} async-done(((bf16[16,32,768]{2,1,0:T(8,128)(2,1)}), bf16[16,32,768]{2,1,0:T(8,128)(2,1)S(1)}, u32[]{:S(2)}, u32[]{:S(2)}) %all-to-all-start.3) | async-done | bytes 786464 | tf_op jit(solution)/shard_map/all_to_all | solution.py:348
  92.6 4.4 %shard_map.141 = (bf16[256,768]{1,0:T(8,128)(2,1)}, bf16[256,768]{1,0:T(8,128)(2,1)}, bf16[256,768]{1,0:T(8,128)(2,1)}, bf16[8,192,128]{2,1,0:T(8,128)(2,1)}) custom-call(bf16[16,32,768]{2,1,0:T(8,128)(2,1)} %copy-done.1, f32[256,768]{1,0:T(8,128)} %get-tuple-element.35.row_ref, bf16[256,768]{1,0:T(8,128)(2,1)} %get-tuple-element.36.dn_ref, ...), custom_call_target="tpu_custom_call" | custom-call | tf_op jit(solution)/shard_map/pallas_call | solution.py:33
  96.9 12.8 %all_to_all.45.x_ref = bf16[8,192,128]{2,1,0:T(8,128)(2,1)} all-to-all(bf16[8,192,128]{2,1,0:T(8,128)(2,1)} %get-tuple-element.38), channel_id=1, replica_groups=mesh['row'=16,'col'=8] {'col'}, dimensions={0} | all-to-all | bytes 786432 | tf_op jit(solution)/shard_map/all_to_all | solution.py:348
  109.8 2.0 shard_map.142
  111.7 3.6 %all-to-all-start.5 = ((bf16[8,192,128]{2,1,0:T(8,128)(2,1)}), bf16[8,192,128]{2,1,0:T(8,128)(2,1)S(1)}, u32[]{:S(2)}, u32[]{:S(2)}) async-start(bf16[8,192,128]{2,1,0:T(8,128)(2,1)} %shard_map.142), calls=%async_computation.5 | async-start | bytes 786432 | tf_op jit(solution)/shard_map/all_to_all | solution.py:348
  115.4 9.9 %shard_map.144 = (bf16[256,2304]{1,0:T(8,128)(2,1)}, f32[2,12,256]{2,1,0:T(8,128)}, bf16[256,768]{1,0:T(8,128)(2,1)}) custom-call(bf16[16,32,768]{2,1,0:T(8,128)(2,1)} %copy-done.1, bf16[256,768]{1,0:T(8,128)(2,1)} %get-tuple-element.33.col_ref, bf16[256,768]{1,0:T(8,128)(2,1)} %get-tuple-element.40.dn_ref, f32[1,768]{1,0:T(1,128)} %reshape.73.gain_ref, ...), custom_call_target="tpu_custom_call" | custom-call | tf_op jit(solution)/shard_map/pallas_call | solution.py:33
  126.0 13.8 %shard_map.143 = (bf16[256,2304]{1,0:T(8,128)(2,1)}, f32[2,12,2,128]{3,2,1,0:T(2,128)}) custom-call(bf16[256,2304]{1,0:T(8,128)(2,1)} %get-tuple-element.29.qkv_ref, bf16[256,768]{1,0:T(8,128)(2,1)} %get-tuple-element.37.dm_ref, bf16[8,192,128]{2,1,0:T(8,128)(2,1)} %copy-done.5, bf16[8,192,128]{2,1,0:T(8,128)(2,1)} %copy-done.6, ...), custom_call_target="tpu_custom_call" | custom-call | tf_op jit(solution)/shard_map/pallas_call | solution.py:33
  139.8 7.7 %shard_map.146 = bf16[2,8,48,3200]{3,2,1,0:T(8,128)(2,1)} custom-call(bf16[256,768]{1,0:T(8,128)(2,1)} %bitcast.36, bf16[16,32,768]{2,1,0:T(8,128)(2,1)} %copy-done, bf16[256,2304]{1,0:T(8,128)(2,1)} %get-tuple-element.39.dr_ref, bf16[256,2304]{1,0:T(8,128)(2,1)} %get-tuple-element.43.dc_ref, bf16[256,768]{1,0:T(8,128)(2,1)} %get-tuple-element.44.normed_ref, ...), custom_call_target="tpu_custom_call" | custom-call | tf_op jit(solution)/shard_map/pallas_call | solution.py:33
  147.5 1.9 dynamic-slice_bitcast_fusion
  149.5 4.8 %collective-permute-done = bf16[8,48,3200]{2,1,0:T(8,128)(2,1)} collective-permute-done((bf16[8,48,3200]{2,1,0:T(8,128)(2,1)S(1)}, bf16[8,48,3200]{2,1,0:T(8,128)(2,1)}, u32[]{:S(2)}, u32[]{:S(2)}) %collective-permute-start) | collective-permute-done | bytes 2457632 | tf_op jit(solution)/shard_map/ppermute | solution.py:426
  154.3 3.0 %fusion = bf16[8,48,3200]{2,1,0:T(8,128)(2,1)S(1)} fusion(bf16[8,48,3200]{2,1,0:T(8,128)(2,1)} %collective-permute-done, bf16[2,8,48,3200]{3,2,1,0:T(8,128)(2,1)} %shard_map.146, s32[]{:T(128)S(6)} %select_n.19), kind=kLoop, calls=%fused_computation.1 | loop fusion | flops 4915200 | bytes 7372804 | tf_op jit(solution)/shard_map/convert_element_type | solution.py:428
  157.3 35.7 %all_to_all.46 = bf16[8,48,3200]{2,1,0:T(8,128)(2,1)S(1)} all-to-all(bf16[8,48,3200]{2,1,0:T(8,128)(2,1)S(1)} %fusion), channel_id=1, replica_groups={{0,16,32,48,64,80,96,112},{8,24,40,56,72,88,104,120},{1,17,33,49,65,81,..., dimensions={0} | all-to-all | bytes 4915200 | tf_op jit(solution)/shard_map/all_to_all | solution.py:348
  193.0 3.7 %all-to-all-start.6 = ((bf16[16,16,768]{2,1,0:T(8,128)(2,1)}), bf16[16,16,768]{2,1,0:T(8,128)(2,1)S(1)}, u32[]{:S(2)}, u32[]{:S(2)}) async-start(bf16[16,16,768]{2,1,0:T(8,128)(2,1)} %bitcast.12), calls=%async_computation.6 | async-start | bytes 786432 | tf_op jit(solution)/shard_map/all_to_all | solution.py:348
  197.9 9.7 %all-to-all-done.6.rx_ref = bf16[16,16,768]{2,1,0:T(8,128)(2,1)S(1)} async-done(((bf16[16,16,768]{2,1,0:T(8,128)(2,1)}), bf16[16,16,768]{2,1,0:T(8,128)(2,1)S(1)}, u32[]{:S(2)}, u32[]{:S(2)}) %all-to-all-start.6) | async-done | bytes 393248 | tf_op jit(solution)/shard_map/all_to_all | solution.py:348
  207.6 5.2 %all-to-all-start.8 = ((bf16[8,6,3200]{2,1,0:T(8,128)(2,1)}), bf16[8,6,3200]{2,1,0:T(8,128)(2,1)S(1)}, u32[]{:S(2)}, u32[]{:S(2)}) async-start(bf16[8,6,3200]{2,1,0:T(8,128)(2,1)} %reshape.76), calls=%async_computation.8 | async-start | bytes 819200 | tf_op jit(solution)/shard_map/all_to_all | solution.py:348
  214.4 4.3 %shard_map.145 = bf16[256,768]{1,0:T(8,128)(2,1)} custom-call(bf16[256,2304]{1,0:T(8,128)(2,1)} %get-tuple-element.39.dr_ref, bf16[768,2304]{1,0:T(8,128)(2,1)} %w_ref.7, bf16[16,16,768]{2,1,0:T(8,128)(2,1)} %copy-done.7), custom_call_target="tpu_custom_call" | custom-call | tf_op jit(solution)/shard_map/pallas_call | solution.py:33
  218.7 2.4 %all-to-all-done.8 = bf16[8,6,3200]{2,1,0:T(8,128)(2,1)S(1)} async-done(((bf16[8,6,3200]{2,1,0:T(8,128)(2,1)}), bf16[8,6,3200]{2,1,0:T(8,128)(2,1)S(1)}, u32[]{:S(2)}, u32[]{:S(2)}) %all-to-all-start.8) | async-done | bytes 307232 | tf_op jit(solution)/shard_map/all_to_all | solution.py:348
  (43 shorter events, 11.5 us)
Async XLA Ops:
  12.4 10.9 %copy-start.3 = (bf16[2,128,768]{2,1,0:T(8,128)(2,1)S(1)}, bf16[2,128,768]{2,1,0:T(8,128)(2,1)}, u32[]{:S(2)}) copy-start(bf16[2,128,768]{2,1,0:T(8,128)(2,1)} %param.9) | copy-start | bytes 1179652
  12.4 10.9 %copy-start.4 = (bf16[2,128,768]{2,1,0:T(8,128)(2,1)S(1)}, bf16[2,128,768]{2,1,0:T(8,128)(2,1)}, u32[]{:S(2)}) copy-start(bf16[2,128,768]{2,1,0:T(8,128)(2,1)} %param.10) | copy-start | bytes 1179652
  17.9 14.4 %all-to-all-start = ((bf16[8,208,128]{2,1,0:T(8,128)(2,1)}), bf16[8,208,128]{2,1,0:T(8,128)(2,1)S(1)}, u32[]{:S(2)}, u32[]{:S(2)}) async-start(bf16[8,208,128]{2,1,0:T(8,128)(2,1)} %get-tuple-element.30), calls=%async_computation | async-start | bytes 851968 | tf_op jit(solution)/shard_map/all_to_all | solution.py:348
  32.3 7.8 %copy-start.2 = (bf16[8,208,128]{2,1,0:T(8,128)(2,1)}, bf16[8,208,128]{2,1,0:T(8,128)(2,1)S(1)}, u32[]{:S(2)}) copy-start(bf16[8,208,128]{2,1,0:T(8,128)(2,1)S(1)} %all-to-all-done.th_ref.x_ref) | copy-start | bytes 1277956
  32.3 22.9 %all-to-all-start.2 = ((bf16[16,32,768]{2,1,0:T(8,128)(2,1)}), bf16[16,32,768]{2,1,0:T(8,128)(2,1)S(1)}, u32[]{:S(2)}, u32[]{:S(2)}) async-start(bf16[16,32,768]{2,1,0:T(8,128)(2,1)} %pad_maximum_fusion), calls=%async_computation.2 | async-start | bytes 1572864 | tf_op jit(solution)/shard_map/all_to_all | solution.py:348
  55.2 3.5 %copy-start = (bf16[16,32,768]{2,1,0:T(8,128)(2,1)}, bf16[16,32,768]{2,1,0:T(8,128)(2,1)S(1)}, u32[]{:S(2)}) copy-start(bf16[16,32,768]{2,1,0:T(8,128)(2,1)S(1)} %all-to-all-done.2.rx_ref) | copy-start | bytes 2359300
  55.2 12.2 %all-to-all-start.1 = ((bf16[8,192,128]{2,1,0:T(8,128)(2,1)}), bf16[8,192,128]{2,1,0:T(8,128)(2,1)S(1)}, u32[]{:S(2)}, u32[]{:S(2)}) async-start(bf16[8,192,128]{2,1,0:T(8,128)(2,1)} %shard_map.138), calls=%async_computation.1 | async-start | bytes 786432 | tf_op jit(solution)/shard_map/all_to_all | solution.py:348
  67.4 0.7 copy-start.5
  68.1 8.4 %copy-start.10 = (f32[768]{0:T(1024)S(1)}, f32[768]{0:T(1024)}, u32[]{:S(2)}) copy-start(f32[768]{0:T(1024)} %param.13) | copy-start | bytes 9220
  72.9 18.8 %all-to-all-start.3 = ((bf16[16,32,768]{2,1,0:T(8,128)(2,1)}), bf16[16,32,768]{2,1,0:T(8,128)(2,1)S(1)}, u32[]{:S(2)}, u32[]{:S(2)}) async-start(bf16[16,32,768]{2,1,0:T(8,128)(2,1)} %get-tuple-element.34), calls=%async_computation.3 | async-start | bytes 1572864 | tf_op jit(solution)/shard_map/all_to_all | solution.py:348
  91.7 0.9 copy-start.1
  111.7 13.5 %all-to-all-start.5 = ((bf16[8,192,128]{2,1,0:T(8,128)(2,1)}), bf16[8,192,128]{2,1,0:T(8,128)(2,1)S(1)}, u32[]{:S(2)}, u32[]{:S(2)}) async-start(bf16[8,192,128]{2,1,0:T(8,128)(2,1)} %shard_map.142), calls=%async_computation.5 | async-start | bytes 786432 | tf_op jit(solution)/shard_map/all_to_all | solution.py:348
  125.3 0.7 copy-start.6
  149.4 4.9 %collective-permute-start = (bf16[8,48,3200]{2,1,0:T(8,128)(2,1)S(1)}, bf16[8,48,3200]{2,1,0:T(8,128)(2,1)}, u32[]{:S(2)}, u32[]{:S(2)}) collective-permute-start(bf16[8,48,3200]{2,1,0:T(8,128)(2,1)S(1)} %dynamic-slice_bitcast_fusion), channel_id=1, source_target_pairs={{0,8},{8,0},{16,24},{24,16},{32,40},{40,32},{48,56},{56,48},{64,72... | collective-permute-start | bytes 7372808 | tf_op jit(solution)/shard_map/ppermute | solution.py:426
  193.0 19.8 %copy-start.8 = (f32[2,12,256]{2,1,0:T(8,128)S(1)}, f32[2,12,256]{2,1,0:T(8,128)}, u32[]{:S(2)}) copy-start(f32[2,12,256]{2,1,0:T(8,128)} %get-tuple-element.47) | copy-start | bytes 73732
  193.0 14.6 %all-to-all-start.6 = ((bf16[16,16,768]{2,1,0:T(8,128)(2,1)}), bf16[16,16,768]{2,1,0:T(8,128)(2,1)S(1)}, u32[]{:S(2)}, u32[]{:S(2)}) async-start(bf16[16,16,768]{2,1,0:T(8,128)(2,1)} %bitcast.12), calls=%async_computation.6 | async-start | bytes 786432 | tf_op jit(solution)/shard_map/all_to_all | solution.py:348
  196.7 17.1 %copy-start.9 = (f32[2,12,2,128]{3,2,1,0:T(2,128)S(1)}, f32[2,12,2,128]{3,2,1,0:T(2,128)}, u32[]{:S(2)}) copy-start(f32[2,12,2,128]{3,2,1,0:T(2,128)} %get-tuple-element.46) | copy-start | bytes 73732
  207.6 6.8 %copy-start.7 = (bf16[16,16,768]{2,1,0:T(8,128)(2,1)}, bf16[16,16,768]{2,1,0:T(8,128)(2,1)S(1)}, u32[]{:S(2)}) copy-start(bf16[16,16,768]{2,1,0:T(8,128)(2,1)S(1)} %all-to-all-done.6.rx_ref) | copy-start | bytes 1179652
  207.6 13.5 %all-to-all-start.8 = ((bf16[8,6,3200]{2,1,0:T(8,128)(2,1)}), bf16[8,6,3200]{2,1,0:T(8,128)(2,1)S(1)}, u32[]{:S(2)}, u32[]{:S(2)}) async-start(bf16[8,6,3200]{2,1,0:T(8,128)(2,1)} %reshape.76), calls=%async_computation.8 | async-start | bytes 819200 | tf_op jit(solution)/shard_map/all_to_all | solution.py:348

commit v2 on v1

v2 whole, which is shorter than its diff:
```python
import jax
import jax.numpy as jnp
from jax import lax
from jax.experimental import pallas as pl
from jax.experimental.pallas import tpu as pltpu
from jax.sharding import PartitionSpec as P

EPSILON = 1e-05
HEADS = 12
HEAD_DIM = 64
PAIRS = HEADS // 2
D = 768
F = 3 * D
ROWS = 2
COLS = 128
TOK = ROWS * COLS
GRID_H = 32
CD = 8
SCALE = HEAD_DIM ** (-0.5)
WIDE = F + D + 128
F32 = jnp.float32
BF = jnp.bfloat16
EVEN_ODD = [list(range(0, 16, 2)), list(range(1, 16, 2))]
CORE_SWAP = [(i, i ^ 1) for i in range(16)]


UNITS = ROWS * PAIRS
STATE = UNITS * HEAD_DIM
LOAD = STATE + 16


def call(body, us, outs, *args, smem=(), scratch=()):
    specs = [
        pl.BlockSpec(memory_space=pltpu.SMEM if n in smem else pltpu.VMEM) for n in range(len(args))
    ]
    return pl.pallas_call(
        body,
        out_shape=[jax.ShapeDtypeStruct(s, t) for s, t in outs],
        in_specs=specs,
        out_specs=[pl.BlockSpec(memory_space=pltpu.VMEM)] * len(outs),
        scratch_shapes=list(scratch),
        cost_estimate=pl.CostEstimate(
            flops=int(us * 1.1e9), bytes_accessed=int(us * 3.6e6), transcendentals=0
        ),
        compiler_params=pltpu.CompilerParams(vmem_limit_bytes=56 * 1024 * 1024),
    )(*args)


def iota(shape, dim):
    return lax.broadcasted_iota(jnp.int32, shape, dim)


def nn(a, b):
    return lax.dot_general(a, b, (((1,), (0,)), ((), ())), preferred_element_type=F32)


def nt(a, b):
    return lax.dot_general(a, b, (((1,), (1,)), ((), ())), preferred_element_type=F32)


def tn(a, b):
    return lax.dot_general(a, b, (((0,), (0,)), ((), ())), preferred_element_type=F32)


def left_half(shape):
    return iota(shape, len(shape) - 1) < HEAD_DIM


def split_heads(x):
    mask = left_half(x.shape)
    zero = jnp.zeros_like(x)
    return jnp.concatenate([jnp.where(mask, x, zero), jnp.where(mask, zero, x)], axis=0)


def side(x):
    half = x.shape[0] // 2
    return jnp.concatenate([x[:half], x[half:]], axis=1)


def lanes_of(fac, p):
    shape = (fac.shape[0], 128)
    return jnp.where(left_half(shape), fac[:, 2 * p : 2 * p + 1], fac[:, 2 * p + 1 : 2 * p + 2])


def compact(m):
    return jnp.where(left_half((HEAD_DIM, 128)), m[:HEAD_DIM], m[HEAD_DIM:])


def unit_rows(r, p):
    u = r * PAIRS + p
    return slice(u * HEAD_DIM, (u + 1) * HEAD_DIM)


def spread(both_ref, place, toward_right, out_ref):
    for d in range(8):
        side_of = d > place if toward_right else d < place
        out_ref[d] = both_ref[jnp.where(side_of, 0, 1)]


def gather_states(place, rx_ref, from_left, state_ref):
    state_ref[...] = jnp.zeros_like(state_ref)

    def step(direction, source):
        for u in range(UNITS):
            rows = slice(u * HEAD_DIM, (u + 1) * HEAD_DIM)
            th = rx_ref[source, STATE:LOAD, :].astype(F32)[u : u + 1]
            state_ref[direction, rows, :] = th * state_ref[direction, rows, :] + rx_ref[source, rows, :].astype(F32)

    lax.fori_loop(0, place, lambda n, c: (step(0 if from_left else 1, n), c)[1], 0)
    lax.fori_loop(0, 7 - place, lambda n, c: (step(1 if from_left else 0, 7 - n), c)[1], 0)


def pick_rows(core):
    m, f = iota((D // 2, D), 0), iota((D // 2, D), 1)
    n = (m * 683) >> 15
    return (f == m + 48 * (n + core)).astype(BF)


def per_head(shape):
    return (iota(shape, 0) == (iota(shape, 1) >> 6)).astype(BF)


def weights(col_r, row_r, col_l, row_l, lower, mask):
    return jnp.exp(jnp.where(lower, col_r - row_r, col_l - row_l)) * mask


def row_masks(bc_ref):
    i0, i1 = iota((COLS, COLS), 0), iota((COLS, COLS), 1)
    le, ge = (i0 <= i1).astype(BF), (i0 >= i1).astype(BF)
    b = bc_ref[...].astype(F32)
    b8 = jnp.broadcast_to(b[0:1], (8, COLS)).astype(BF)
    seg_row = nn(b8, le)[0:1]
    seg_col = nt(ge, b8)[:, 0:1]
    return i0, i1, le, ge, seg_row, seg_col, b[1:2, 0:1]


def summary_kernel(place_ref, ldr_ref, bc_ref, x_ref, w_ref, fac_ref, th_ref, kv_ref, u_ref, both_ref):
    i0, i1, le, ge, seg_row, seg_col, following = row_masks(bc_ref)
    first, last = seg_row[:, 0:1], seg_row[:, COLS - 1 : COLS]
    after = last + following
    th_ref[...] = jnp.zeros_like(th_ref)
    for r in range(ROWS):
        lr, ll = ldr_ref[r, 0], ldr_ref[r, 1]
        row_r, row_l = nn(lr, le), nn(ll, ge)
        col_r, col_l = nt(ge, lr), nt(le, ll)
        fac_ref[0, r] = jnp.where(seg_col == 0.0, jnp.exp(col_r), 0.0) * SCALE
        fac_ref[1, r] = jnp.where(seg_col == after, jnp.exp(col_l), 0.0) * SCALE
        fac_ref[2, r] = jnp.where(seg_col == last, jnp.exp(col_r[COLS - 1 : COLS] - col_r), 0.0)
        fac_ref[3, r] = jnp.where(seg_col == first, jnp.exp(col_l[0:1] - col_l), 0.0)
        th_r = jnp.where(last == 0.0, jnp.exp(row_r[:, COLS - 1 : COLS]), 0.0)
        th_l = jnp.where(after == first, jnp.exp(row_l[:, 0:1]), 0.0)
        for direction, th in enumerate((th_r, th_l)):
            for p in range(PAIRS):
                n = r * PAIRS + p
                both = jnp.where(left_half((1, 128)), th[2 * p : 2 * p + 1], th[2 * p + 1 : 2 * p + 2])
                th_ref[direction, n : n + 1, :] = both
    kv_ref[...] = nn(x_ref[...], w_ref[:, D:]).astype(BF)
    for r in range(ROWS):
        rows = slice(r * COLS, (r + 1) * COLS)
        for p in range(PAIRS):
            k = kv_ref[rows, p * 128 : (p + 1) * 128]
            v = kv_ref[rows, D + p * 128 : D + (p + 1) * 128].astype(F32)
            for direction in range(2):
                tv = (lanes_of(fac_ref[2 + direction, r], p) * v).astype(BF)
                both_ref[direction, unit_rows(r, p), :] = compact(tn(k, tv)).astype(BF)
    both_ref[:, STATE:LOAD, :] = th_ref[...].astype(BF)
    spread(both_ref, place_ref[0], True, u_ref)


def mask_kernel(ldr_ref, ldc_ref, bc_ref, br_ref, dep_ref, wr_ref, wc_ref):
    i0, i1, le, ge, seg_row, seg_col, _ = row_masks(bc_ref)
    lower = i0 >= i1
    mask = jnp.where(seg_col == seg_row, jnp.where(i0 == i1, 2.0 * SCALE, SCALE), 0.0)
    for r in range(ROWS):
        lr, ll = ldr_ref[r, 0], ldr_ref[r, 1]
        row_r, row_l = nn(lr, le), nn(ll, ge)
        col_r, col_l = nt(ge, lr), nt(le, ll)
        for h in range(HEADS):
            w = weights(col_r[:, h : h + 1], row_r[h : h + 1], col_l[:, h : h + 1], row_l[h : h + 1], lower, mask)
            wr_ref[r * PAIRS + h // 2, (h % 2) * COLS : (h % 2 + 1) * COLS, :] = w.astype(BF)
    j0, j1 = iota((TOK, TOK), 0), iota((TOK, TOK), 1)
    same = (j0 & 7) == (j1 & 7)
    below = (j0 >> 3) >= (j1 >> 3)
    cle = (same & ((j0 >> 3) <= (j1 >> 3))).astype(BF)
    cge = (same & below).astype(BF)
    r8 = jnp.broadcast_to(br_ref[...].astype(F32), (8, TOK)).astype(BF)
    seg_row = nn(r8, cle)[0:1]
    seg_col = nt(cge, r8)[:, 0:1]
    mask = jnp.where(same & (seg_col == seg_row), jnp.where(j0 == j1, 2.0 * SCALE, SCALE), 0.0)
    lr, ll = ldc_ref[0], ldc_ref[1]
    row_r, row_l = nn(lr, cle), nn(ll, cge)
    col_r, col_l = nt(cge, lr), nt(cle, ll)
    for h in range(HEADS):
        w = weights(col_r[:, h : h + 1], row_r[h : h + 1], col_l[:, h : h + 1], row_l[h : h + 1], below, mask)
        wc_ref[h // 2, (h % 2) * TOK : (h % 2 + 1) * TOK, :] = w.astype(BF)


def row_inside_kernel(
    core_ref, x_ref, g_ref, w_ref, wo_ref, kv_ref, wr_ref, q_ref, dn_ref, keep_ref, send_ref, out_ref, probs_ref
):
    core = core_ref[0]
    send_ref[...] = nt(pick_rows(1 - core), x_ref[...]).astype(BF)
    keep_ref[...] = nt(pick_rows(core), x_ref[...]).astype(BF)
    q_ref[...] = nn(x_ref[...], w_ref[:, :D]).astype(BF)
    dn_ref[...] = nt(g_ref[...], wo_ref[...]).astype(BF)
    for r in range(ROWS):
        rows = slice(r * COLS, (r + 1) * COLS)
        for p in range(PAIRS):
            lanes = slice(p * 128, (p + 1) * 128)
            k = kv_ref[rows, lanes]
            v = kv_ref[rows, D + p * 128 : D + (p + 1) * 128]
            n = r * PAIRS + p
            probs = (nt(split_heads(q_ref[rows, lanes]), k) * wr_ref[n].astype(F32)).astype(BF)
            probs_ref[n] = probs
            out_ref[rows, lanes] = nn(side(probs), split_heads(v))


def col_forward_kernel(
    core_ref, rx_ref, w_ref, wo_ref, wc_ref, qkv_ref, dn_ref, out_ref, probs_ref, keep_ref, send_ref
):
    x = rx_ref[:, 0:16, :].reshape(TOK, D)
    g = rx_ref[:, 16:32, :].reshape(TOK, D)
    qkv_ref[...] = nn(x, w_ref[...]).astype(BF)
    for p in range(PAIRS):
        q = qkv_ref[:, p * 128 : (p + 1) * 128]
        k = qkv_ref[:, D + p * 128 : D + (p + 1) * 128]
        v = qkv_ref[:, 2 * D + p * 128 : 2 * D + (p + 1) * 128]
        probs = (nt(split_heads(q), k) * wc_ref[p].astype(F32)).astype(BF)
        probs_ref[p] = probs
        out_ref[:, p * 128 : (p + 1) * 128] = nn(side(probs), split_heads(v)).astype(BF)
    dn_ref[...] = nt(g, wo_ref[...]).astype(BF)
    core = core_ref[0]
    keep_ref[...] = nt(pick_rows(core), x).astype(BF)
    send_ref[...] = nt(pick_rows(1 - core), x).astype(BF)


def state_of(s_ref, direction, r, p):
    return s_ref[direction, unit_rows(r, p), :]


def both_states(s_ref, r, p):
    return jnp.concatenate([split_heads(state_of(s_ref, d, r, p)) for d in range(2)], axis=1)


def row_join_kernel(place_ref, q_ref, rs_ref, fac_ref, inside_ref, col_ref, out_ref, xch_ref, s_ref, wide_ref):
    gather_states(place_ref[0], rs_ref, True, wide_ref)
    s_ref[...] = wide_ref[...].astype(BF)
    xch_ref[:, 0:16, :] = col_ref[...].reshape(16, 16, D)
    for r in range(ROWS):
        rows = slice(r * COLS, (r + 1) * COLS)
        for p in range(PAIRS):
            lanes = slice(p * 128, (p + 1) * 128)
            carried = nn(q_ref[rows, lanes], both_states(s_ref, r, p))
            out = inside_ref[rows, lanes]
            out = out + lanes_of(fac_ref[0, r], p) * carried[:, :128]
            out = out + lanes_of(fac_ref[1, r], p) * carried[:, 128:]
            out_ref[rows, lanes] = out
    slab = out_ref[...].reshape(2, 16, 8, D).swapaxes(0, 1).reshape(16, 16, D)
    xch_ref[:, 16:32, :] = slab.astype(BF)


def norm_backward(mixed, dn, gain):
    inv = lax.rsqrt(jnp.mean(mixed * mixed, axis=-1, keepdims=True) + EPSILON)
    unit = mixed * inv
    scaled = dn * gain
    d_mixed = inv * (scaled - unit * jnp.mean(scaled * unit, axis=-1, keepdims=True))
    return unit, d_mixed


def from_slab(x):
    return x.astype(F32).reshape(16, 2, 8, D).swapaxes(0, 1).reshape(TOK, D)


def row_middle_kernel(
    place_ref, rx_ref, row_ref, dn_ref, gain_ref, q_ref, fac_ref, th_ref, dm_ref, g_ref, both_ref
):
    mixed = row_ref[...] + from_slab(rx_ref[:, 0:16, :])
    _, d_mixed = norm_backward(mixed, dn_ref[...].astype(F32), gain_ref[...])
    dm_ref[...] = d_mixed.astype(BF)
    for r in range(ROWS):
        rows = slice(r * COLS, (r + 1) * COLS)
        for p in range(PAIRS):
            q = q_ref[rows, p * 128 : (p + 1) * 128]
            do = d_mixed[rows, p * 128 : (p + 1) * 128]
            for direction in range(2):
                eo = (lanes_of(fac_ref[direction, r], p) * do).astype(BF)
                both_ref[direction, unit_rows(r, p), :] = compact(tn(q, eo)).astype(BF)
    both_ref[:, STATE:LOAD, :] = th_ref[...].astype(BF)
    spread(both_ref, place_ref[0], False, g_ref)


def local_backward(q, k, v, do, w, probs):
    q2, do2 = split_heads(q), split_heads(do)
    dp = nt(do2, v)
    dw = (dp * w.astype(F32)).astype(BF)
    both = (dp * probs.astype(F32)).astype(BF)
    dq = nn(side(dw), split_heads(k))
    dk = tn(dw, q2)
    dv = tn(probs, do2)
    return dq, dk, dv, both


def col_backward_kernel(
    rx_ref, col_ref, dn_ref, gain_ref, qkv_ref, wc_ref, probs_ref, w_ref, dqkv_ref, gd_ref, tok_ref
):
    mixed = rx_ref[:, 16:32, :].reshape(TOK, D).astype(F32) + col_ref[...].astype(F32)
    _, d_mixed = norm_backward(mixed, dn_ref[...].astype(F32), gain_ref[...])
    d_mixed = d_mixed.astype(BF)
    j0, j1 = iota((TOK, TOK), 0), iota((TOK, TOK), 1)
    same = (j0 & 7) == (j1 & 7)
    k0, k1 = j0 >> 3, j1 >> 3
    before, behind = (same & (k0 < k1)).astype(BF), (same & (k0 > k1)).astype(BF)
    table = jnp.concatenate([before, behind], axis=1)
    for p in range(PAIRS):
        lanes = slice(p * 128, (p + 1) * 128)
        q = qkv_ref[:, p * 128 : (p + 1) * 128]
        k = qkv_ref[:, D + p * 128 : D + (p + 1) * 128]
        v = qkv_ref[:, 2 * D + p * 128 : 2 * D + (p + 1) * 128]
        dq, dk, dv, both = local_backward(q, k, v, d_mixed[:, lanes], wc_ref[p], probs_ref[p])
        dqkv_ref[:, p * 128 : (p + 1) * 128] = dq.astype(BF)
        dqkv_ref[:, D + p * 128 : D + (p + 1) * 128] = dk.astype(BF)
        dqkv_ref[:, 2 * D + p * 128 : 2 * D + (p + 1) * 128] = dv.astype(BF)
        sums = nn(both, table)
        for half in range(2):
            part = sums[half * TOK : (half + 1) * TOK]
            h = 2 * p + half
            gd_ref[0, h : h + 1, :] = jnp.sum(jnp.where(k0 >= k1, part[:, :TOK], 0.0), axis=0, keepdims=True)
            gd_ref[1, h : h + 1, :] = jnp.sum(jnp.where(k0 <= k1, part[:, TOK:], 0.0), axis=0, keepdims=True)
    tok_ref[...] = nt(dqkv_ref[...], w_ref[...]).astype(BF)


def row_local_kernel(
    core_ref, rx_ref, row_ref, dn_ref, gain_ref, q_ref, kv_ref, dm_ref, s_ref, wr_ref, probs_ref, fac_ref,
    dq_ref, part_ref, gd_ref, keep_ref, send_ref,
):
    mixed = row_ref[...] + from_slab(rx_ref[:, 0:16, :])
    unit = mixed * lax.rsqrt(jnp.mean(mixed * mixed, axis=-1, keepdims=True) + EPSILON)
    normed = (unit * gain_ref[...]).astype(BF)
    gain_terms = (dn_ref[...].astype(F32) * unit).astype(BF)
    core = core_ref[0]
    for ref, c in ((keep_ref, core), (send_ref, 1 - core)):
        pick = pick_rows(c)
        ref[0 : D // 2, :] = nt(pick, normed).astype(BF)
        ref[D // 2 : D, :] = nt(pick, gain_terms).astype(BF)
    i0, i1 = iota((COLS, COLS), 0), iota((COLS, COLS), 1)
    table = jnp.concatenate([(i0 < i1).astype(BF), (i0 > i1).astype(BF)], axis=1)
    entries = [[], []]
    for r in range(ROWS):
        rows = slice(r * COLS, (r + 1) * COLS)
        for p in range(PAIRS):
            lanes = slice(p * 128, (p + 1) * 128)
            q = q_ref[rows, lanes]
            k = kv_ref[rows, lanes]
            v = kv_ref[rows, D + p * 128 : D + (p + 1) * 128]
            do = dm_ref[rows, lanes]
            n = r * PAIRS + p
            dq, dk, dv, both = local_backward(q, k, v, do, wr_ref[n], probs_ref[n])
            states = both_states(s_ref, r, p)
            wide_do = do.astype(F32)
            eo = [lanes_of(fac_ref[d, r], p) * wide_do for d in range(2)]
            dq = dq + nt(jnp.concatenate(eo, axis=1).astype(BF), states)
            carried = nn(q, states)
            dq_ref[rows, lanes] = dq.astype(BF)
            part_ref[rows, lanes] = dk
            part_ref[rows, D + p * 128 : D + (p + 1) * 128] = dv
            sums = nn(both, table)
            for direction in range(2):
                entries[direction].append(
                    (carried[:, direction * 128 : (direction + 1) * 128] * eo[direction]).astype(BF)
                )
                keep = (i0 >= i1) if direction == 0 else (i0 <= i1)
                for half in range(2):
                    piece = sums[half * COLS : (half + 1) * COLS, direction * COLS : (direction + 1) * COLS]
                    n = r * HEADS + 2 * p + half
                    gd_ref[direction, n : n + 1, :] = jnp.sum(jnp.where(keep, piece, 0.0), axis=0, keepdims=True)
    heads = per_head((32, 2 * D))
    for direction in range(2):
        keep = ((i0 >= i1) if direction == 0 else (i0 <= i1)).astype(BF)
        total = nt(heads, jnp.concatenate(entries[direction], axis=1))
        gd_ref[direction] += nn(total.astype(BF), keep)[: 2 * HEADS]


def row_finish_kernel(
    place_ref, kv_ref, s_ref, ra_ref, fac_ref, th_ref, part_ref, gdp_ref, dkv_ref, gd_ref, wide_ref, a_ref
):
    gather_states(place_ref[0], ra_ref, False, wide_ref)
    a_ref[...] = wide_ref[...].astype(BF)
    i0, i1 = iota((COLS, COLS), 0), iota((COLS, COLS), 1)
    tails, throughs = [[], []], [[], []]
    for r in range(ROWS):
        rows = slice(r * COLS, (r + 1) * COLS)
        for p in range(PAIRS):
            lanes = slice(p * 128, (p + 1) * 128)
            far = slice(D + p * 128, D + (p + 1) * 128)
            k = kv_ref[rows, lanes]
            v = kv_ref[rows, far].astype(F32)
            adjoints = both_states(a_ref, r, p)
            tail = [lanes_of(fac_ref[2 + d, r], p) for d in range(2)]
            tv = [t * v for t in tail]
            dk = part_ref[rows, lanes] + nt(jnp.concatenate(tv, axis=1).astype(BF), adjoints)
            leaving = nn(k, adjoints)
            dv = part_ref[rows, far] + tail[0] * leaving[:, :128] + tail[1] * leaving[:, 128:]
            dkv_ref[rows, lanes] = dk.astype(BF)
            dkv_ref[rows, far] = dv.astype(BF)
            for d in range(2):
                tails[d].append((leaving[:, d * 128 : (d + 1) * 128] * tv[d]).astype(BF))
                n = r * PAIRS + p
                prod = state_of(s_ref, d, r, p).astype(F32) * state_of(a_ref, d, r, p).astype(F32)
                throughs[d].append(th_ref[d, n : n + 1, :] * jnp.sum(prod, axis=0, keepdims=True))
    heads = per_head((32, 2 * D))
    for d in range(2):
        before = ((i0 < i1) if d == 0 else (i0 > i1)).astype(BF)
        total = nt(heads, jnp.concatenate(tails[d], axis=1))
        through = jnp.broadcast_to(jnp.concatenate(throughs[d], axis=1), (8, 2 * D)).astype(BF)
        through = nt(heads, through)[: 2 * HEADS, 0:1]
        gd_ref[d] = gdp_ref[d] + nn(total.astype(BF), before)[: 2 * HEADS] + through


def weight_early_kernel(
    xk_ref, xr_ref, xck_ref, xcr_ref, dq_ref, dqr_ref, dc_ref, dcr_ref, nk_ref, nr_ref, g_ref, gr_ref, out_ref
):
    x = jnp.concatenate([xk_ref[...], xr_ref[...], xck_ref[...], xcr_ref[...]], axis=1)

    def put(value, start):
        out_ref[:, :, start : start + value.shape[1]] = value.astype(BF).reshape(8, 48, -1)

    for start in range(0, D, 384):
        cols = slice(start, start + 384)
        d = [dq_ref[:, cols], dqr_ref[:, cols], dc_ref[:, cols], dcr_ref[:, cols]]
        put(nn(x, jnp.concatenate(d, axis=0)), start)
    normed = jnp.concatenate([nk_ref[0 : D // 2, :], nr_ref[0 : D // 2, :]], axis=1)
    gain_terms = jnp.concatenate([nk_ref[D // 2 : D, :], nr_ref[D // 2 : D, :]], axis=1)
    for start in range(0, D, 384):
        d = jnp.concatenate([g_ref[:, start : start + 384], gr_ref[:, start : start + 384]], axis=0)
        put(nn(normed, d), D + start)
    put(nn(gain_terms, jnp.ones((2 * TOK, 128), BF)), 2 * D)


def weight_late_kernel(
    xk_ref, xr_ref, xck_ref, xcr_ref, dkv_ref, dkvr_ref, dc_ref, dcr_ref, early_ref, out_ref
):
    x = jnp.concatenate([xk_ref[...], xr_ref[...], xck_ref[...], xcr_ref[...]], axis=1)
    out_ref[:, :, 2 * D :] = early_ref[...]
    for start in range(0, 2 * D, 384):
        cols, far = slice(start, start + 384), slice(D + start, D + start + 384)
        d = [dkv_ref[:, cols], dkvr_ref[:, cols], dc_ref[:, far], dcr_ref[:, far]]
        out_ref[:, :, cols] = nn(x, jnp.concatenate(d, axis=0)).astype(BF).reshape(8, 48, 384)


def token_kernel(dq_ref, dkv_ref, w_ref, rx_ref, out_ref):
    total = nt(dq_ref[...], w_ref[:, :D]) + nt(dkv_ref[...], w_ref[:, D:])
    out_ref[...] = (total + from_slab(rx_ref[...])).astype(BF)


def exchange(x, axis, groups=None):
    return lax.all_to_all(x, axis, 0, 0, tiled=True, axis_index_groups=groups)


def swap(x):
    return lax.ppermute(x, "row", CORE_SWAP)


def after(value, *others):
    return lax.optimization_barrier((value, *others))[0]


def per_device(
    tokens, grad_out, w_qkv, w_out, gain, log_decay_rows, log_decay_cols, border_cols, border_rows
):
    place = lax.axis_index("col")
    at = place.astype(jnp.int32).reshape(1)
    core = (lax.axis_index("row") % 2).astype(jnp.int32).reshape(1)
    x = tokens.reshape(TOK, D)
    g = grad_out.reshape(TOK, D)
    gain = gain.reshape(1, D)
    half = (D // 2, TOK)
    load = ((8, LOAD, 128), BF)
    wide = pltpu.VMEM((2, STATE, 128), F32)
    narrow = pltpu.VMEM((2, LOAD, 128), BF)

    def slab(a):
        return a.reshape(ROWS, 16, CD, D).swapaxes(0, 1).reshape(16, ROWS * CD, D)

    rx = exchange(jnp.concatenate([slab(tokens), slab(grad_out)], axis=1), "row")

    ldr = log_decay_rows.transpose(2, 0, 1, 3)
    ldc = log_decay_cols.swapaxes(2, 3).reshape(2, HEADS, TOK)
    tiles = jnp.concatenate([border_cols, jnp.zeros((COLS,), jnp.int32)]).reshape(9, COLS)
    bc = lax.dynamic_slice_in_dim(tiles, place, 2)
    br = jnp.broadcast_to(border_rows[:, None], (GRID_H, CD)).reshape(1, TOK)
    fac, th, kv, update = call(
        summary_kernel, 4.6,
        [((4, ROWS, COLS, HEADS), F32), ((2, 16, 128), F32), ((TOK, 2 * D), BF), load],
        at, ldr, bc, x, w_qkv, smem=(0,), scratch=[narrow],
    )
    wr, wc = call(
        mask_kernel, 4.3,
        [((UNITS, 2 * COLS, COLS), BF), ((PAIRS, 2 * TOK, TOK), BF)],
        ldr, ldc, bc, br, th,
    )
    states = exchange(after(update, rx, wr), "col")
    q, dn, x_keep, x_send, inside, probs = call(
        row_inside_kernel, 5.7,
        [((TOK, D), BF), ((TOK, D), BF), (half, BF), (half, BF), ((TOK, D), F32), ((UNITS, 2 * COLS, COLS), BF)],
        core, x, g, w_qkv, w_out, kv, wr, smem=(0,),
    )
    x_far, g_far = swap(x_send), swap(g)
    qkv_c, dn_c, col_out, probs_c, xc_keep, xc_send = call(
        col_forward_kernel, 6.8,
        [((TOK, F), BF), ((TOK, D), BF), ((TOK, D), BF), ((PAIRS, 2 * TOK, TOK), BF), (half, BF), (half, BF)],
        core, rx, w_qkv, w_out, wc, smem=(0,),
    )
    states = after(states, col_out, q)
    row_out, out_swap, entering = call(
        row_join_kernel, 5.0,
        [((TOK, D), F32), ((16, 32, D), BF), ((2, STATE, 128), BF)],
        at, q, states, fac, inside, col_out, smem=(0,), scratch=[wide],
    )
    xc_far = swap(xc_send)
    rx2 = exchange(out_swap, "row")
    rx2, x_far, g_far, xc_far = lax.optimization_barrier((rx2, x_far, g_far, xc_far))
    dm, adj = call(
        row_middle_kernel, 4.5,
        [((TOK, D), BF), load],
        at, rx2, row_out, dn, gain, q, fac, th, smem=(0,), scratch=[narrow],
    )
    adj = exchange(adj, "col")
    dq, part, gd_part, n_keep, n_send = call(
        row_local_kernel, 8.9,
        [((TOK, D), BF), ((TOK, 2 * D), F32), ((2, 2 * HEADS, COLS), F32), ((D, TOK), BF), ((D, TOK), BF)],
        core, rx2, row_out, dn, gain, q, kv, dm, entering, wr, probs, fac, smem=(0,),
    )
    n_far, dq_far = swap(n_send), swap(dq)
    dqkv_c, gdc, tok_c = call(
        col_backward_kernel, 9.7,
        [((TOK, F), BF), ((2, HEADS, TOK), F32), ((TOK, D), BF)],
        after(rx2, dm), col_out, dn_c, gain, qkv_c, wc, probs_c, w_qkv,
    )
    dqkv_c_far = swap(dqkv_c)
    adj, n_far, dq_far, tok_c = lax.optimization_barrier((adj, n_far, dq_far, tok_c))
    rx3 = exchange(tok_c.reshape(16, 16, D), "row")
    dkv, gdr = call(
        row_finish_kernel, 5.5,
        [((TOK, 2 * D), BF), ((2, 2 * HEADS, COLS), F32)],
        at, kv, entering, adj, fac, th, part, gd_part,
        smem=(0,), scratch=[wide, pltpu.VMEM((2, STATE, 128), BF)],
    )
    dkv_far = swap(dkv)
    (early,) = call(
        weight_early_kernel, 5.0,
        [((8, 48, 2 * D + 128), BF)],
        x_keep, x_far, xc_keep, xc_far, after(dq, dkv), dq_far, dqkv_c, dqkv_c_far, n_keep, n_far, g, g_far,
    )
    (wg,) = call(
        weight_late_kernel, 6.0,
        [((8, 48, WIDE), BF)],
        x_keep, x_far, xc_keep, xc_far, dkv, dkv_far, dqkv_c, dqkv_c_far, early,
    )
    wg = exchange(after(wg, rx3), "row", EVEN_ODD)
    wg = jnp.sum(wg.astype(F32), axis=0).astype(BF).reshape(8, 6, WIDE)
    wg = exchange(wg, "col")
    wg = jnp.sum(wg.astype(F32), axis=0) * (32768.0 ** (-0.5))
    (grad_tokens,) = call(token_kernel, 4.0, [((TOK, D), BF)], dq, dkv, w_qkv, rx3)
    gdr = gdr.reshape(2, ROWS, HEADS, COLS).swapaxes(1, 2)
    return (
        grad_tokens.reshape(ROWS, COLS, D),
        jnp.concatenate([wg[:, 2 * D : 3 * D], wg[:, : 2 * D]], axis=1),
        wg[:, F : F + D],
        wg[:, F + D],
        gdr.astype(BF),
        gdc.astype(BF).reshape(2, HEADS, GRID_H, CD).swapaxes(2, 3),
    )


def solution(mesh):
    in_specs = (
        P("row", "col", None),
        P("row", "col", None),
        P(),
        P(),
        P(),
        P(None, None, "row", "col"),
        P(None, None, ("col", "row"), None),
        P(),
        P(),
    )
    out_specs = (
        P("row", "col", None),
        P(("row", "col"), None),
        P(("row", "col"), None),
        P(("row", "col")),
        P(None, None, "row", "col"),
        P(None, None, ("col", "row"), None),
    )
    return jax.shard_map(
        per_device, mesh=mesh, in_specs=in_specs, out_specs=out_specs, check_vma=False
    )
```

time: 224 us -> 190 us (0.85)
  blocking collectives: 48.5 us -> 0 us
  waiting for transfers between devices: 54.3 us -> 63.1 us
  starting transfers between devices: 32.8 us -> 37.9 us
  Pallas kernels: 67.2 us -> 70.2 us
  other arithmetic: 5.07 us -> 2.1 us
    all_to_all x2 -> x0, blocking collectives: 48.5 us -> none  [exchange(): return lax.all_to_all(x, axis, 0, 0, tiled=True, axis_index_groups=groups)]
    all_to_all x7, waiting for transfers between devices: 49.5 us -> 62.3 us  [exchange(): return lax.all_to_all(x, axis, 0, 0, tiled=True, axis_index_groups=groups)]
    ppermute x1 -> x7, waiting for transfers between devices: 4.79 us -> 0.82 us  [swap(): return lax.ppermute(x, 'row', CORE_SWAP)]
    all_to_all x7, starting transfers between devices: 32.7 us -> 36.3 us  [exchange(): return lax.all_to_all(x, axis, 0, 0, tiled=True, axis_index_groups=groups)]
    unnamed x24 -> x45, local copies, waits for them, and re-layouts: 4.46 us -> 7.82 us
    convert_element_type x1 -> x0, other arithmetic: 2.99 us -> none  [per_device(): wg = (mine.astype(F32) + other.astype(F32)).astype(BF)]
    pallas_call x11 -> x12, Pallas kernels: 67.2 us -> 70.2 us  [call(): pl.pallas_call(body, out_shape=[jax.ShapeDtypeStruct(s, t) for s, t in ou...]
  transfers between devices with their start and end apart: 8 -> 14, of which waited for: 7 -> 8; matrix products, arithmetic and copies ran while one was open for 2% -> 3% of each run, Pallas kernels for 10% -> 32%
where the time goes in v2:
time: 190 us; the launch traced here: 189 us
  Pallas kernels  70.2 us (37%)
  waiting for transfers between devices  63.1 us (33%)
  starting transfers between devices  37.9 us (20%)
  local copies, waits for them, and re-layouts  15.1 us (8%)
  other arithmetic  2.1 us (1%)
    pallas_call x12, Pallas kernels, call(): pl.pallas_call(body, out_shape=[jax.ShapeDtypeStruct(s, t) for s, t in ou...  70.2 us
    all_to_all x7, waiting for transfers between devices, exchange(): return lax.all_to_all(x, axis, 0, 0, tiled=True, axis_index_groups=groups)  62.3 us
    all_to_all x7, starting transfers between devices, exchange(): return lax.all_to_all(x, axis, 0, 0, tiled=True, axis_index_groups=groups)  36.3 us
    unnamed x45, local copies, waits for them, and re-layouts  7.82 us
  transfers between devices with their start and end apart: 14, of which 8 were waited for; matrix products, arithmetic and copies ran while one was open for 3% of the time, Pallas kernels for 32%

profile of v2, /device:TPU:0, one launch (start us, length us, event | category | flops | bytes accessed | tf_op | source)
XLA Modules:
  0.0 189.3 jit_solution(17557758113881318204)
XLA Ops:
  0.6 1.0 copy_bitcast_fusion
  1.7 1.0 copy_bitcast_fusion.1
  2.7 1.0 pad_maximum_fusion
  3.7 8.1 %all-to-all-start = ((bf16[16,32,768]{2,1,0:T(8,128)(2,1)}), bf16[16,32,768]{2,1,0:T(8,128)(2,1)S(1)}, u32[]{:S(2)}, u32[]{:S(2)}) async-start(bf16[16,32,768]{2,1,0:T(8,128)(2,1)} %pad_maximum_fusion), calls=%async_computation | async-start | bytes 1572864 | tf_op jit(solution)/shard_map/all_to_all | solution.py:456
  14.8 5.1 %shard_map.136 = (f32[4,2,128,12]{3,2,1,0:T(8,128)}, f32[2,16,128]{2,1,0:T(8,128)}, bf16[256,1536]{1,0:T(8,128)(2,1)}, bf16[8,784,128]{2,1,0:T(8,128)(2,1)}) custom-call(s32[1]{0:T(128)} %bitcast.1.place_ref, bf16[2,2,12,128]{3,2,1,0:T(8,128)(2,1)} %bitcast.42, s32[2,128]{1,0:T(2,128)} %constant_dynamic-slice_fusion.bc_ref, bf16[256,768]{1,0:T(8,128)(2,1)} %bitcast.35, ...), custom_call_target="tpu_custom_call" | custom-call | flops 5059999744 | bytes 16559999 | tf_op jit(solution)/shard_map/pallas_call | solution.py:36
  19.8 4.1 %shard_map.137 = (bf16[12,256,128]{2,1,0:T(8,128)(2,1)}, bf16[6,512,256]{2,1,0:T(8,128)(2,1)}) custom-call(bf16[2,2,12,128]{3,2,1,0:T(8,128)(2,1)} %bitcast.43, bf16[2,12,256]{2,1,0:T(8,128)(2,1)} %reshape.79.ldc_ref, s32[2,128]{1,0:T(2,128)} %constant_dynamic-slice_fusion.bc_ref, s32[1,256]{1,0:T(1,128)} %reshape.69.br_ref, ...), custom_call_target="tpu_custom_call" | custom-call | flops 4729999872 | bytes 15480000 | tf_op jit(solution)/shard_map/pallas_call | solution.py:36
  24.0 3.0 %all-to-all-done.rx_ref = bf16[16,32,768]{2,1,0:T(8,128)(2,1)S(1)} async-done(((bf16[16,32,768]{2,1,0:T(8,128)(2,1)}), bf16[16,32,768]{2,1,0:T(8,128)(2,1)S(1)}, u32[]{:S(2)}, u32[]{:S(2)}) %all-to-all-start) | async-done | bytes 786464 | tf_op jit(solution)/shard_map/all_to_all | solution.py:456
  27.9 4.5 %all-to-all-start.1 = ((bf16[8,784,128]{2,1,0:T(8,128)(2,1)}), bf16[8,784,128]{2,1,0:T(8,128)(2,1)S(1)}, u32[]{:S(2)}, u32[]{:S(2)}) async-start(bf16[8,784,128]{2,1,0:T(8,128)(2,1)} %get-tuple-element.57), calls=%async_computation.1 | async-start | bytes 3211264 | tf_op jit(solution)/shard_map/all_to_all | solution.py:456
  32.4 5.7 %shard_map.138 = (bf16[256,768]{1,0:T(8,128)(2,1)}, bf16[256,768]{1,0:T(8,128)(2,1)}, bf16[384,256]{1,0:T(8,128)(2,1)}, bf16[384,256]{1,0:T(8,128)(2,1)}, f32[25...) custom-call(s32[1]{0:T(128)} %bitcast.core_ref, bf16[256,768]{1,0:T(8,128)(2,1)} %bitcast.36, bf16[256,768]{1,0:T(8,128)(2,1)} %bitcast.37, ...), custom_call_target="tpu_custom_call" | custom-call | flops 6270000128 | bytes 20520000 | tf_op jit(solution)/shard_map/pallas_call | solution.py:36
  38.1 6.7 %shard_map.139 = (bf16[256,2304]{1,0:T(8,128)(2,1)}, bf16[256,768]{1,0:T(8,128)(2,1)}, bf16[256,768]{1,0:T(8,128)(2,1)}, bf16[6,512,256]{2,1,0:T(8,128)(2,1)}, b...) custom-call(s32[1]{0:T(128)} %bitcast.core_ref, bf16[16,32,768]{2,1,0:T(8,128)(2,1)} %copy-done.2, ...), custom_call_target="tpu_custom_call" | custom-call | flops 7480000000 | bytes 24480000 | tf_op jit(solution)/shard_map/pallas_call | solution.py:36
  44.8 9.0 %all-to-all-done.1.rs_ref = bf16[8,784,128]{2,1,0:T(8,128)(2,1)S(1)} async-done(((bf16[8,784,128]{2,1,0:T(8,128)(2,1)}), bf16[8,784,128]{2,1,0:T(8,128)(2,1)S(1)}, u32[]{:S(2)}, u32[]{:S(2)}) %all-to-all-start.1) | async-done | bytes 1605664 | tf_op jit(solution)/shard_map/all_to_all | solution.py:456
  53.8 1.2 copy-done
  55.0 4.7 %shard_map.140 = (f32[256,768]{1,0:T(8,128)}, bf16[16,32,768]{2,1,0:T(8,128)(2,1)}, bf16[2,768,128]{2,1,0:T(8,128)(2,1)}) custom-call(s32[1]{0:T(128)} %bitcast.1.place_ref, bf16[256,768]{1,0:T(8,128)(2,1)} %get-tuple-element.55.q_ref, bf16[8,784,128]{2,1,0:T(8,128)(2,1)} %copy-done, f32[4,2,128,12]{3,2,1,0:T(8,128)} %get-tuple-element.61.fac_ref, ...), custom_call_target="tpu_custom_call" | custom-call | flops 5500000256 | bytes 18000000 | tf_op jit(solution)/shard_map/pallas_call | solution.py:36
  59.7 5.5 %all-to-all-start.2 = ((bf16[16,32,768]{2,1,0:T(8,128)(2,1)}), bf16[16,32,768]{2,1,0:T(8,128)(2,1)S(1)}, u32[]{:S(2)}, u32[]{:S(2)}) async-start(bf16[16,32,768]{2,1,0:T(8,128)(2,1)} %get-tuple-element.63), calls=%async_computation.2 | async-start | bytes 1572864 | tf_op jit(solution)/shard_map/all_to_all | solution.py:456
  67.6 12.8 %all-to-all-done.2.rx_ref = bf16[16,32,768]{2,1,0:T(8,128)(2,1)S(1)} async-done(((bf16[16,32,768]{2,1,0:T(8,128)(2,1)}), bf16[16,32,768]{2,1,0:T(8,128)(2,1)S(1)}, u32[]{:S(2)}, u32[]{:S(2)}) %all-to-all-start.2) | async-done | bytes 786464 | tf_op jit(solution)/shard_map/all_to_all | solution.py:456
  80.3 0.9 copy-done.3
  81.2 4.5 %shard_map.141 = (bf16[256,768]{1,0:T(8,128)(2,1)}, bf16[8,784,128]{2,1,0:T(8,128)(2,1)}) custom-call(s32[1]{0:T(128)} %bitcast.1.place_ref, bf16[16,32,768]{2,1,0:T(8,128)(2,1)} %copy-done.3, f32[256,768]{1,0:T(8,128)} %get-tuple-element.67.row_ref, bf16[256,768]{1,0:T(8,128)(2,1)} %get-tuple-element.68.dn_ref, f32[1,768]{1,0:T(1,128)} %reshape.74.gain_ref, ...), custom_call_target="tpu_custom_call" | custom-call | flops 4950000128 | bytes 16200000 | tf_op jit(solution)/shard_map/pallas_call | solution.py:36
  85.8 3.6 %all-to-all-start.3 = ((bf16[8,784,128]{2,1,0:T(8,128)(2,1)}), bf16[8,784,128]{2,1,0:T(8,128)(2,1)S(1)}, u32[]{:S(2)}, u32[]{:S(2)}) async-start(bf16[8,784,128]{2,1,0:T(8,128)(2,1)} %get-tuple-element.73), calls=%async_computation.3 | async-start | bytes 3211264 | tf_op jit(solution)/shard_map/all_to_all | solution.py:456
  89.4 8.9 %shard_map.142 = (bf16[256,768]{1,0:T(8,128)(2,1)}, f32[256,1536]{1,0:T(8,128)}, f32[2,24,128]{2,1,0:T(8,128)}, bf16[768,256]{1,0:T(8,128)(2,1)}, bf16[768,256]{1,0:T(8,128)(2,1)}) custom-call(s32[1]{0:T(128)} %bitcast.core_ref, bf16[16,32,768]{2,1,0:T(8,128)(2,1)} %copy-done.3, f32[256,768]{1,0:T(8,128)} %get-tuple-element.67.row_ref, ...), custom_call_target="tpu_custom_call" | custom-call | flops 9790000128 | bytes 32040000 | tf_op jit(solution)/shard_map/pallas_call | solution.py:36
  98.8 9.5 %shard_map.143 = (bf16[256,2304]{1,0:T(8,128)(2,1)}, f32[2,12,256]{2,1,0:T(8,128)}, bf16[256,768]{1,0:T(8,128)(2,1)}) custom-call(bf16[16,32,768]{2,1,0:T(8,128)(2,1)} %copy-done.3, bf16[256,768]{1,0:T(8,128)(2,1)} %get-tuple-element.59.col_ref, bf16[256,768]{1,0:T(8,128)(2,1)} %get-tuple-element.76.dn_ref, f32[1,768]{1,0:T(1,128)} %reshape.74.gain_ref, ...), custom_call_target="tpu_custom_call" | custom-call | flops 10670000128 | bytes 34920000 | tf_op jit(solution)/shard_map/pallas_call | solution.py:36
  108.4 2.7 %all-to-all-done.3.ra_ref = bf16[8,784,128]{2,1,0:T(8,128)(2,1)S(1)} async-done(((bf16[8,784,128]{2,1,0:T(8,128)(2,1)}), bf16[8,784,128]{2,1,0:T(8,128)(2,1)S(1)}, u32[]{:S(2)}, u32[]{:S(2)}) %all-to-all-start.3) | async-done | bytes 1605664 | tf_op jit(solution)/shard_map/all_to_all | solution.py:456
  111.1 1.2 copy-done.1
  112.3 5.4 %shard_map.144 = (bf16[256,1536]{1,0:T(8,128)(2,1)}, f32[2,24,128]{2,1,0:T(8,128)}) custom-call(s32[1]{0:T(128)} %bitcast.1.place_ref, bf16[256,1536]{1,0:T(8,128)(2,1)} %get-tuple-element.52.kv_ref, bf16[2,768,128]{2,1,0:T(8,128)(2,1)} %get-tuple-element.70.s_ref, bf16[8,784,128]{2,1,0:T(8,128)(2,1)} %copy-done.1, ...), custom_call_target="tpu_custom_call" | custom-call | flops 6049999872 | bytes 19800000 | tf_op jit(solution)/shard_map/pallas_call | solution.py:36
  117.7 3.6 %all-to-all-start.4 = ((bf16[16,16,768]{2,1,0:T(8,128)(2,1)}), bf16[16,16,768]{2,1,0:T(8,128)(2,1)S(1)}, u32[]{:S(2)}, u32[]{:S(2)}) async-start(bf16[16,16,768]{2,1,0:T(8,128)(2,1)} %bitcast.13), calls=%async_computation.4 | async-start | bytes 786432 | tf_op jit(solution)/shard_map/all_to_all | solution.py:456
  121.3 5.2 %shard_map.146.early_ref = bf16[8,48,1664]{2,1,0:T(8,128)(2,1)} custom-call(bf16[384,256]{1,0:T(8,128)(2,1)} %get-tuple-element.85.xk_ref, bf16[384,256]{1,0:T(8,128)(2,1)} %copy-done.17, bf16[384,256]{1,0:T(8,128)(2,1)} %get-tuple-element.87.xck_ref, bf16[384,256]{1,0:T(8,128)(2,1)} %copy-done.18, bf16[256,768]{1,0:T(8,128)(2,1)} %get-tuple-element.90.dq_ref, ...), custom_call_target="tpu_custom_call" | custom-call | flops 5500000256 | bytes 18000000 | tf_op jit(solution)/shard_map/pallas_call | solution.py:36
  126.5 0.9 copy-done.13
  127.4 6.1 %shard_map.147 = bf16[8,48,3200]{2,1,0:T(8,128)(2,1)} custom-call(bf16[384,256]{1,0:T(8,128)(2,1)} %get-tuple-element.85.xk_ref, bf16[384,256]{1,0:T(8,128)(2,1)} %copy-done.17, bf16[384,256]{1,0:T(8,128)(2,1)} %get-tuple-element.87.xck_ref, bf16[384,256]{1,0:T(8,128)(2,1)} %copy-done.18, bf16[256,1536]{1,0:T(8,128)(2,1)} %get-tuple-element.83.dkv_ref, ...), custom_call_target="tpu_custom_call" | custom-call | flops 6600000000 | bytes 21600000 | tf_op jit(solution)/shard_map/pallas_call | solution.py:36
  134.3 7.0 %all-to-all-start.5 = ((bf16[8,48,3200]{2,1,0:T(8,128)(2,1)}), bf16[8,48,3200]{2,1,0:T(8,128)(2,1)S(1)}, u32[]{:S(2)}, u32[]{:S(2)}) async-start(bf16[8,48,3200]{2,1,0:T(8,128)(2,1)} %shard_map.147), calls=%async_computation.5 | async-start | bytes 4915200 | tf_op jit(solution)/shard_map/all_to_all | solution.py:456
  143.0 31.0 %all-to-all-done.5 = bf16[8,48,3200]{2,1,0:T(8,128)(2,1)S(1)} async-done(((bf16[8,48,3200]{2,1,0:T(8,128)(2,1)}), bf16[8,48,3200]{2,1,0:T(8,128)(2,1)S(1)}, u32[]{:S(2)}, u32[]{:S(2)}) %all-to-all-start.5) | async-done | bytes 2457632 | tf_op jit(solution)/shard_map/all_to_all | solution.py:456
  175.2 4.0 %all-to-all-start.6 = ((bf16[8,6,3200]{2,1,0:T(8,128)(2,1)}), bf16[8,6,3200]{2,1,0:T(8,128)(2,1)S(1)}, u32[]{:S(2)}, u32[]{:S(2)}) async-start(bf16[8,6,3200]{2,1,0:T(8,128)(2,1)} %reshape.77), calls=%async_computation.6 | async-start | bytes 819200 | tf_op jit(solution)/shard_map/all_to_all | solution.py:456
  179.2 4.3 %shard_map.145 = bf16[256,768]{1,0:T(8,128)(2,1)} custom-call(bf16[256,768]{1,0:T(8,128)(2,1)} %get-tuple-element.90.dq_ref, bf16[256,1536]{1,0:T(8,128)(2,1)} %get-tuple-element.83.dkv_ref, bf16[768,2304]{1,0:T(8,128)(2,1)} %w_ref.9, bf16[16,16,768]{2,1,0:T(8,128)(2,1)} %copy-done.5), custom_call_target="tpu_custom_call" | custom-call | flops 4400000000 | bytes 14400000 | tf_op jit(solution)/shard_map/pallas_call | solution.py:36
  183.5 3.8 %all-to-all-done.6 = bf16[8,6,3200]{2,1,0:T(8,128)(2,1)S(1)} async-done(((bf16[8,6,3200]{2,1,0:T(8,128)(2,1)}), bf16[8,6,3200]{2,1,0:T(8,128)(2,1)S(1)}, u32[]{:S(2)}, u32[]{:S(2)}) %all-to-all-start.6) | async-done | bytes 307232 | tf_op jit(solution)/shard_map/all_to_all | solution.py:456
  (76 shorter events, 12.5 us)
Async XLA Ops:
  2.7 9.2 %copy-start.10 = (s32[1024]{0:T(1024)S(1)}, s32[1024]{0:T(1024)}, u32[]{:S(2)}) copy-start(s32[1024]{0:T(1024)} %param.16) | copy-start | bytes 12292
  2.7 9.2 %copy-start.9 = (bf16[2,12,2,128]{3,2,1,0:T(2,128)(2,1)S(1)}, bf16[2,12,2,128]{3,2,1,0:T(2,128)(2,1)}, u32[]{:S(2)}) copy-start(bf16[2,12,2,128]{3,2,1,0:T(2,128)(2,1)} %param.14) | copy-start | bytes 36868
  2.7 9.8 %copy-start.6 = (bf16[2,12,8,32]{3,2,1,0:T(8,128)(2,1)S(1)}, bf16[2,12,8,32]{3,2,1,0:T(8,128)(2,1)}, u32[]{:S(2)}) copy-start(bf16[2,12,8,32]{3,2,1,0:T(8,128)(2,1)} %param.15) | copy-start | bytes 36868
  2.7 10.8 %copy-start.12 = (s32[32]{0:T(128)S(1)}, s32[32]{0:T(128)}, u32[]{:S(2)}) copy-start(s32[32]{0:T(128)} %param.17) | copy-start | bytes 388
  3.7 23.3 %all-to-all-start = ((bf16[16,32,768]{2,1,0:T(8,128)(2,1)}), bf16[16,32,768]{2,1,0:T(8,128)(2,1)S(1)}, u32[]{:S(2)}, u32[]{:S(2)}) async-start(bf16[16,32,768]{2,1,0:T(8,128)(2,1)} %pad_maximum_fusion), calls=%async_computation | async-start | bytes 1572864 | tf_op jit(solution)/shard_map/all_to_all | solution.py:456
  27.9 25.9 %all-to-all-start.1 = ((bf16[8,784,128]{2,1,0:T(8,128)(2,1)}), bf16[8,784,128]{2,1,0:T(8,128)(2,1)S(1)}, u32[]{:S(2)}, u32[]{:S(2)}) async-start(bf16[8,784,128]{2,1,0:T(8,128)(2,1)} %get-tuple-element.57), calls=%async_computation.1 | async-start | bytes 3211264 | tf_op jit(solution)/shard_map/all_to_all | solution.py:456
  53.8 1.2 copy-start
  59.7 5.5 %copy-start.4 = (bf16[2,128,768]{2,1,0:T(8,128)(2,1)S(1)}, bf16[2,128,768]{2,1,0:T(8,128)(2,1)}, u32[]{:S(2)}) copy-start(bf16[2,128,768]{2,1,0:T(8,128)(2,1)} %param.10) | copy-start | bytes 1179652
  59.7 6.0 %copy-start.19 = (bf16[384,256]{1,0:T(8,128)(2,1)S(1)}, bf16[384,256]{1,0:T(8,128)(2,1)}, u32[]{:S(2)}) copy-start(bf16[384,256]{1,0:T(8,128)(2,1)} %get-tuple-element.64) | copy-start | bytes 589828
  59.7 6.1 %copy-start.20 = (bf16[384,256]{1,0:T(8,128)(2,1)S(1)}, bf16[384,256]{1,0:T(8,128)(2,1)}, u32[]{:S(2)}) copy-start(bf16[384,256]{1,0:T(8,128)(2,1)} %get-tuple-element.65) | copy-start | bytes 589828
  59.7 6.5 %copy-start.11 = (f32[768]{0:T(1024)S(1)}, f32[768]{0:T(1024)}, u32[]{:S(2)}) copy-start(f32[768]{0:T(1024)} %param.13) | copy-start | bytes 9220
  59.7 20.6 %all-to-all-start.2 = ((bf16[16,32,768]{2,1,0:T(8,128)(2,1)}), bf16[16,32,768]{2,1,0:T(8,128)(2,1)S(1)}, u32[]{:S(2)}, u32[]{:S(2)}) async-start(bf16[16,32,768]{2,1,0:T(8,128)(2,1)} %get-tuple-element.63), calls=%async_computation.2 | async-start | bytes 1572864 | tf_op jit(solution)/shard_map/all_to_all | solution.py:456
  65.2 2.1 %collective-permute-start.1 = (bf16[256,768]{1,0:T(8,128)(2,1)S(1)}, bf16[256,768]{1,0:T(8,128)(2,1)S(1)}, u32[]{:S(2)}, u32[]{:S(2)}) collective-permute-start(bf16[256,768]{1,0:T(8,128)(2,1)S(1)} %bitcast.39), channel_id=1, source_target_pairs={{0,8},{8,0},{16,24},{24,16},{32,40},{40,32},{48,56},{56,48},{64,72... | collective-permute-start | bytes 1179656 | tf_op jit(solution)/shard_map/ppermute | solution.py:460
  65.7 1.6 collective-permute-start
  65.8 1.8 collective-permute-start.2
  67.3 18.5 %copy-start.17 = (bf16[384,256]{1,0:T(8,128)(2,1)}, bf16[384,256]{1,0:T(8,128)(2,1)S(1)}, u32[]{:S(2)}) copy-start(bf16[384,256]{1,0:T(8,128)(2,1)S(1)} %collective-permute-done.xr_ref) | copy-start | bytes 589828
  67.3 18.5 %copy-start.14 = (bf16[256,768]{1,0:T(8,128)(2,1)}, bf16[256,768]{1,0:T(8,128)(2,1)S(1)}, u32[]{:S(2)}) copy-start(bf16[256,768]{1,0:T(8,128)(2,1)S(1)} %collective-permute-done.1.gr_ref) | copy-start | bytes 1179652
  67.6 18.2 %copy-start.18 = (bf16[384,256]{1,0:T(8,128)(2,1)}, bf16[384,256]{1,0:T(8,128)(2,1)S(1)}, u32[]{:S(2)}) copy-start(bf16[384,256]{1,0:T(8,128)(2,1)S(1)} %collective-permute-done.2.xcr_ref) | copy-start | bytes 589828
  85.8 25.3 %all-to-all-start.3 = ((bf16[8,784,128]{2,1,0:T(8,128)(2,1)}), bf16[8,784,128]{2,1,0:T(8,128)(2,1)S(1)}, u32[]{:S(2)}, u32[]{:S(2)}) async-start(bf16[8,784,128]{2,1,0:T(8,128)(2,1)} %get-tuple-element.73), calls=%async_computation.3 | async-start | bytes 3211264 | tf_op jit(solution)/shard_map/all_to_all | solution.py:456
  98.3 10.1 %collective-permute-start.3 = (bf16[768,256]{1,0:T(8,128)(2,1)}, bf16[768,256]{1,0:T(8,128)(2,1)S(1)}, u32[]{:S(2)}, u32[]{:S(2)}) collective-permute-start(bf16[768,256]{1,0:T(8,128)(2,1)} %get-tuple-element.74), channel_id=1, source_target_pairs={{0,8},{8,0},{16,24},{24,16},{32,40},{40,32},{48,56},{56,48},{64,72... | collective-permute-start | bytes 1179656 | tf_op jit(solution)/shard_map/ppermute | solution.py:460
  98.3 10.1 %collective-permute-start.4 = (bf16[256,768]{1,0:T(8,128)(2,1)}, bf16[256,768]{1,0:T(8,128)(2,1)S(1)}, u32[]{:S(2)}, u32[]{:S(2)}) collective-permute-start(bf16[256,768]{1,0:T(8,128)(2,1)} %get-tuple-element.90.dq_ref), channel_id=1, source_target_pairs={{0,8},{8,0},{16,24},{24,16},{32,40},{40,32},{48,56},{56,48},{64,72... | collective-permute-start | bytes 1179656 | tf_op jit(solution)/shard_map/ppermute | solution.py:460
  108.3 13.0 %collective-permute-start.6 = (bf16[256,2304]{1,0:T(8,128)(2,1)}, bf16[256,2304]{1,0:T(8,128)(2,1)}, u32[]{:S(2)}, u32[]{:S(2)}) collective-permute-start(bf16[256,2304]{1,0:T(8,128)(2,1)} %get-tuple-element.89.dc_ref), channel_id=1, source_target_pairs={{0,8},{8,0},{16,24},{24,16},{32,40},{40,32},{48,56},{56,48},{64,72... | collective-permute-start | bytes 3538952 | tf_op jit(solution)/shard_map/ppermute | solution.py:460
  108.4 9.3 %copy-start.15 = (bf16[768,256]{1,0:T(8,128)(2,1)}, bf16[768,256]{1,0:T(8,128)(2,1)S(1)}, u32[]{:S(2)}) copy-start(bf16[768,256]{1,0:T(8,128)(2,1)S(1)} %collective-permute-done.3.nr_ref) | copy-start | bytes 1179652
  108.4 9.3 %copy-start.16 = (bf16[256,768]{1,0:T(8,128)(2,1)}, bf16[256,768]{1,0:T(8,128)(2,1)S(1)}, u32[]{:S(2)}) copy-start(bf16[256,768]{1,0:T(8,128)(2,1)S(1)} %collective-permute-done.4.dqr_ref) | copy-start | bytes 1179652
  111.1 1.2 copy-start.1
  117.6 8.9 %collective-permute-start.5 = (bf16[256,1536]{1,0:T(8,128)(2,1)}, bf16[256,1536]{1,0:T(8,128)(2,1)S(1)}, u32[]{:S(2)}, u32[]{:S(2)}) collective-permute-start(bf16[256,1536]{1,0:T(8,128)(2,1)} %get-tuple-element.83.dkv_ref), channel_id=1, source_target_pairs={{0,8},{8,0},{16,24},{24,16},{32,40},{40,32},{48,56},{56,48},{64,72... | collective-permute-start | bytes 2359304 | tf_op jit(solution)/shard_map/ppermute | solution.py:460
  117.7 15.8 %all-to-all-start.4 = ((bf16[16,16,768]{2,1,0:T(8,128)(2,1)}), bf16[16,16,768]{2,1,0:T(8,128)(2,1)S(1)}, u32[]{:S(2)}, u32[]{:S(2)}) async-start(bf16[16,16,768]{2,1,0:T(8,128)(2,1)} %bitcast.13), calls=%async_computation.4 | async-start | bytes 786432 | tf_op jit(solution)/shard_map/all_to_all | solution.py:456
  126.5 0.9 copy-start.13
  133.5 7.8 %copy-start.7 = (f32[2,12,256]{2,1,0:T(8,128)S(1)}, f32[2,12,256]{2,1,0:T(8,128)}, u32[]{:S(2)}) copy-start(f32[2,12,256]{2,1,0:T(8,128)} %get-tuple-element.97) | copy-start | bytes 73732
  133.5 8.9 %copy-start.8 = (f32[2,24,128]{2,1,0:T(8,128)S(1)}, f32[2,24,128]{2,1,0:T(8,128)}, u32[]{:S(2)}) copy-start(f32[2,24,128]{2,1,0:T(8,128)} %get-tuple-element.96) | copy-start | bytes 73732
  134.3 39.7 %all-to-all-start.5 = ((bf16[8,48,3200]{2,1,0:T(8,128)(2,1)}), bf16[8,48,3200]{2,1,0:T(8,128)(2,1)S(1)}, u32[]{:S(2)}, u32[]{:S(2)}) async-start(bf16[8,48,3200]{2,1,0:T(8,128)(2,1)} %shard_map.147), calls=%async_computation.5 | async-start | bytes 4915200 | tf_op jit(solution)/shard_map/all_to_all | solution.py:456
  175.2 12.1 %all-to-all-start.6 = ((bf16[8,6,3200]{2,1,0:T(8,128)(2,1)}), bf16[8,6,3200]{2,1,0:T(8,128)(2,1)S(1)}, u32[]{:S(2)}, u32[]{:S(2)}) async-start(bf16[8,6,3200]{2,1,0:T(8,128)(2,1)} %reshape.77), calls=%async_computation.6 | async-start | bytes 819200 | tf_op jit(solution)/shard_map/all_to_all | solution.py:456
  (3 other events, 2.5 us)

commit v3 on v2

--- a/solution.py
+++ b/solution.py
@@ -17,10 +17,12 @@
 GRID_H = 32
 CD = 8
 SCALE = HEAD_DIM ** (-0.5)
-WIDE = F + D + 128
+WIDE = F + 128
+SPLIT = 512
+VMEM_MIB = 20
 F32 = jnp.float32
 BF = jnp.bfloat16
-EVEN_ODD = [list(range(0, 16, 2)), list(range(1, 16, 2))]
+SAME_CORE = [[r * 8 + c for r in range(core, 16, 2) for c in range(8)] for core in range(2)]
 CORE_SWAP = [(i, i ^ 1) for i in range(16)]
 
 
@@ -29,20 +31,24 @@
 LOAD = STATE + 16
 
 
-def call(body, us, outs, *args, smem=(), scratch=()):
+def call(body, us, outs, *args, smem=(), near=(), keep=(), scratch=()):
     specs = [
         pl.BlockSpec(memory_space=pltpu.SMEM if n in smem else pltpu.VMEM) for n in range(len(args))
     ]
+    args = [
+        a if n in smem or n in near else pltpu.with_memory_space_constraint(a, pltpu.HBM)
+        for n, a in enumerate(args)
+    ]
     return pl.pallas_call(
         body,
-        out_shape=[jax.ShapeDtypeStruct(s, t) for s, t in outs],
+        out_shape=[(pltpu.VMEM if n in keep else pltpu.HBM)(s, t) for n, (s, t) in enumerate(outs)],
         in_specs=specs,
         out_specs=[pl.BlockSpec(memory_space=pltpu.VMEM)] * len(outs),
         scratch_shapes=list(scratch),
         cost_estimate=pl.CostEstimate(
             flops=int(us * 1.1e9), bytes_accessed=int(us * 3.6e6), transcendentals=0
         ),
-        compiler_params=pltpu.CompilerParams(vmem_limit_bytes=56 * 1024 * 1024),
+        compiler_params=pltpu.CompilerParams(vmem_limit_bytes=VMEM_MIB * 1024 * 1024),
     )(*args)
 
 
@@ -77,9 +83,10 @@
     return jnp.concatenate([x[:half], x[half:]], axis=1)
 
 
-def lanes_of(fac, p):
+def lanes_of(fac, kind, p):
     shape = (fac.shape[0], 128)
-    return jnp.where(left_half(shape), fac[:, 2 * p : 2 * p + 1], fac[:, 2 * p + 1 : 2 * p + 2])
+    n = kind * HEADS + 2 * p
+    return jnp.where(left_half(shape), fac[:, n : n + 1], fac[:, n + 1 : n + 2])
 
 
 def compact(m):
@@ -110,10 +117,25 @@
     lax.fori_loop(0, 7 - place, lambda n, c: (step(1 if from_left else 0, 7 - n), c)[1], 0)
 
 
+def first_feature(n, j, core):
+    return 48 * (2 * n + core) + 6 * j
+
+
 def pick_rows(core):
+    m, f = iota((SPLIT, D), 0), iota((SPLIT, D), 1)
+    t = m & 7
+    return ((f == first_feature(m >> 6, (m >> 3) & 7, core) + t) & (t < 6)).astype(BF)
+
+
+def pick_thirds(core):
     m, f = iota((D // 2, D), 0), iota((D // 2, D), 1)
-    n = (m * 683) >> 15
-    return (f == m + 48 * (n + core)).astype(BF)
+    b, d = m >> 7, (m >> 1) & 63
+    return (f == first_feature(d >> 3, d & 7, core) + 3 * (m & 1) + b).astype(BF)
+
+
+def place_thirds():
+    m, n = iota((SPLIT, 128), 0), iota((SPLIT, 128), 1)
+    return (((m >> 3) == (n >> 1)) & ((m & 7) == 6 + (n & 1))).astype(BF)
 
 
 def per_head(shape):
@@ -134,6 +156,12 @@
     return i0, i1, le, ge, seg_row, seg_col, b[1:2, 0:1]
 
 
+def layout_kernel(x_ref, g_ref, out_ref):
+    for n, ref in enumerate((x_ref, g_ref)):
+        wide = ref[...].astype(F32).reshape(2, 16, 8, D).swapaxes(0, 1).reshape(16, 16, D)
+        out_ref[:, n * 16 : (n + 1) * 16, :] = wide.astype(BF)
+
+
 def summary_kernel(place_ref, ldr_ref, bc_ref, x_ref, w_ref, fac_ref, th_ref, kv_ref, u_ref, both_ref):
     i0, i1, le, ge, seg_row, seg_col, following = row_masks(bc_ref)
     first, last = seg_row[:, 0:1], seg_row[:, COLS - 1 : COLS]
@@ -143,10 +171,15 @@
         lr, ll = ldr_ref[r, 0], ldr_ref[r, 1]
         row_r, row_l = nn(lr, le), nn(ll, ge)
         col_r, col_l = nt(ge, lr), nt(le, ll)
-        fac_ref[0, r] = jnp.where(seg_col == 0.0, jnp.exp(col_r), 0.0) * SCALE
-        fac_ref[1, r] = jnp.where(seg_col == after, jnp.exp(col_l), 0.0) * SCALE
-        fac_ref[2, r] = jnp.where(seg_col == last, jnp.exp(col_r[COLS - 1 : COLS] - col_r), 0.0)
-        fac_ref[3, r] = jnp.where(seg_col == first, jnp.exp(col_l[0:1] - col_l), 0.0)
+        fac_ref[r] = jnp.concatenate(
+            [
+                jnp.where(seg_col == 0.0, jnp.exp(col_r), 0.0) * SCALE,
+                jnp.where(seg_col == after, jnp.exp(col_l), 0.0) * SCALE,
+                jnp.where(seg_col == last, jnp.exp(col_r[COLS - 1 : COLS] - col_r), 0.0),
+                jnp.where(seg_col == first, jnp.exp(col_l[0:1] - col_l), 0.0),
+            ],
+            axis=1,
+        )
         th_r = jnp.where(last == 0.0, jnp.exp(row_r[:, COLS - 1 : COLS]), 0.0)
         th_l = jnp.where(after == first, jnp.exp(row_l[:, 0:1]), 0.0)
         for direction, th in enumerate((th_r, th_l)):
@@ -161,7 +194,7 @@
             k = kv_ref[rows, p * 128 : (p + 1) * 128]
             v = kv_ref[rows, D + p * 128 : D + (p + 1) * 128].astype(F32)
             for direction in range(2):
-                tv = (lanes_of(fac_ref[2 + direction, r], p) * v).astype(BF)
+                tv = (lanes_of(fac_ref[r], 2 + direction, p) * v).astype(BF)
                 both_ref[direction, unit_rows(r, p), :] = compact(tn(k, tv)).astype(BF)
     both_ref[:, STATE:LOAD, :] = th_ref[...].astype(BF)
     spread(both_ref, place_ref[0], True, u_ref)
@@ -252,8 +285,8 @@
             lanes = slice(p * 128, (p + 1) * 128)
             carried = nn(q_ref[rows, lanes], both_states(s_ref, r, p))
             out = inside_ref[rows, lanes]
-            out = out + lanes_of(fac_ref[0, r], p) * carried[:, :128]
-            out = out + lanes_of(fac_ref[1, r], p) * carried[:, 128:]
+            out = out + lanes_of(fac_ref[r], 0, p) * carried[:, :128]
+            out = out + lanes_of(fac_ref[r], 1, p) * carried[:, 128:]
             out_ref[rows, lanes] = out
     slab = out_ref[...].reshape(2, 16, 8, D).swapaxes(0, 1).reshape(16, 16, D)
     xch_ref[:, 16:32, :] = slab.astype(BF)
@@ -283,7 +316,7 @@
             q = q_ref[rows, p * 128 : (p + 1) * 128]
             do = d_mixed[rows, p * 128 : (p + 1) * 128]
             for direction in range(2):
-                eo = (lanes_of(fac_ref[direction, r], p) * do).astype(BF)
+                eo = (lanes_of(fac_ref[r], direction, p) * do).astype(BF)
                 both_ref[direction, unit_rows(r, p), :] = compact(tn(q, eo)).astype(BF)
     both_ref[:, STATE:LOAD, :] = th_ref[...].astype(BF)
     spread(both_ref, place_ref[0], False, g_ref)
@@ -339,9 +372,8 @@
     gain_terms = (dn_ref[...].astype(F32) * unit).astype(BF)
     core = core_ref[0]
     for ref, c in ((keep_ref, core), (send_ref, 1 - core)):
-        pick = pick_rows(c)
-        ref[0 : D // 2, :] = nt(pick, normed).astype(BF)
-        ref[D // 2 : D, :] = nt(pick, gain_terms).astype(BF)
+        ref[0:SPLIT, :] = nt(pick_rows(c), gain_terms).astype(BF)
+        ref[SPLIT : SPLIT + D // 2, :] = nt(pick_thirds(c), normed).astype(BF)
     i0, i1 = iota((COLS, COLS), 0), iota((COLS, COLS), 1)
     table = jnp.concatenate([(i0 < i1).astype(BF), (i0 > i1).astype(BF)], axis=1)
     entries = [[], []]
@@ -357,12 +389,12 @@
             dq, dk, dv, both = local_backward(q, k, v, do, wr_ref[n], probs_ref[n])
             states = both_states(s_ref, r, p)
             wide_do = do.astype(F32)
-            eo = [lanes_of(fac_ref[d, r], p) * wide_do for d in range(2)]
+            eo = [lanes_of(fac_ref[r], d, p) * wide_do for d in range(2)]
             dq = dq + nt(jnp.concatenate(eo, axis=1).astype(BF), states)
             carried = nn(q, states)
             dq_ref[rows, lanes] = dq.astype(BF)
-            part_ref[rows, lanes] = dk
-            part_ref[rows, D + p * 128 : D + (p + 1) * 128] = dv
+            part_ref[rows, lanes] = dk.astype(BF)
+            part_ref[rows, D + p * 128 : D + (p + 1) * 128] = dv.astype(BF)
             sums = nn(both, table)
             for direction in range(2):
                 entries[direction].append(
@@ -395,11 +427,11 @@
             k = kv_ref[rows, lanes]
             v = kv_ref[rows, far].astype(F32)
             adjoints = both_states(a_ref, r, p)
-            tail = [lanes_of(fac_ref[2 + d, r], p) for d in range(2)]
+            tail = [lanes_of(fac_ref[r], 2 + d, p) for d in range(2)]
             tv = [t * v for t in tail]
-            dk = part_ref[rows, lanes] + nt(jnp.concatenate(tv, axis=1).astype(BF), adjoints)
+            dk = part_ref[rows, lanes].astype(F32) + nt(jnp.concatenate(tv, axis=1).astype(BF), adjoints)
             leaving = nn(k, adjoints)
-            dv = part_ref[rows, far] + tail[0] * leaving[:, :128] + tail[1] * leaving[:, 128:]
+            dv = part_ref[rows, far].astype(F32) + tail[0] * leaving[:, :128] + tail[1] * leaving[:, 128:]
             dkv_ref[rows, lanes] = dk.astype(BF)
             dkv_ref[rows, far] = dv.astype(BF)
             for d in range(2):
@@ -419,32 +451,43 @@
 def weight_early_kernel(
     xk_ref, xr_ref, xck_ref, xcr_ref, dq_ref, dqr_ref, dc_ref, dcr_ref, nk_ref, nr_ref, g_ref, gr_ref, out_ref
 ):
-    x = jnp.concatenate([xk_ref[...], xr_ref[...], xck_ref[...], xcr_ref[...]], axis=1)
-
-    def put(value, start):
-        out_ref[:, :, start : start + value.shape[1]] = value.astype(BF).reshape(8, 48, -1)
-
-    for start in range(0, D, 384):
-        cols = slice(start, start + 384)
-        d = [dq_ref[:, cols], dqr_ref[:, cols], dc_ref[:, cols], dcr_ref[:, cols]]
-        put(nn(x, jnp.concatenate(d, axis=0)), start)
-    normed = jnp.concatenate([nk_ref[0 : D // 2, :], nr_ref[0 : D // 2, :]], axis=1)
-    gain_terms = jnp.concatenate([nk_ref[D // 2 : D, :], nr_ref[D // 2 : D, :]], axis=1)
-    for start in range(0, D, 384):
-        d = jnp.concatenate([g_ref[:, start : start + 384], gr_ref[:, start : start + 384]], axis=0)
-        put(nn(normed, d), D + start)
-    put(nn(gain_terms, jnp.ones((2 * TOK, 128), BF)), 2 * D)
-
-
-def weight_late_kernel(
-    xk_ref, xr_ref, xck_ref, xcr_ref, dkv_ref, dkvr_ref, dc_ref, dcr_ref, early_ref, out_ref
-):
-    x = jnp.concatenate([xk_ref[...], xr_ref[...], xck_ref[...], xcr_ref[...]], axis=1)
-    out_ref[:, :, 2 * D :] = early_ref[...]
-    for start in range(0, 2 * D, 384):
-        cols, far = slice(start, start + 384), slice(D + start, D + start + 384)
-        d = [dkv_ref[:, cols], dkvr_ref[:, cols], dc_ref[:, far], dcr_ref[:, far]]
-        out_ref[:, :, cols] = nn(x, jnp.concatenate(d, axis=0)).astype(BF).reshape(8, 48, 384)
+    x = jnp.concatenate([xk_ref[...], xr_ref[...]], axis=1)
+    xc = jnp.concatenate([xck_ref[...], xcr_ref[...]], axis=1)
+    normed = jnp.concatenate([nk_ref[SPLIT:, :], nr_ref[SPLIT:, :]], axis=1)
+    gain_terms = jnp.concatenate([nk_ref[0:SPLIT, :], nr_ref[0:SPLIT, :]], axis=1)
+    expand = place_thirds()
+    for start in range(0, D, 256):
+        part = slice(start, start + 256)
+        out_weight = nn(normed, jnp.concatenate([g_ref[:, part], gr_ref[:, part]], axis=0)).astype(BF)
+        for b in range(3):
+            cols = slice(b * D + start, b * D + start + 256)
+            total = nn(expand, out_weight[b * 128 : (b + 1) * 128])
+            total = total + nn(xc, jnp.concatenate([dc_ref[:, cols], dcr_ref[:, cols]], axis=0))
+            if b == 0:
+                total = total + nn(x, jnp.concatenate([dq_ref[:, cols], dqr_ref[:, cols]], axis=0))
+            out_ref[:, cols] = total.astype(BF)
+    out_ref[:, F:] = nn(gain_terms, jnp.ones((2 * TOK, 128), BF)).astype(BF)
+
+
+def weight_late_kernel(xk_ref, xr_ref, dkv_ref, dkvr_ref, early_ref, out_ref):
+    x = jnp.concatenate([xk_ref[...], xr_ref[...]], axis=1)
+    out_ref[:, :, 0:D] = early_ref[:, 0:D].reshape(64, 8, D)
+    out_ref[:, :, F:] = early_ref[:, F:].reshape(64, 8, 128)
+    for start in range(0, 2 * D, 256):
+        cols = slice(start, start + 256)
+        far = slice(D + start, D + start + 256)
+        total = nn(x, jnp.concatenate([dkv_ref[:, cols], dkvr_ref[:, cols]], axis=0))
+        total = total + early_ref[:, far].astype(F32)
+        out_ref[:, :, far] = total.reshape(64, 8, 256).astype(BF)
+
+
+def weight_sum_kernel(rx_ref, qkv_ref, out_ref, gain_ref):
+    total = jnp.sum(rx_ref[...].astype(F32), axis=0) * (32768.0 ** (-0.5))
+    qkv_ref[...] = total[0:6, 0:F]
+    for t in range(6):
+        out_ref[t : t + 1, :] = total[6 + t // 3 : 7 + t // 3, (t % 3) * D : (t % 3 + 1) * D]
+    same = iota((8, 128), 0) == iota((8, 128), 1)
+    gain_ref[...] = jnp.sum(jnp.where(same, total[:, F:], 0.0), axis=0, keepdims=True)[:, 0:6]
 
 
 def token_kernel(dq_ref, dkv_ref, w_ref, rx_ref, out_ref):
@@ -470,18 +513,16 @@
     place = lax.axis_index("col")
     at = place.astype(jnp.int32).reshape(1)
     core = (lax.axis_index("row") % 2).astype(jnp.int32).reshape(1)
-    x = tokens.reshape(TOK, D)
-    g = grad_out.reshape(TOK, D)
     gain = gain.reshape(1, D)
-    half = (D // 2, TOK)
+    half = (SPLIT, TOK)
     load = ((8, LOAD, 128), BF)
     wide = pltpu.VMEM((2, STATE, 128), F32)
     narrow = pltpu.VMEM((2, LOAD, 128), BF)
 
-    def slab(a):
-        return a.reshape(ROWS, 16, CD, D).swapaxes(0, 1).reshape(16, ROWS * CD, D)
-
-    rx = exchange(jnp.concatenate([slab(tokens), slab(grad_out)], axis=1), "row")
+    x = tokens.reshape(TOK, D)
+    g = grad_out.reshape(TOK, D)
+    (first,) = call(layout_kernel, 2.0, [((16, 32, D), BF)], tokens, grad_out, keep=(0,))
+    rx = exchange(first, "row")
 
     ldr = log_decay_rows.transpose(2, 0, 1, 3)
     ldc = log_decay_cols.swapaxes(2, 3).reshape(2, HEADS, TOK)
@@ -490,13 +531,13 @@
     br = jnp.broadcast_to(border_rows[:, None], (GRID_H, CD)).reshape(1, TOK)
     fac, th, kv, update = call(
         summary_kernel, 4.6,
-        [((4, ROWS, COLS, HEADS), F32), ((2, 16, 128), F32), ((TOK, 2 * D), BF), load],
-        at, ldr, bc, x, w_qkv, smem=(0,), scratch=[narrow],
+        [((ROWS, COLS, 4 * HEADS), F32), ((2, 16, 128), F32), ((TOK, 2 * D), BF), load],
+        at, ldr, bc, x, w_qkv, smem=(0,), near=(1, 2), keep=(3,), scratch=[narrow],
     )
     wr, wc = call(
         mask_kernel, 4.3,
         [((UNITS, 2 * COLS, COLS), BF), ((PAIRS, 2 * TOK, TOK), BF)],
-        ldr, ldc, bc, br, th,
+        ldr, ldc, bc, br, th, near=(0, 1, 2, 3),
     )
     states = exchange(after(update, rx, wr), "col")
     q, dn, x_keep, x_send, inside, probs = call(
@@ -508,13 +549,13 @@
     qkv_c, dn_c, col_out, probs_c, xc_keep, xc_send = call(
         col_forward_kernel, 6.8,
         [((TOK, F), BF), ((TOK, D), BF), ((TOK, D), BF), ((PAIRS, 2 * TOK, TOK), BF), (half, BF), (half, BF)],
-        core, rx, w_qkv, w_out, wc, smem=(0,),
+        core, rx, w_qkv, w_out, wc, smem=(0,), near=(1,),
     )
     states = after(states, col_out, q)
     row_out, out_swap, entering = call(
         row_join_kernel, 5.0,
         [((TOK, D), F32), ((16, 32, D), BF), ((2, STATE, 128), BF)],
-        at, q, states, fac, inside, col_out, smem=(0,), scratch=[wide],
+        at, q, states, fac, inside, col_out, smem=(0,), near=(2,), keep=(1,), scratch=[wide],
     )
     xc_far = swap(xc_send)
     rx2 = exchange(out_swap, "row")
@@ -522,19 +563,19 @@
     dm, adj = call(
         row_middle_kernel, 4.5,
         [((TOK, D), BF), load],
-        at, rx2, row_out, dn, gain, q, fac, th, smem=(0,), scratch=[narrow],
+        at, rx2, row_out, dn, gain, q, fac, th, smem=(0,), near=(1, 4), keep=(1,), scratch=[narrow],
     )
     adj = exchange(adj, "col")
     dq, part, gd_part, n_keep, n_send = call(
         row_local_kernel, 8.9,
-        [((TOK, D), BF), ((TOK, 2 * D), F32), ((2, 2 * HEADS, COLS), F32), ((D, TOK), BF), ((D, TOK), BF)],
-        core, rx2, row_out, dn, gain, q, kv, dm, entering, wr, probs, fac, smem=(0,),
+        [((TOK, D), BF), ((TOK, 2 * D), BF), ((2, 2 * HEADS, COLS), F32), ((SPLIT + D // 2, TOK), BF), ((SPLIT + D // 2, TOK), BF)],
+        core, rx2, row_out, dn, gain, q, kv, dm, entering, wr, probs, fac, smem=(0,), near=(1, 4),
     )
     n_far, dq_far = swap(n_send), swap(dq)
     dqkv_c, gdc, tok_c = call(
         col_backward_kernel, 9.7,
         [((TOK, F), BF), ((2, HEADS, TOK), F32), ((TOK, D), BF)],
-        after(rx2, dm), col_out, dn_c, gain, qkv_c, wc, probs_c, w_qkv,
+        after(rx2, dm), col_out, dn_c, gain, qkv_c, wc, probs_c, w_qkv, near=(0, 3),
     )
     dqkv_c_far = swap(dqkv_c)
     adj, n_far, dq_far, tok_c = lax.optimization_barrier((adj, n_far, dq_far, tok_c))
@@ -543,30 +584,31 @@
         row_finish_kernel, 5.5,
         [((TOK, 2 * D), BF), ((2, 2 * HEADS, COLS), F32)],
         at, kv, entering, adj, fac, th, part, gd_part,
-        smem=(0,), scratch=[wide, pltpu.VMEM((2, STATE, 128), BF)],
+        smem=(0,), near=(3,), scratch=[wide, pltpu.VMEM((2, STATE, 128), BF)],
     )
     dkv_far = swap(dkv)
     (early,) = call(
         weight_early_kernel, 5.0,
-        [((8, 48, 2 * D + 128), BF)],
+        [((SPLIT, WIDE), BF)],
         x_keep, x_far, xc_keep, xc_far, after(dq, dkv), dq_far, dqkv_c, dqkv_c_far, n_keep, n_far, g, g_far,
+        keep=(0,),
     )
     (wg,) = call(
-        weight_late_kernel, 6.0,
-        [((8, 48, WIDE), BF)],
-        x_keep, x_far, xc_keep, xc_far, dkv, dkv_far, dqkv_c, dqkv_c_far, early,
-    )
-    wg = exchange(after(wg, rx3), "row", EVEN_ODD)
-    wg = jnp.sum(wg.astype(F32), axis=0).astype(BF).reshape(8, 6, WIDE)
-    wg = exchange(wg, "col")
-    wg = jnp.sum(wg.astype(F32), axis=0) * (32768.0 ** (-0.5))
-    (grad_tokens,) = call(token_kernel, 4.0, [((TOK, D), BF)], dq, dkv, w_qkv, rx3)
+        weight_late_kernel, 4.0,
+        [((64, 8, WIDE), BF)],
+        x_keep, x_far, dkv, dkv_far, early, near=(3, 4), keep=(0,),
+    )
+    wg = exchange(after(wg, rx3), ("row", "col"), SAME_CORE)
+    grad_qkv, grad_out_weight, grad_gain = call(
+        weight_sum_kernel, 2.0, [((6, F), F32), ((6, D), F32), ((1, 6), F32)], wg, near=(0,)
+    )
+    (grad_tokens,) = call(token_kernel, 4.0, [((TOK, D), BF)], dq, dkv, w_qkv, rx3, near=(3,))
     gdr = gdr.reshape(2, ROWS, HEADS, COLS).swapaxes(1, 2)
     return (
         grad_tokens.reshape(ROWS, COLS, D),
-        jnp.concatenate([wg[:, 2 * D : 3 * D], wg[:, : 2 * D]], axis=1),
-        wg[:, F : F + D],
-        wg[:, F + D],
+        grad_qkv,
+        grad_out_weight,
+        grad_gain.reshape(6),
         gdr.astype(BF),
         gdc.astype(BF).reshape(2, HEADS, GRID_H, CD).swapaxes(2, 3),
     )

time: 190 us -> 170 us (0.89)
  local copies, waits for them, and re-layouts: 15.1 us -> 3.7 us
  starting transfers between devices: 37.9 us -> 34.6 us
  waiting for transfers between devices: 63.1 us -> 60.6 us
  other arithmetic: 2.1 us -> 0.01 us
    unnamed x45 -> x31, local copies, waits for them, and re-layouts: 7.82 us -> 2.85 us
    all_to_all x7 -> x6, starting transfers between devices: 36.3 us -> 33 us  [exchange(): return lax.all_to_all(x, axis, 0, 0, tiled=True, axis_index_groups=groups)]
    all_to_all x7 -> x6, waiting for transfers between devices: 62.3 us -> 59 us  [exchange(): return lax.all_to_all(x, axis, 0, 0, tiled=True, axis_index_groups=groups)]
    reshape x3 -> x0, local copies, waits for them, and re-layouts: 2.9 us -> none  [the longest x2 2.05 us: slab(): return a.reshape(ROWS, 16, CD, D).swapaxes(0, 1).reshape(16, ROWS * CD, D)]
    pallas_call x12 -> x14, Pallas kernels: 70.2 us -> 68.9 us  [call(): pl.pallas_call(body, out_shape=[(pltpu.VMEM if n in keep else pltpu.HBM)(...]
  transfers between devices with their start and end apart: 14 -> 13, of which waited for: 8 -> 7; matrix products, arithmetic and copies ran while one was open for 3% -> 1% of each run, Pallas kernels for 32% -> 34%
where the time goes in v3:
time: 170 us; the launch traced here: 169 us
  Pallas kernels  68.9 us (41%)
  waiting for transfers between devices  60.6 us (36%)
  starting transfers between devices  34.6 us (20%)
  local copies, waits for them, and re-layouts  3.7 us (2%)
    pallas_call x14, Pallas kernels, call(): pl.pallas_call(body, out_shape=[(pltpu.VMEM if n in keep else pltpu.HBM)(...  68.9 us
    all_to_all x6, waiting for transfers between devices, exchange(): return lax.all_to_all(x, axis, 0, 0, tiled=True, axis_index_groups=groups)  59 us
    all_to_all x6, starting transfers between devices, exchange(): return lax.all_to_all(x, axis, 0, 0, tiled=True, axis_index_groups=groups)  33 us
  transfers between devices with their start and end apart: 13, of which 7 were waited for; matrix products, arithmetic and copies ran while one was open for 1% of the time, Pallas kernels for 34%

profile of v3, /device:TPU:0, one launch (start us, length us, event | category | flops | bytes accessed | tf_op | source)
XLA Modules:
  0.0 168.8 jit_solution(11984690314147931108)
XLA Ops:
  0.7 2.0 %shard_map.139 = bf16[16,32,768]{2,1,0:T(8,128)(2,1)} custom-call(bf16[2,128,768]{2,1,0:T(8,128)(2,1)} %x_ref.1, bf16[2,128,768]{2,1,0:T(8,128)(2,1)} %g_ref.1), custom_call_target="tpu_custom_call" | custom-call | flops 2200000000 | bytes 7200000 | tf_op jit(solution)/shard_map/pallas_call | solution.py:42
  2.7 8.3 %all-to-all-start = ((bf16[16,32,768]{2,1,0:T(8,128)(2,1)}), bf16[16,32,768]{2,1,0:T(8,128)(2,1)S(1)}, u32[]{:S(2)}, u32[]{:S(2)}) async-start(bf16[16,32,768]{2,1,0:T(8,128)(2,1)} %shard_map.139), calls=%async_computation | async-start | bytes 1572864 | tf_op jit(solution)/shard_map/all_to_all | solution.py:499
  11.6 5.2 %shard_map.136 = (f32[2,128,48]{2,1,0:T(8,128)}, f32[2,16,128]{2,1,0:T(8,128)}, bf16[256,1536]{1,0:T(8,128)(2,1)}, bf16[8,784,128]{2,1,0:T(8,128)(2,1)}) custom-call(s32[1]{0:T(128)} %bitcast.1.place_ref, bf16[2,2,12,128]{3,2,1,0:T(8,128)(2,1)S(1)} %bitcast.21, s32[2,128]{1,0:T(2,128)S(1)} %constant_dynamic-slice_fusion.bc_ref, bf16[256,768]{1,0:T(8,128)(2,1)} %bitcast.26, ...), custom_call_target="tpu_custom_call" | custom-call | flops 5059999744 | bytes 16559999 | tf_op jit(solution)/shard_map/pallas_call | solution.py:42
  16.8 4.1 %shard_map.137 = (bf16[12,256,128]{2,1,0:T(8,128)(2,1)}, bf16[6,512,256]{2,1,0:T(8,128)(2,1)}) custom-call(bf16[2,2,12,128]{3,2,1,0:T(8,128)(2,1)S(1)} %bitcast.22, bf16[2,12,256]{2,1,0:T(8,128)(2,1)S(1)} %reshape.63.ldc_ref, s32[2,128]{1,0:T(2,128)S(1)} %constant_dynamic-slice_fusion.bc_ref, s32[1,256]{1,0:T(1,128)S(1)} %reshape.57.br_ref, ...), custom_call_target="tpu_custom_call" | custom-call | flops 4729999872 | bytes 15480000 | tf_op jit(solution)/shard_map/pallas_call | solution.py:42
  20.8 5.3 %all-to-all-done.rx_ref = bf16[16,32,768]{2,1,0:T(8,128)(2,1)S(1)} async-done(((bf16[16,32,768]{2,1,0:T(8,128)(2,1)}), bf16[16,32,768]{2,1,0:T(8,128)(2,1)S(1)}, u32[]{:S(2)}, u32[]{:S(2)}) %all-to-all-start) | async-done | bytes 786464 | tf_op jit(solution)/shard_map/all_to_all | solution.py:499
  26.1 4.5 %all-to-all-start.1 = ((bf16[8,784,128]{2,1,0:T(8,128)(2,1)}), bf16[8,784,128]{2,1,0:T(8,128)(2,1)S(1)}, u32[]{:S(2)}, u32[]{:S(2)}) async-start(bf16[8,784,128]{2,1,0:T(8,128)(2,1)} %get-tuple-element.60), calls=%async_computation.1 | async-start | bytes 3211264 | tf_op jit(solution)/shard_map/all_to_all | solution.py:499
  30.6 5.9 %shard_map.138 = (bf16[256,768]{1,0:T(8,128)(2,1)}, bf16[256,768]{1,0:T(8,128)(2,1)}, bf16[512,256]{1,0:T(8,128)(2,1)}, bf16[512,256]{1,0:T(8,128)(2,1)}, f32[25...) custom-call(s32[1]{0:T(128)} %bitcast.core_ref, bf16[256,768]{1,0:T(8,128)(2,1)} %bitcast.27, bf16[256,768]{1,0:T(8,128)(2,1)} %bitcast.28, ...), custom_call_target="tpu_custom_call" | custom-call | flops 6270000128 | bytes 20520000 | tf_op jit(solution)/shard_map/pallas_call | solution.py:42
  36.5 6.5 %shard_map.140 = (bf16[256,2304]{1,0:T(8,128)(2,1)}, bf16[256,768]{1,0:T(8,128)(2,1)}, bf16[256,768]{1,0:T(8,128)(2,1)}, bf16[6,512,256]{2,1,0:T(8,128)(2,1)}, b...) custom-call(s32[1]{0:T(128)} %bitcast.core_ref, bf16[16,32,768]{2,1,0:T(8,128)(2,1)S(1)} %all-to-all-done.rx_ref, ...), custom_call_target="tpu_custom_call" | custom-call | flops 7480000000 | bytes 24480000 | tf_op jit(solution)/shard_map/pallas_call | solution.py:42
  43.0 9.0 %all-to-all-done.1.rs_ref = bf16[8,784,128]{2,1,0:T(8,128)(2,1)S(1)} async-done(((bf16[8,784,128]{2,1,0:T(8,128)(2,1)}), bf16[8,784,128]{2,1,0:T(8,128)(2,1)S(1)}, u32[]{:S(2)}, u32[]{:S(2)}) %all-to-all-start.1) | async-done | bytes 1605664 | tf_op jit(solution)/shard_map/all_to_all | solution.py:499
  52.0 4.3 %shard_map.141 = (f32[256,768]{1,0:T(8,128)}, bf16[16,32,768]{2,1,0:T(8,128)(2,1)}, bf16[2,768,128]{2,1,0:T(8,128)(2,1)}) custom-call(s32[1]{0:T(128)} %bitcast.1.place_ref, bf16[256,768]{1,0:T(8,128)(2,1)} %get-tuple-element.58.q_ref, bf16[8,784,128]{2,1,0:T(8,128)(2,1)S(1)} %all-to-all-done.1.rs_ref, f32[2,128,48]{2,1,0:T(8,128)} %get-tuple-element.64.fac_ref, ...), custom_call_target="tpu_custom_call" | custom-call | flops 5500000256 | bytes 18000000 | tf_op jit(solution)/shard_map/pallas_call | solution.py:42
  56.3 3.6 %all-to-all-start.2 = ((bf16[16,32,768]{2,1,0:T(8,128)(2,1)}), bf16[16,32,768]{2,1,0:T(8,128)(2,1)S(1)}, u32[]{:S(2)}, u32[]{:S(2)}) async-start(bf16[16,32,768]{2,1,0:T(8,128)(2,1)} %get-tuple-element.66), calls=%async_computation.2 | async-start | bytes 1572864 | tf_op jit(solution)/shard_map/all_to_all | solution.py:499
  61.0 1.6 collective-permute-done.xr_ref
  62.6 0.7 copy-done.11
  63.3 0.7 copy-done.9
  64.0 11.1 %all-to-all-done.2.rx_ref = bf16[16,32,768]{2,1,0:T(8,128)(2,1)S(1)} async-done(((bf16[16,32,768]{2,1,0:T(8,128)(2,1)}), bf16[16,32,768]{2,1,0:T(8,128)(2,1)S(1)}, u32[]{:S(2)}, u32[]{:S(2)}) %all-to-all-start.2) | async-done | bytes 786464 | tf_op jit(solution)/shard_map/all_to_all | solution.py:499
  75.1 4.2 %shard_map.142 = (bf16[256,768]{1,0:T(8,128)(2,1)}, bf16[8,784,128]{2,1,0:T(8,128)(2,1)}) custom-call(s32[1]{0:T(128)} %bitcast.1.place_ref, bf16[16,32,768]{2,1,0:T(8,128)(2,1)S(1)} %all-to-all-done.2.rx_ref, f32[256,768]{1,0:T(8,128)} %get-tuple-element.70.row_ref, bf16[256,768]{1,0:T(8,128)(2,1)} %get-tuple-element.71.dn_ref, ...), custom_call_target="tpu_custom_call" | custom-call | flops 4950000128 | bytes 16200000 | tf_op jit(solution)/shard_map/pallas_call | solution.py:42
  79.3 4.2 %all-to-all-start.3 = ((bf16[8,784,128]{2,1,0:T(8,128)(2,1)}), bf16[8,784,128]{2,1,0:T(8,128)(2,1)S(1)}, u32[]{:S(2)}, u32[]{:S(2)}) async-start(bf16[8,784,128]{2,1,0:T(8,128)(2,1)} %get-tuple-element.76), calls=%async_computation.3 | async-start | bytes 3211264 | tf_op jit(solution)/shard_map/all_to_all | solution.py:499
  83.5 8.5 %shard_map.143 = (bf16[256,768]{1,0:T(8,128)(2,1)}, bf16[256,1536]{1,0:T(8,128)(2,1)}, f32[2,24,128]{2,1,0:T(8,128)}, bf16[896,256]{1,0:T(8,128)(2,1)}, bf16[896,256]{1,0:T(8,128)(2,1)}) custom-call(s32[1]{0:T(128)} %bitcast.core_ref, bf16[16,32,768]{2,1,0:T(8,128)(2,1)S(1)} %all-to-all-done.2.rx_ref, f32[256,768]{1,0:T(8,128)} %get-tuple-element.70.row_ref, ...), custom_call_target="tpu_custom_call" | custom-call | flops 9790000128 | bytes 32040000 | tf_op jit(solution)/shard_map/pallas_call | solution.py:42
  92.0 0.5 collective-permute-start.4
  92.5 9.3 %shard_map.144 = (bf16[256,2304]{1,0:T(8,128)(2,1)}, f32[2,12,256]{2,1,0:T(8,128)}, bf16[256,768]{1,0:T(8,128)(2,1)}) custom-call(bf16[16,32,768]{2,1,0:T(8,128)(2,1)S(1)} %all-to-all-done.2.rx_ref, bf16[256,768]{1,0:T(8,128)(2,1)} %get-tuple-element.62.col_ref, bf16[256,768]{1,0:T(8,128)(2,1)} %get-tuple-element.79.dn_ref, f32[1,768]{1,0:T(1,128)S(1)} %reshape.58.gain_ref, ...), custom_call_target="tpu_custom_call" | custom-call | flops 10670000128 | bytes 34920000 | tf_op jit(solution)/shard_map/pallas_call | solution.py:42
  101.9 3.0 %all-to-all-done.3.ra_ref = bf16[8,784,128]{2,1,0:T(8,128)(2,1)S(1)} async-done(((bf16[8,784,128]{2,1,0:T(8,128)(2,1)}), bf16[8,784,128]{2,1,0:T(8,128)(2,1)S(1)}, u32[]{:S(2)}, u32[]{:S(2)}) %all-to-all-start.3) | async-done | bytes 1605664 | tf_op jit(solution)/shard_map/all_to_all | solution.py:499
  104.9 4.5 %shard_map.145 = (bf16[256,1536]{1,0:T(8,128)(2,1)}, f32[2,24,128]{2,1,0:T(8,128)}) custom-call(s32[1]{0:T(128)} %bitcast.1.place_ref, bf16[256,1536]{1,0:T(8,128)(2,1)} %get-tuple-element.55.kv_ref, bf16[2,768,128]{2,1,0:T(8,128)(2,1)} %get-tuple-element.73.s_ref, bf16[8,784,128]{2,1,0:T(8,128)(2,1)S(1)} %all-to-all-done.3.ra_ref, ...), custom_call_target="tpu_custom_call" | custom-call | flops 6049999872 | bytes 19800000 | tf_op jit(solution)/shard_map/pallas_call | solution.py:42
  109.6 3.7 %all-to-all-start.4 = ((bf16[16,16,768]{2,1,0:T(8,128)(2,1)}), bf16[16,16,768]{2,1,0:T(8,128)(2,1)S(1)}, u32[]{:S(2)}, u32[]{:S(2)}) async-start(bf16[16,16,768]{2,1,0:T(8,128)(2,1)} %bitcast.7), calls=%async_computation.4 | async-start | bytes 786432 | tf_op jit(solution)/shard_map/all_to_all | solution.py:499
  113.3 5.5 %shard_map.147.early_ref = bf16[512,2432]{1,0:T(8,128)(2,1)S(1)} custom-call(bf16[512,256]{1,0:T(8,128)(2,1)} %get-tuple-element.88.xk_ref, bf16[512,256]{1,0:T(8,128)(2,1)} %copy-done.11, bf16[512,256]{1,0:T(8,128)(2,1)} %get-tuple-element.90.xck_ref, bf16[512,256]{1,0:T(8,128)(2,1)} %collective-permute-done.2.xcr_ref, ...), custom_call_target="tpu_custom_call" | custom-call | flops 5500000256 | bytes 18000000 | tf_op jit(solution)/shard_map/pallas_call | solution.py:42
  118.9 3.8 %shard_map.148 = bf16[64,8,2432]{2,1,0:T(8,128)(2,1)} custom-call(bf16[512,256]{1,0:T(8,128)(2,1)} %get-tuple-element.88.xk_ref, bf16[512,256]{1,0:T(8,128)(2,1)} %copy-done.11, bf16[256,1536]{1,0:T(8,128)(2,1)} %get-tuple-element.86.dkv_ref, bf16[256,1536]{1,0:T(8,128)(2,1)S(1)} %collective-permute-done.5.dkvr_ref, bf16[512,2432]{1,0:T(8,128)(2,1)S(1)} %shard_map.147.early_ref), custom_call_target="tpu_custom_call" | custom-call | flops 4400000000 | bytes 14400000 | tf_op jit(solution)/shard_map/pallas_call | solution.py:42
  122.6 1.7 all-to-all-done.4.rx_ref
  124.3 8.7 %all-to-all-start.5 = ((bf16[64,8,2432]{2,1,0:T(8,128)(2,1)}), bf16[64,8,2432]{2,1,0:T(8,128)(2,1)S(1)}, u32[]{:S(2)}, u32[]{:S(2)}) async-start(bf16[64,8,2432]{2,1,0:T(8,128)(2,1)} %shard_map.148), calls=%async_computation.5 | async-start | bytes 4980736 | tf_op jit(solution)/shard_map/all_to_all | solution.py:499
  133.3 0.7 copy.25
  134.0 0.6 copy.24
  134.7 4.2 %shard_map.146 = bf16[256,768]{1,0:T(8,128)(2,1)} custom-call(bf16[256,768]{1,0:T(8,128)(2,1)} %get-tuple-element.92.dq_ref, bf16[256,1536]{1,0:T(8,128)(2,1)} %get-tuple-element.86.dkv_ref, bf16[768,2304]{1,0:T(8,128)(2,1)} %w_ref.9, bf16[16,16,768]{2,1,0:T(8,128)(2,1)S(1)} %all-to-all-done.4.rx_ref), custom_call_target="tpu_custom_call" | custom-call | flops 4400000000 | bytes 14400000 | tf_op jit(solution)/shard_map/pallas_call | solution.py:42
  138.9 28.9 %all-to-all-done.5.rx_ref = bf16[64,8,2432]{2,1,0:T(8,128)(2,1)S(1)} async-done(((bf16[64,8,2432]{2,1,0:T(8,128)(2,1)}), bf16[64,8,2432]{2,1,0:T(8,128)(2,1)S(1)}, u32[]{:S(2)}, u32[]{:S(2)}) %all-to-all-start.5) | async-done | bytes 2490400 | tf_op jit(solution)/shard_map/all_to_all | solution.py:499
  167.8 1.0 shard_map.149
  (51 shorter events, 2.1 us)
Async XLA Ops:
  0.6 10.3 %copy-start.4 = (s32[1024]{0:T(1024)S(1)}, s32[1024]{0:T(1024)}, u32[]{:S(2)}) copy-start(s32[1024]{0:T(1024)} %param.16) | copy-start | bytes 12292
  0.6 10.4 %copy-start.3 = (bf16[2,12,2,128]{3,2,1,0:T(2,128)(2,1)S(1)}, bf16[2,12,2,128]{3,2,1,0:T(2,128)(2,1)}, u32[]{:S(2)}) copy-start(bf16[2,12,2,128]{3,2,1,0:T(2,128)(2,1)} %param.14) | copy-start | bytes 36868
  2.7 8.3 %copy-start = (bf16[2,12,8,32]{3,2,1,0:T(8,128)(2,1)S(1)}, bf16[2,12,8,32]{3,2,1,0:T(8,128)(2,1)}, u32[]{:S(2)}) copy-start(bf16[2,12,8,32]{3,2,1,0:T(8,128)(2,1)} %param.15) | copy-start | bytes 36868
  2.7 8.7 %copy-start.6 = (s32[32]{0:T(128)S(1)}, s32[32]{0:T(128)}, u32[]{:S(2)}) copy-start(s32[32]{0:T(128)} %param.17) | copy-start | bytes 388
  2.7 23.4 %all-to-all-start = ((bf16[16,32,768]{2,1,0:T(8,128)(2,1)}), bf16[16,32,768]{2,1,0:T(8,128)(2,1)S(1)}, u32[]{:S(2)}, u32[]{:S(2)}) async-start(bf16[16,32,768]{2,1,0:T(8,128)(2,1)} %shard_map.139), calls=%async_computation | async-start | bytes 1572864 | tf_op jit(solution)/shard_map/all_to_all | solution.py:499
  26.1 25.9 %all-to-all-start.1 = ((bf16[8,784,128]{2,1,0:T(8,128)(2,1)}), bf16[8,784,128]{2,1,0:T(8,128)(2,1)S(1)}, u32[]{:S(2)}, u32[]{:S(2)}) async-start(bf16[8,784,128]{2,1,0:T(8,128)(2,1)} %get-tuple-element.60), calls=%async_computation.1 | async-start | bytes 3211264 | tf_op jit(solution)/shard_map/all_to_all | solution.py:499
  52.0 7.9 %copy-start.8 = (bf16[2,128,768]{2,1,0:T(8,128)(2,1)S(1)}, bf16[2,128,768]{2,1,0:T(8,128)(2,1)}, u32[]{:S(2)}) copy-start(bf16[2,128,768]{2,1,0:T(8,128)(2,1)} %g_ref.1) | copy-start | bytes 1179652
  52.0 8.4 %copy-start.12 = (bf16[512,256]{1,0:T(8,128)(2,1)S(1)}, bf16[512,256]{1,0:T(8,128)(2,1)}, u32[]{:S(2)}) copy-start(bf16[512,256]{1,0:T(8,128)(2,1)} %get-tuple-element.67) | copy-start | bytes 786436
  52.0 8.5 %copy-start.13 = (bf16[512,256]{1,0:T(8,128)(2,1)S(1)}, bf16[512,256]{1,0:T(8,128)(2,1)}, u32[]{:S(2)}) copy-start(bf16[512,256]{1,0:T(8,128)(2,1)} %get-tuple-element.68) | copy-start | bytes 786436
  52.0 8.9 %copy-start.5 = (f32[768]{0:T(1024)S(1)}, f32[768]{0:T(1024)}, u32[]{:S(2)}) copy-start(f32[768]{0:T(1024)} %param.13) | copy-start | bytes 9220
  56.3 18.8 %all-to-all-start.2 = ((bf16[16,32,768]{2,1,0:T(8,128)(2,1)}), bf16[16,32,768]{2,1,0:T(8,128)(2,1)S(1)}, u32[]{:S(2)}, u32[]{:S(2)}) async-start(bf16[16,32,768]{2,1,0:T(8,128)(2,1)} %get-tuple-element.66), calls=%async_computation.2 | async-start | bytes 1572864 | tf_op jit(solution)/shard_map/all_to_all | solution.py:499
  60.0 2.6 %collective-permute-start.1 = (bf16[256,768]{1,0:T(8,128)(2,1)S(1)}, bf16[256,768]{1,0:T(8,128)(2,1)S(1)}, u32[]{:S(2)}, u32[]{:S(2)}) collective-permute-start(bf16[256,768]{1,0:T(8,128)(2,1)S(1)} %bitcast.30), channel_id=1, source_target_pairs={{0,8},{8,0},{16,24},{24,16},{32,40},{40,32},{48,56},{56,48},{64,72... | collective-permute-start | bytes 1179656 | tf_op jit(solution)/shard_map/ppermute | solution.py:503
  60.5 2.1 %collective-permute-start = (bf16[512,256]{1,0:T(8,128)(2,1)S(1)}, bf16[512,256]{1,0:T(8,128)(2,1)S(1)}, u32[]{:S(2)}, u32[]{:S(2)}) collective-permute-start(bf16[512,256]{1,0:T(8,128)(2,1)S(1)} %copy-done.12), channel_id=1, source_target_pairs={{0,8},{8,0},{16,24},{24,16},{32,40},{40,32},{48,56},{56,48},{64,72... | collective-permute-start | bytes 786440 | tf_op jit(solution)/shard_map/ppermute | solution.py:503
  60.6 3.4 %collective-permute-start.2 = (bf16[512,256]{1,0:T(8,128)(2,1)S(1)}, bf16[512,256]{1,0:T(8,128)(2,1)}, u32[]{:S(2)}, u32[]{:S(2)}) collective-permute-start(bf16[512,256]{1,0:T(8,128)(2,1)S(1)} %copy-done.13), channel_id=1, source_target_pairs={{0,8},{8,0},{16,24},{24,16},{32,40},{40,32},{48,56},{56,48},{64,72... | collective-permute-start | bytes 786440 | tf_op jit(solution)/shard_map/ppermute | solution.py:503
  62.6 0.7 copy-start.11
  63.3 0.7 copy-start.9
  79.3 25.6 %all-to-all-start.3 = ((bf16[8,784,128]{2,1,0:T(8,128)(2,1)}), bf16[8,784,128]{2,1,0:T(8,128)(2,1)S(1)}, u32[]{:S(2)}, u32[]{:S(2)}) async-start(bf16[8,784,128]{2,1,0:T(8,128)(2,1)} %get-tuple-element.76), calls=%async_computation.3 | async-start | bytes 3211264 | tf_op jit(solution)/shard_map/all_to_all | solution.py:499
  92.0 9.8 %collective-permute-start.3 = (bf16[896,256]{1,0:T(8,128)(2,1)}, bf16[896,256]{1,0:T(8,128)(2,1)S(1)}, u32[]{:S(2)}, u32[]{:S(2)}) collective-permute-start(bf16[896,256]{1,0:T(8,128)(2,1)} %get-tuple-element.77), channel_id=1, source_target_pairs={{0,8},{8,0},{16,24},{24,16},{32,40},{40,32},{48,56},{56,48},{64,72... | collective-permute-start | bytes 1376264 | tf_op jit(solution)/shard_map/ppermute | solution.py:503
  92.0 9.8 %collective-permute-start.4 = (bf16[256,768]{1,0:T(8,128)(2,1)}, bf16[256,768]{1,0:T(8,128)(2,1)S(1)}, u32[]{:S(2)}, u32[]{:S(2)}) collective-permute-start(bf16[256,768]{1,0:T(8,128)(2,1)} %get-tuple-element.92.dq_ref), channel_id=1, source_target_pairs={{0,8},{8,0},{16,24},{24,16},{32,40},{40,32},{48,56},{56,48},{64,72... | collective-permute-start | bytes 1179656 | tf_op jit(solution)/shard_map/ppermute | solution.py:503
  101.8 11.5 %collective-permute-start.6 = (bf16[256,2304]{1,0:T(8,128)(2,1)}, bf16[256,2304]{1,0:T(8,128)(2,1)}, u32[]{:S(2)}, u32[]{:S(2)}) collective-permute-start(bf16[256,2304]{1,0:T(8,128)(2,1)} %get-tuple-element.94.dc_ref), channel_id=1, source_target_pairs={{0,8},{8,0},{16,24},{24,16},{32,40},{40,32},{48,56},{56,48},{64,72... | collective-permute-start | bytes 3538952 | tf_op jit(solution)/shard_map/ppermute | solution.py:503
  101.9 7.6 %copy-start.10 = (bf16[256,768]{1,0:T(8,128)(2,1)}, bf16[256,768]{1,0:T(8,128)(2,1)S(1)}, u32[]{:S(2)}) copy-start(bf16[256,768]{1,0:T(8,128)(2,1)S(1)} %collective-permute-done.4.dqr_ref) | copy-start | bytes 1179652
  101.9 7.6 %copy-start.7 = (bf16[896,256]{1,0:T(8,128)(2,1)}, bf16[896,256]{1,0:T(8,128)(2,1)S(1)}, u32[]{:S(2)}) copy-start(bf16[896,256]{1,0:T(8,128)(2,1)S(1)} %collective-permute-done.3.nr_ref) | copy-start | bytes 1376260
  109.5 9.4 %collective-permute-start.5 = (bf16[256,1536]{1,0:T(8,128)(2,1)}, bf16[256,1536]{1,0:T(8,128)(2,1)S(1)}, u32[]{:S(2)}, u32[]{:S(2)}) collective-permute-start(bf16[256,1536]{1,0:T(8,128)(2,1)} %get-tuple-element.86.dkv_ref), channel_id=1, source_target_pairs={{0,8},{8,0},{16,24},{24,16},{32,40},{40,32},{48,56},{56,48},{64,72... | collective-permute-start | bytes 2359304 | tf_op jit(solution)/shard_map/ppermute | solution.py:503
  109.6 14.7 %all-to-all-start.4 = ((bf16[16,16,768]{2,1,0:T(8,128)(2,1)}), bf16[16,16,768]{2,1,0:T(8,128)(2,1)S(1)}, u32[]{:S(2)}, u32[]{:S(2)}) async-start(bf16[16,16,768]{2,1,0:T(8,128)(2,1)} %bitcast.7), calls=%async_computation.4 | async-start | bytes 786432 | tf_op jit(solution)/shard_map/all_to_all | solution.py:499
  122.6 10.3 %copy-start.1 = (f32[2,12,256]{2,1,0:T(8,128)S(1)}, f32[2,12,256]{2,1,0:T(8,128)}, u32[]{:S(2)}) copy-start(f32[2,12,256]{2,1,0:T(8,128)} %get-tuple-element.103) | copy-start | bytes 73732
  122.6 11.4 %copy-start.2 = (f32[2,24,128]{2,1,0:T(8,128)S(1)}, f32[2,24,128]{2,1,0:T(8,128)}, u32[]{:S(2)}) copy-start(f32[2,24,128]{2,1,0:T(8,128)} %get-tuple-element.102) | copy-start | bytes 73732
  124.3 43.5 %all-to-all-start.5 = ((bf16[64,8,2432]{2,1,0:T(8,128)(2,1)}), bf16[64,8,2432]{2,1,0:T(8,128)(2,1)S(1)}, u32[]{:S(2)}, u32[]{:S(2)}) async-start(bf16[64,8,2432]{2,1,0:T(8,128)(2,1)} %shard_map.148), calls=%async_computation.5 | async-start | bytes 4980736 | tf_op jit(solution)/shard_map/all_to_all | solution.py:499

commit v4 on v3

--- a/solution.py
+++ b/solution.py
@@ -31,20 +31,55 @@
 LOAD = STATE + 16
 
 
-def call(body, us, outs, *args, smem=(), near=(), keep=(), scratch=()):
-    specs = [
-        pl.BlockSpec(memory_space=pltpu.SMEM if n in smem else pltpu.VMEM) for n in range(len(args))
-    ]
-    args = [
-        a if n in smem or n in near else pltpu.with_memory_space_constraint(a, pltpu.HBM)
-        for n, a in enumerate(args)
-    ]
+class Arriving:
+    def __init__(self, source, buffer, semaphore):
+        self.copy = pltpu.make_async_copy(source, buffer, semaphore)
+        self.copy.start()
+        self.buffer = buffer
+        self.here = False
+
+    def arrive(self):
+        if not self.here:
+            self.copy.wait()
+            self.here = True
+
+    def __getitem__(self, index):
+        self.arrive()
+        return self.buffer[index]
+
+
+def call(body, us, outs, *args, smem=(), near=(), keep=(), scratch=(), staged=False):
+    far = [n for n in range(len(args)) if n not in smem and n not in near]
+    specs = [pl.BlockSpec(memory_space=pltpu.VMEM)] * len(args)
+    args = list(args)
+    for n in smem:
+        specs[n] = pl.BlockSpec(memory_space=pltpu.SMEM)
+    for n in far:
+        args[n] = pltpu.with_memory_space_constraint(args[n], pltpu.HBM)
+    scratch = list(scratch)
+    kernel = body
+    if staged:
+        for n in far:
+            specs[n] = pl.BlockSpec(memory_space=pl.ANY)
+        scratch += [pltpu.VMEM(args[n].shape, args[n].dtype) for n in far]
+        scratch += [pltpu.SemaphoreType.DMA((len(far),))]
+
+        def kernel(*refs):
+            refs, semaphores = list(refs[:-1]), refs[-1]
+            last = len(refs) - len(far)
+            arriving = [Arriving(refs[n], refs[last + k], semaphores.at[k]) for k, n in enumerate(far)]
+            for k, n in enumerate(far):
+                refs[n] = arriving[k]
+            body(*refs[:last])
+            for operand in arriving:
+                operand.arrive()
+
     return pl.pallas_call(
-        body,
+        kernel,
         out_shape=[(pltpu.VMEM if n in keep else pltpu.HBM)(s, t) for n, (s, t) in enumerate(outs)],
         in_specs=specs,
         out_specs=[pl.BlockSpec(memory_space=pltpu.VMEM)] * len(outs),
-        scratch_shapes=list(scratch),
+        scratch_shapes=scratch,
         cost_estimate=pl.CostEstimate(
             flops=int(us * 1.1e9), bytes_accessed=int(us * 3.6e6), transcendentals=0
         ),
@@ -105,16 +140,38 @@
 
 
 def gather_states(place, rx_ref, from_left, state_ref):
+    few = 3
+
+    def run(direction, count, source_of):
+        for first in range(0, UNITS, few):
+            rows = slice(first * HEAD_DIM, (first + few) * HEAD_DIM)
+
+            def step(n, state):
+                source = source_of(n)
+                th = rx_ref[source, STATE:LOAD, :].astype(F32)
+                wide = [jnp.broadcast_to(th[u : u + 1], (HEAD_DIM, 128)) for u in range(first, first + few)]
+                return jnp.concatenate(wide, axis=0) * state + rx_ref[source, rows, :].astype(F32)
+
+            state = lax.fori_loop(0, count, step, jnp.zeros((few * HEAD_DIM, 128), F32))
+            state_ref[direction, rows, :] = state.astype(BF)
+
+    run(0 if from_left else 1, place, lambda n: n)
+    run(1 if from_left else 0, 7 - place, lambda n: 7 - n)
+
+
+def chain_states(place, refs, state_ref):
     state_ref[...] = jnp.zeros_like(state_ref)
 
-    def step(direction, source):
+    def step(direction, ref):
         for u in range(UNITS):
             rows = slice(u * HEAD_DIM, (u + 1) * HEAD_DIM)
-            th = rx_ref[source, STATE:LOAD, :].astype(F32)[u : u + 1]
-            state_ref[direction, rows, :] = th * state_ref[direction, rows, :] + rx_ref[source, rows, :].astype(F32)
-
-    lax.fori_loop(0, place, lambda n, c: (step(0 if from_left else 1, n), c)[1], 0)
-    lax.fori_loop(0, 7 - place, lambda n, c: (step(1 if from_left else 0, 7 - n), c)[1], 0)
+            th = ref[STATE:LOAD, :].astype(F32)[u : u + 1]
+            state_ref[direction, rows, :] = th * state_ref[direction, rows, :] + ref[rows, :].astype(F32)
+
+    for back in range(7, 0, -1):
+        pl.when(back <= place)(lambda back=back: step(0, refs[back - 1]))
+    for back in range(1, 8):
+        pl.when(back > place)(lambda back=back: step(1, refs[back - 1]))
 
 
 def first_feature(n, j, core):
@@ -162,7 +219,8 @@
         out_ref[:, n * 16 : (n + 1) * 16, :] = wide.astype(BF)
 
 
-def summary_kernel(place_ref, ldr_ref, bc_ref, x_ref, w_ref, fac_ref, th_ref, kv_ref, u_ref, both_ref):
+def summary_kernel(place_ref, ldr_ref, bc_ref, x_ref, w_ref, fac_ref, th_ref, kv_ref, *refs):
+    u_refs, both_ref = refs[:7], refs[7]
     i0, i1, le, ge, seg_row, seg_col, following = row_masks(bc_ref)
     first, last = seg_row[:, 0:1], seg_row[:, COLS - 1 : COLS]
     after = last + following
@@ -197,7 +255,8 @@
                 tv = (lanes_of(fac_ref[r], 2 + direction, p) * v).astype(BF)
                 both_ref[direction, unit_rows(r, p), :] = compact(tn(k, tv)).astype(BF)
     both_ref[:, STATE:LOAD, :] = th_ref[...].astype(BF)
-    spread(both_ref, place_ref[0], True, u_ref)
+    for n, u_ref in enumerate(u_refs):
+        u_ref[...] = both_ref[jnp.where(place_ref[0] + n + 1 < 8, 0, 1)]
 
 
 def mask_kernel(ldr_ref, ldc_ref, bc_ref, br_ref, dep_ref, wr_ref, wc_ref):
@@ -228,14 +287,22 @@
         wc_ref[h // 2, (h % 2) * TOK : (h % 2 + 1) * TOK, :] = w.astype(BF)
 
 
-def row_inside_kernel(
-    core_ref, x_ref, g_ref, w_ref, wo_ref, kv_ref, wr_ref, q_ref, dn_ref, keep_ref, send_ref, out_ref, probs_ref
+def side_kernel(
+    core_ref, x_ref, g_ref, rx_ref, wo_ref, dn_ref, dnc_ref, keep_ref, send_ref, ckeep_ref, csend_ref
 ):
     core = core_ref[0]
-    send_ref[...] = nt(pick_rows(1 - core), x_ref[...]).astype(BF)
-    keep_ref[...] = nt(pick_rows(core), x_ref[...]).astype(BF)
+    own, other = pick_rows(core), pick_rows(1 - core)
+    xc = rx_ref[:, 0:16, :].reshape(TOK, D)
+    csend_ref[...] = nt(other, xc).astype(BF)
+    ckeep_ref[...] = nt(own, xc).astype(BF)
+    send_ref[...] = nt(other, x_ref[...]).astype(BF)
+    keep_ref[...] = nt(own, x_ref[...]).astype(BF)
+    dn_ref[...] = nt(g_ref[...], wo_ref[...]).astype(BF)
+    dnc_ref[...] = nt(rx_ref[:, 16:32, :].reshape(TOK, D), wo_ref[...]).astype(BF)
+
+
+def row_inside_kernel(x_ref, w_ref, kv_ref, wr_ref, q_ref, out_ref, probs_ref):
     q_ref[...] = nn(x_ref[...], w_ref[:, :D]).astype(BF)
-    dn_ref[...] = nt(g_ref[...], wo_ref[...]).astype(BF)
     for r in range(ROWS):
         rows = slice(r * COLS, (r + 1) * COLS)
         for p in range(PAIRS):
@@ -248,11 +315,8 @@
             out_ref[rows, lanes] = nn(side(probs), split_heads(v))
 
 
-def col_forward_kernel(
-    core_ref, rx_ref, w_ref, wo_ref, wc_ref, qkv_ref, dn_ref, out_ref, probs_ref, keep_ref, send_ref
-):
+def col_forward_kernel(rx_ref, w_ref, wc_ref, qkv_ref, out_ref, probs_ref):
     x = rx_ref[:, 0:16, :].reshape(TOK, D)
-    g = rx_ref[:, 16:32, :].reshape(TOK, D)
     qkv_ref[...] = nn(x, w_ref[...]).astype(BF)
     for p in range(PAIRS):
         q = qkv_ref[:, p * 128 : (p + 1) * 128]
@@ -261,10 +325,6 @@
         probs = (nt(split_heads(q), k) * wc_ref[p].astype(F32)).astype(BF)
         probs_ref[p] = probs
         out_ref[:, p * 128 : (p + 1) * 128] = nn(side(probs), split_heads(v)).astype(BF)
-    dn_ref[...] = nt(g, wo_ref[...]).astype(BF)
-    core = core_ref[0]
-    keep_ref[...] = nt(pick_rows(core), x).astype(BF)
-    send_ref[...] = nt(pick_rows(1 - core), x).astype(BF)
 
 
 def state_of(s_ref, direction, r, p):
@@ -275,10 +335,10 @@
     return jnp.concatenate([split_heads(state_of(s_ref, d, r, p)) for d in range(2)], axis=1)
 
 
-def row_join_kernel(place_ref, q_ref, rs_ref, fac_ref, inside_ref, col_ref, out_ref, xch_ref, s_ref, wide_ref):
-    gather_states(place_ref[0], rs_ref, True, wide_ref)
+def row_join_kernel(place_ref, q_ref, fac_ref, inside_ref, col_ref, *refs):
+    out_ref, xch_ref, s_ref, wide_ref = refs[7:]
+    chain_states(place_ref[0], refs[:7], wide_ref)
     s_ref[...] = wide_ref[...].astype(BF)
-    xch_ref[:, 0:16, :] = col_ref[...].reshape(16, 16, D)
     for r in range(ROWS):
         rows = slice(r * COLS, (r + 1) * COLS)
         for p in range(PAIRS):
@@ -287,9 +347,10 @@
             out = inside_ref[rows, lanes]
             out = out + lanes_of(fac_ref[r], 0, p) * carried[:, :128]
             out = out + lanes_of(fac_ref[r], 1, p) * carried[:, 128:]
-            out_ref[rows, lanes] = out
-    slab = out_ref[...].reshape(2, 16, 8, D).swapaxes(0, 1).reshape(16, 16, D)
+            out_ref[rows, lanes] = out.astype(BF)
+    slab = out_ref[...].astype(F32).reshape(2, 16, 8, D).swapaxes(0, 1).reshape(16, 16, D)
     xch_ref[:, 16:32, :] = slab.astype(BF)
+    xch_ref[:, 0:16, :] = col_ref[...].reshape(16, 16, D)
 
 
 def norm_backward(mixed, dn, gain):
@@ -307,7 +368,7 @@
 def row_middle_kernel(
     place_ref, rx_ref, row_ref, dn_ref, gain_ref, q_ref, fac_ref, th_ref, dm_ref, g_ref, both_ref
 ):
-    mixed = row_ref[...] + from_slab(rx_ref[:, 0:16, :])
+    mixed = row_ref[...].astype(F32) + from_slab(rx_ref[:, 0:16, :])
     _, d_mixed = norm_backward(mixed, dn_ref[...].astype(F32), gain_ref[...])
     dm_ref[...] = d_mixed.astype(BF)
     for r in range(ROWS):
@@ -366,7 +427,7 @@
     core_ref, rx_ref, row_ref, dn_ref, gain_ref, q_ref, kv_ref, dm_ref, s_ref, wr_ref, probs_ref, fac_ref,
     dq_ref, part_ref, gd_ref, keep_ref, send_ref,
 ):
-    mixed = row_ref[...] + from_slab(rx_ref[:, 0:16, :])
+    mixed = row_ref[...].astype(F32) + from_slab(rx_ref[:, 0:16, :])
     unit = mixed * lax.rsqrt(jnp.mean(mixed * mixed, axis=-1, keepdims=True) + EPSILON)
     normed = (unit * gain_ref[...]).astype(BF)
     gain_terms = (dn_ref[...].astype(F32) * unit).astype(BF)
@@ -413,10 +474,9 @@
 
 
 def row_finish_kernel(
-    place_ref, kv_ref, s_ref, ra_ref, fac_ref, th_ref, part_ref, gdp_ref, dkv_ref, gd_ref, wide_ref, a_ref
+    place_ref, kv_ref, s_ref, ra_ref, fac_ref, th_ref, part_ref, gdp_ref, dkv_ref, gd_ref, a_ref
 ):
-    gather_states(place_ref[0], ra_ref, False, wide_ref)
-    a_ref[...] = wide_ref[...].astype(BF)
+    gather_states(place_ref[0], ra_ref, False, a_ref)
     i0, i1 = iota((COLS, COLS), 0), iota((COLS, COLS), 1)
     tails, throughs = [[], []], [[], []]
     for r in range(ROWS):
@@ -516,7 +576,6 @@
     gain = gain.reshape(1, D)
     half = (SPLIT, TOK)
     load = ((8, LOAD, 128), BF)
-    wide = pltpu.VMEM((2, STATE, 128), F32)
     narrow = pltpu.VMEM((2, LOAD, 128), BF)
 
     x = tokens.reshape(TOK, D)
@@ -529,35 +588,41 @@
     tiles = jnp.concatenate([border_cols, jnp.zeros((COLS,), jnp.int32)]).reshape(9, COLS)
     bc = lax.dynamic_slice_in_dim(tiles, place, 2)
     br = jnp.broadcast_to(border_rows[:, None], (GRID_H, CD)).reshape(1, TOK)
-    fac, th, kv, update = call(
-        summary_kernel, 4.6,
-        [((ROWS, COLS, 4 * HEADS), F32), ((2, 16, 128), F32), ((TOK, 2 * D), BF), load],
-        at, ldr, bc, x, w_qkv, smem=(0,), near=(1, 2), keep=(3,), scratch=[narrow],
-    )
+    fac, th, kv, *updates = call(
+        summary_kernel, 0.1,
+        [((ROWS, COLS, 4 * HEADS), F32), ((2, 16, 128), F32), ((TOK, 2 * D), BF)] + [((LOAD, 128), BF)] * 7,
+        at, ldr, bc, after(x, first), w_qkv, smem=(0,), near=(1, 2), scratch=[narrow], staged=True,
+    )
+    states = [
+        lax.ppermute(u, "col", [(i, (i + n + 1) % 8) for i in range(8)]) for n, u in enumerate(updates)
+    ]
     wr, wc = call(
-        mask_kernel, 4.3,
+        mask_kernel, 0.1,
         [((UNITS, 2 * COLS, COLS), BF), ((PAIRS, 2 * TOK, TOK), BF)],
-        ldr, ldc, bc, br, th, near=(0, 1, 2, 3),
-    )
-    states = exchange(after(update, rx, wr), "col")
-    q, dn, x_keep, x_send, inside, probs = call(
-        row_inside_kernel, 5.7,
-        [((TOK, D), BF), ((TOK, D), BF), (half, BF), (half, BF), ((TOK, D), F32), ((UNITS, 2 * COLS, COLS), BF)],
-        core, x, g, w_qkv, w_out, kv, wr, smem=(0,),
-    )
-    x_far, g_far = swap(x_send), swap(g)
-    qkv_c, dn_c, col_out, probs_c, xc_keep, xc_send = call(
+        ldr, ldc, bc, br, th, near=(0, 1, 2, 3), staged=True,
+    )
+    q, inside, probs = call(
+        row_inside_kernel, 0.1,
+        [((TOK, D), BF), ((TOK, D), F32), ((UNITS, 2 * COLS, COLS), BF)],
+        x, w_qkv, after(kv, states[0]), wr, staged=True,
+    )
+    qkv_c, col_out, probs_c = call(
         col_forward_kernel, 6.8,
-        [((TOK, F), BF), ((TOK, D), BF), ((TOK, D), BF), ((PAIRS, 2 * TOK, TOK), BF), (half, BF), (half, BF)],
-        core, rx, w_qkv, w_out, wc, smem=(0,), near=(1,),
-    )
-    states = after(states, col_out, q)
+        [((TOK, F), BF), ((TOK, D), BF), ((PAIRS, 2 * TOK, TOK), BF)],
+        after(rx, *states[:5]), w_qkv, wc, near=(0,), staged=True,
+    )
     row_out, out_swap, entering = call(
         row_join_kernel, 5.0,
-        [((TOK, D), F32), ((16, 32, D), BF), ((2, STATE, 128), BF)],
-        at, q, states, fac, inside, col_out, smem=(0,), near=(2,), keep=(1,), scratch=[wide],
-    )
-    xc_far = swap(xc_send)
+        [((TOK, D), BF), ((16, 32, D), BF), ((2, STATE, 128), BF)],
+        at, q, fac, inside, after(col_out, q), *states, smem=(0,), near=tuple(range(5, 12)), keep=(1,),
+        scratch=[pltpu.VMEM((2, STATE, 128), F32)], staged=True,
+    )
+    dn, dn_c, x_keep, x_send, xc_keep, xc_send = call(
+        side_kernel, 5.0,
+        [((TOK, D), BF), ((TOK, D), BF), (half, BF), (half, BF), (half, BF), (half, BF)],
+        core, after(x, entering), g, rx, w_out, smem=(0,),
+    )
+    x_far, g_far, xc_far = swap(x_send), swap(g), swap(xc_send)
     rx2 = exchange(out_swap, "row")
     rx2, x_far, g_far, xc_far = lax.optimization_barrier((rx2, x_far, g_far, xc_far))
     dm, adj = call(
@@ -581,22 +646,22 @@
     adj, n_far, dq_far, tok_c = lax.optimization_barrier((adj, n_far, dq_far, tok_c))
     rx3 = exchange(tok_c.reshape(16, 16, D), "row")
     dkv, gdr = call(
-        row_finish_kernel, 5.5,
+        row_finish_kernel, 0.3,
         [((TOK, 2 * D), BF), ((2, 2 * HEADS, COLS), F32)],
         at, kv, entering, adj, fac, th, part, gd_part,
-        smem=(0,), near=(3,), scratch=[wide, pltpu.VMEM((2, STATE, 128), BF)],
+        smem=(0,), near=(3,), scratch=[pltpu.VMEM((2, STATE, 128), BF)], staged=True,
     )
     dkv_far = swap(dkv)
     (early,) = call(
-        weight_early_kernel, 5.0,
+        weight_early_kernel, 0.3,
         [((SPLIT, WIDE), BF)],
         x_keep, x_far, xc_keep, xc_far, after(dq, dkv), dq_far, dqkv_c, dqkv_c_far, n_keep, n_far, g, g_far,
         keep=(0,),
     )
     (wg,) = call(
-        weight_late_kernel, 4.0,
+        weight_late_kernel, 0.3,
         [((64, 8, WIDE), BF)],
-        x_keep, x_far, dkv, dkv_far, early, near=(3, 4), keep=(0,),
+        x_keep, x_far, dkv, dkv_far, early, near=(3, 4), keep=(0,), staged=True,
     )
     wg = exchange(after(wg, rx3), ("row", "col"), SAME_CORE)
     grad_qkv, grad_out_weight, grad_gain = call(

time: 170 us -> 165 us (0.971)
  waiting for transfers between devices: 60.6 us -> 46.5 us
  starting transfers between devices: 34.6 us -> 45.1 us
    all_to_all x6 -> x5, waiting for transfers between devices: 59 us -> 42.5 us  [exchange(): return lax.all_to_all(x, axis, 0, 0, tiled=True, axis_index_groups=groups)]
    ppermute x0 -> x7, starting transfers between devices: none -> 11.5 us  [per_device(): lax.ppermute(u, 'col', [(i, (i + n + 1) % 8) for i in range(8)])]
    ppermute x0 -> x7, waiting for transfers between devices: none -> 2.26 us  [per_device(): lax.ppermute(u, 'col', [(i, (i + n + 1) % 8) for i in range(8)])]
    all_to_all x6 -> x5, starting transfers between devices: 33 us -> 32.2 us  [exchange(): return lax.all_to_all(x, axis, 0, 0, tiled=True, axis_index_groups=groups)]
    pallas_call x14 -> x15, Pallas kernels: 68.9 us -> 69.7 us  [call(): pl.pallas_call(kernel, out_shape=[(pltpu.VMEM if n in keep else pltpu.HBM...]
  transfers between devices with their start and end apart: 13 -> 19, of which waited for: 7 -> 8; matrix products, arithmetic and copies ran while one was open for 1% -> 1% of each run, Pallas kernels for 34% -> 38%
where the time goes in v4:
time: 165 us
  Pallas kernels  69.7 us (42%)
  waiting for transfers between devices  46.5 us (28%)
  starting transfers between devices  45.1 us (27%)
  local copies, waits for them, and re-layouts  2.27 us (1%)
    pallas_call x15, Pallas kernels, call(): pl.pallas_call(kernel, out_shape=[(pltpu.VMEM if n in keep else pltpu.HBM...  69.7 us
    all_to_all x5, waiting for transfers between devices, exchange(): return lax.all_to_all(x, axis, 0, 0, tiled=True, axis_index_groups=groups)  42.5 us
    all_to_all x5, starting transfers between devices, exchange(): return lax.all_to_all(x, axis, 0, 0, tiled=True, axis_index_groups=groups)  32.2 us
    ppermute x7, starting transfers between devices, per_device(): lax.ppermute(u, 'col', [(i, (i + n + 1) % 8) for i in range(8)])  11.5 us
  transfers between devices with their start and end apart: 19, of which 8 were waited for; matrix products, arithmetic and copies ran while one was open for 1% of the time, Pallas kernels for 38%

profile of v4, /device:TPU:0, one launch (start us, length us, event | category | flops | bytes accessed | tf_op | source)
XLA Modules:
  0.0 164.6 jit_solution(4461143773047871990)
XLA Ops:
  0.6 2.1 %shard_map.136 = bf16[16,32,768]{2,1,0:T(8,128)(2,1)} custom-call(bf16[2,128,768]{2,1,0:T(8,128)(2,1)} %x_ref.1, bf16[2,128,768]{2,1,0:T(8,128)(2,1)} %g_ref.1), custom_call_target="tpu_custom_call" | custom-call | flops 2200000000 | bytes 7200000 | tf_op jit(solution)/shard_map/pallas_call | solution.py:77
  2.7 8.3 %all-to-all-start = ((bf16[16,32,768]{2,1,0:T(8,128)(2,1)}), bf16[16,32,768]{2,1,0:T(8,128)(2,1)S(1)}, u32[]{:S(2)}, u32[]{:S(2)}) async-start(bf16[16,32,768]{2,1,0:T(8,128)(2,1)} %shard_map.136), calls=%async_computation | async-start | bytes 1572864 | tf_op jit(solution)/shard_map/all_to_all | solution.py:559
  11.1 4.8 %shard_map.137 = (f32[2,128,48]{2,1,0:T(8,128)}, f32[2,16,128]{2,1,0:T(8,128)}, bf16[256,1536]{1,0:T(8,128)(2,1)}, bf16[784,128]{1,0:T(8,128)(2,1)}, bf16[784,12...) custom-call(s32[1]{0:T(128)} %bitcast.1.refs_0_.place_ref, ...), custom_call_target="tpu_custom_call" | custom-call | flops 110000000 | bytes 360000 | tf_op jit(solution)/shard_map/pallas_call | solution.py:77
  15.8 1.6 collective-permute-start
  17.4 2.7 %collective-permute-start.1 = (bf16[784,128]{1,0:T(8,128)(2,1)}, bf16[784,128]{1,0:T(8,128)(2,1)S(1)}, u32[]{:S(2)}, u32[]{:S(2)}) collective-permute-start(bf16[784,128]{1,0:T(8,128)(2,1)} %get-tuple-element.73), channel_id=1, source_target_pairs={{0,2},{1,3},{2,4},{3,5},{4,6},{5,7},{6,0},{7,1},{8,10},{9,11},{10,... | collective-permute-start | bytes 602120 | tf_op jit(solution)/shard_map/ppermute | solution.py:597
  20.1 1.6 collective-permute-start.2
  21.7 1.3 collective-permute-start.3
  24.3 3.5 %shard_map.138 = (bf16[12,256,128]{2,1,0:T(8,128)(2,1)}, bf16[6,512,256]{2,1,0:T(8,128)(2,1)}) custom-call(bf16[2,2,12,128]{3,2,1,0:T(8,128)(2,1)S(1)} %bitcast.22, bf16[2,12,256]{2,1,0:T(8,128)(2,1)S(1)} %reshape.63.refs_1_, s32[2,128]{1,0:T(2,128)S(1)} %constant_dynamic-slice_fusion.refs_2_, s32[1,256]{1,0:T(1,128)S(1)} %reshape.56.refs_3_, ...), custom_call_target="tpu_custom_call" | custom-call | flops 110000000 | bytes 360000 | tf_op jit(solution)/shard_map/pallas_call | solution.py:77
  27.9 2.8 %collective-permute-start.5 = (bf16[784,128]{1,0:T(8,128)(2,1)}, bf16[784,128]{1,0:T(8,128)(2,1)S(1)}, u32[]{:S(2)}, u32[]{:S(2)}) collective-permute-start(bf16[784,128]{1,0:T(8,128)(2,1)} %get-tuple-element.81), channel_id=1, source_target_pairs={{0,6},{1,7},{2,0},{3,1},{4,2},{5,3},{6,4},{7,5},{8,14},{9,15},{10,... | collective-permute-start | bytes 602120 | tf_op jit(solution)/shard_map/ppermute | solution.py:597
  30.7 5.0 %shard_map.139 = (bf16[256,768]{1,0:T(8,128)(2,1)}, f32[256,768]{1,0:T(8,128)}, bf16[12,256,128]{2,1,0:T(8,128)(2,1)}) custom-call(bf16[256,768]{1,0:T(8,128)(2,1)} %bitcast.24, bf16[768,2304]{1,0:T(8,128)(2,1)} %w_ref.3, bf16[256,1536]{1,0:T(8,128)(2,1)} %get-tuple-element.67.refs_2_.kv_ref.refs_1_, bf16[12,256,128]{2,1,0:T(8,128)(2,1)} %get-tuple-element.69.refs_3_.wr_ref), custom_call_target="tpu_custom_call" | custom-call | flops 110000000 | bytes 360000 | tf_op jit(solution)/shard_map/pallas_call | solution.py:77
  36.5 2.2 %collective-permute-done.3.refs_8_ = bf16[784,128]{1,0:T(8,128)(2,1)S(1)} collective-permute-done((bf16[784,128]{1,0:T(8,128)(2,1)}, bf16[784,128]{1,0:T(8,128)(2,1)S(1)}, u32[]{:S(2)}, u32[]{:S(2)}) %collective-permute-start.3) | collective-permute-done | bytes 200736 | tf_op jit(solution)/shard_map/ppermute | solution.py:597
  39.3 5.8 %shard_map.140 = (bf16[256,2304]{1,0:T(8,128)(2,1)}, bf16[256,768]{1,0:T(8,128)(2,1)}, bf16[6,512,256]{2,1,0:T(8,128)(2,1)}) custom-call(bf16[16,32,768]{2,1,0:T(8,128)(2,1)S(1)} %all-to-all-done.refs_0_.rx_ref, bf16[768,2304]{1,0:T(8,128)(2,1)} %w_ref.3, bf16[6,512,256]{2,1,0:T(8,128)(2,1)} %get-tuple-element.78.refs_2_.wc_ref), custom_call_target="tpu_custom_call" | custom-call | flops 7480000000 | bytes 24480000 | tf_op jit(solution)/shard_map/pallas_call | solution.py:77
  45.1 3.6 %shard_map.141 = (bf16[256,768]{1,0:T(8,128)(2,1)}, bf16[16,32,768]{2,1,0:T(8,128)(2,1)}, bf16[2,768,128]{2,1,0:T(8,128)(2,1)}) custom-call(s32[1]{0:T(128)} %bitcast.1.refs_0_.place_ref, bf16[256,768]{1,0:T(8,128)(2,1)} %get-tuple-element.70.refs_1_.q_ref, f32[2,128,48]{2,1,0:T(8,128)} %get-tuple-element.71.refs_2_.fac_ref.refs_4_, ...), custom_call_target="tpu_custom_call" | custom-call | flops 5500000256 | bytes 18000000 | tf_op jit(solution)/shard_map/pallas_call | solution.py:77
  48.8 7.1 %all-to-all-start.1 = ((bf16[16,32,768]{2,1,0:T(8,128)(2,1)}), bf16[16,32,768]{2,1,0:T(8,128)(2,1)S(1)}, u32[]{:S(2)}, u32[]{:S(2)}) async-start(bf16[16,32,768]{2,1,0:T(8,128)(2,1)} %get-tuple-element.83), calls=%async_computation.1 | async-start | bytes 1572864 | tf_op jit(solution)/shard_map/all_to_all | solution.py:559
  55.9 4.3 %shard_map.142 = (bf16[256,768]{1,0:T(8,128)(2,1)}, bf16[256,768]{1,0:T(8,128)(2,1)}, bf16[512,256]{1,0:T(8,128)(2,1)}, bf16[512,256]{1,0:T(8,128)(2,1)}, bf16[5...) custom-call(s32[1]{0:T(128)} %bitcast.core_ref, bf16[256,768]{1,0:T(8,128)(2,1)} %bitcast.25, bf16[256,768]{1,0:T(8,128)(2,1)} %bitcast.27, ...), custom_call_target="tpu_custom_call" | custom-call | flops 5500000256 | bytes 18000000 | tf_op jit(solution)/shard_map/pallas_call | solution.py:77
  60.7 1.2 collective-permute-done.7.xr_ref.refs_1_
  62.5 8.6 %all-to-all-done.1.rx_ref = bf16[16,32,768]{2,1,0:T(8,128)(2,1)S(1)} async-done(((bf16[16,32,768]{2,1,0:T(8,128)(2,1)}), bf16[16,32,768]{2,1,0:T(8,128)(2,1)S(1)}, u32[]{:S(2)}, u32[]{:S(2)}) %all-to-all-start.1) | async-done | bytes 786464 | tf_op jit(solution)/shard_map/all_to_all | solution.py:559
  71.0 4.1 %shard_map.143 = (bf16[256,768]{1,0:T(8,128)(2,1)}, bf16[8,784,128]{2,1,0:T(8,128)(2,1)}) custom-call(s32[1]{0:T(128)} %bitcast.1.refs_0_.place_ref, bf16[16,32,768]{2,1,0:T(8,128)(2,1)S(1)} %all-to-all-done.1.rx_ref, bf16[256,768]{1,0:T(8,128)(2,1)} %get-tuple-element.89.row_ref, bf16[256,768]{1,0:T(8,128)(2,1)} %get-tuple-element.90.dn_ref, ...), custom_call_target="tpu_custom_call" | custom-call | flops 4950000128 | bytes 16200000 | tf_op jit(solution)/shard_map/pallas_call | solution.py:77
  75.1 4.6 %all-to-all-start.2 = ((bf16[8,784,128]{2,1,0:T(8,128)(2,1)}), bf16[8,784,128]{2,1,0:T(8,128)(2,1)S(1)}, u32[]{:S(2)}, u32[]{:S(2)}) async-start(bf16[8,784,128]{2,1,0:T(8,128)(2,1)} %get-tuple-element.94), calls=%async_computation.2 | async-start | bytes 3211264 | tf_op jit(solution)/shard_map/all_to_all | solution.py:559
  79.7 8.4 %shard_map.144 = (bf16[256,768]{1,0:T(8,128)(2,1)}, bf16[256,1536]{1,0:T(8,128)(2,1)}, f32[2,24,128]{2,1,0:T(8,128)}, bf16[896,256]{1,0:T(8,128)(2,1)}, bf16[896,256]{1,0:T(8,128)(2,1)}) custom-call(s32[1]{0:T(128)} %bitcast.core_ref, bf16[16,32,768]{2,1,0:T(8,128)(2,1)S(1)} %all-to-all-done.1.rx_ref, bf16[256,768]{1,0:T(8,128)(2,1)} %get-tuple-element.89.row_ref, ...), custom_call_target="tpu_custom_call" | custom-call | flops 9790000128 | bytes 32040000 | tf_op jit(solution)/shard_map/pallas_call | solution.py:77
  88.7 9.3 %shard_map.145 = (bf16[256,2304]{1,0:T(8,128)(2,1)}, f32[2,12,256]{2,1,0:T(8,128)}, bf16[256,768]{1,0:T(8,128)(2,1)}) custom-call(bf16[16,32,768]{2,1,0:T(8,128)(2,1)S(1)} %all-to-all-done.1.rx_ref, bf16[256,768]{1,0:T(8,128)(2,1)} %get-tuple-element.80.refs_4_.col_ref, bf16[256,768]{1,0:T(8,128)(2,1)} %get-tuple-element.97.dn_ref, ...), custom_call_target="tpu_custom_call" | custom-call | flops 10670000128 | bytes 34920000 | tf_op jit(solution)/shard_map/pallas_call | solution.py:77
  98.2 2.9 %all-to-all-done.2.refs_3_ = bf16[8,784,128]{2,1,0:T(8,128)(2,1)S(1)} async-done(((bf16[8,784,128]{2,1,0:T(8,128)(2,1)}), bf16[8,784,128]{2,1,0:T(8,128)(2,1)S(1)}, u32[]{:S(2)}, u32[]{:S(2)}) %all-to-all-start.2) | async-done | bytes 1605664 | tf_op jit(solution)/shard_map/all_to_all | solution.py:559
  101.2 4.2 %shard_map.146 = (bf16[256,1536]{1,0:T(8,128)(2,1)}, f32[2,24,128]{2,1,0:T(8,128)}) custom-call(s32[1]{0:T(128)} %bitcast.1.refs_0_.place_ref, bf16[256,1536]{1,0:T(8,128)(2,1)} %get-tuple-element.67.refs_2_.kv_ref.refs_1_, bf16[2,768,128]{2,1,0:T(8,128)(2,1)} %get-tuple-element.84.s_ref.refs_2_, bf16[8,784,128]{2,1,0:T(8,128)(2,1)S(1)} %all-to-all-done.2.refs_3_, ...), custom_call_target="tpu_custom_call" | custom-call | flops 330000000 | bytes 1080000 | tf_op jit(solution)/shard_map/pallas_call | solution.py:77
  105.5 3.7 %all-to-all-start.3 = ((bf16[16,16,768]{2,1,0:T(8,128)(2,1)}), bf16[16,16,768]{2,1,0:T(8,128)(2,1)S(1)}, u32[]{:S(2)}, u32[]{:S(2)}) async-start(bf16[16,16,768]{2,1,0:T(8,128)(2,1)} %bitcast.7), calls=%async_computation.3 | async-start | bytes 786432 | tf_op jit(solution)/shard_map/all_to_all | solution.py:559
  109.3 5.5 %shard_map.148.refs_4_ = bf16[512,2432]{1,0:T(8,128)(2,1)S(1)} custom-call(bf16[512,256]{1,0:T(8,128)(2,1)} %get-tuple-element.106.xk_ref.refs_0_, bf16[512,256]{1,0:T(8,128)(2,1)} %copy-done.1, bf16[512,256]{1,0:T(8,128)(2,1)} %get-tuple-element.108.xck_ref, bf16[512,256]{1,0:T(8,128)(2,1)} %collective-permute-done.9.xcr_ref, ...), custom_call_target="tpu_custom_call" | custom-call | flops 330000000 | bytes 1080000 | tf_op jit(solution)/shard_map/pallas_call | solution.py:77
  114.8 3.8 %shard_map.149 = bf16[64,8,2432]{2,1,0:T(8,128)(2,1)} custom-call(bf16[512,256]{1,0:T(8,128)(2,1)} %get-tuple-element.106.xk_ref.refs_0_, bf16[512,256]{1,0:T(8,128)(2,1)} %copy-done.1, bf16[256,1536]{1,0:T(8,128)(2,1)} %get-tuple-element.104.dkv_ref.refs_2_, bf16[256,1536]{1,0:T(8,128)(2,1)S(1)} %collective-permute-done.12.refs_3_, ...), custom_call_target="tpu_custom_call" | custom-call | flops 330000000 | bytes 1080000 | tf_op jit(solution)/shard_map/pallas_call | solution.py:77
  118.6 1.6 all-to-all-done.3.rx_ref
  120.2 8.5 %all-to-all-start.4 = ((bf16[64,8,2432]{2,1,0:T(8,128)(2,1)}), bf16[64,8,2432]{2,1,0:T(8,128)(2,1)S(1)}, u32[]{:S(2)}, u32[]{:S(2)}) async-start(bf16[64,8,2432]{2,1,0:T(8,128)(2,1)} %shard_map.149), calls=%async_computation.4 | async-start | bytes 4980736 | tf_op jit(solution)/shard_map/all_to_all | solution.py:559
  129.1 0.7 copy.25
  130.5 4.2 %shard_map.147 = bf16[256,768]{1,0:T(8,128)(2,1)} custom-call(bf16[256,768]{1,0:T(8,128)(2,1)} %get-tuple-element.110.dq_ref, bf16[256,1536]{1,0:T(8,128)(2,1)} %get-tuple-element.104.dkv_ref.refs_2_, bf16[768,2304]{1,0:T(8,128)(2,1)} %w_ref.3, bf16[16,16,768]{2,1,0:T(8,128)(2,1)S(1)} %all-to-all-done.3.rx_ref), custom_call_target="tpu_custom_call" | custom-call | flops 4400000000 | bytes 14400000 | tf_op jit(solution)/shard_map/pallas_call | solution.py:77
  134.7 28.9 %all-to-all-done.4.rx_ref = bf16[64,8,2432]{2,1,0:T(8,128)(2,1)S(1)} async-done(((bf16[64,8,2432]{2,1,0:T(8,128)(2,1)}), bf16[64,8,2432]{2,1,0:T(8,128)(2,1)S(1)}, u32[]{:S(2)}, u32[]{:S(2)}) %all-to-all-start.4) | async-done | bytes 2490400 | tf_op jit(solution)/shard_map/all_to_all | solution.py:559
  163.6 1.0 shard_map.150
  (64 shorter events, 5.4 us)
Async XLA Ops:
  0.6 10.4 %copy-start.9 = (bf16[2,12,2,128]{3,2,1,0:T(2,128)(2,1)S(1)}, bf16[2,12,2,128]{3,2,1,0:T(2,128)(2,1)}, u32[]{:S(2)}) copy-start(bf16[2,12,2,128]{3,2,1,0:T(2,128)(2,1)} %param.14) | copy-start | bytes 36868
  2.7 8.3 %copy-start.10 = (s32[1024]{0:T(1024)S(1)}, s32[1024]{0:T(1024)}, u32[]{:S(2)}) copy-start(s32[1024]{0:T(1024)} %param.16) | copy-start | bytes 12292
  2.7 36.6 %all-to-all-start = ((bf16[16,32,768]{2,1,0:T(8,128)(2,1)}), bf16[16,32,768]{2,1,0:T(8,128)(2,1)S(1)}, u32[]{:S(2)}, u32[]{:S(2)}) async-start(bf16[16,32,768]{2,1,0:T(8,128)(2,1)} %shard_map.136), calls=%async_computation | async-start | bytes 1572864 | tf_op jit(solution)/shard_map/all_to_all | solution.py:559
  11.1 12.7 %copy-start.6 = (bf16[2,12,8,32]{3,2,1,0:T(8,128)(2,1)S(1)}, bf16[2,12,8,32]{3,2,1,0:T(8,128)(2,1)}, u32[]{:S(2)}) copy-start(bf16[2,12,8,32]{3,2,1,0:T(8,128)(2,1)} %param.15) | copy-start | bytes 36868
  11.1 13.1 %copy-start.12 = (s32[32]{0:T(128)S(1)}, s32[32]{0:T(128)}, u32[]{:S(2)}) copy-start(s32[32]{0:T(128)} %param.17) | copy-start | bytes 388
  15.8 12.0 %collective-permute-start = (bf16[784,128]{1,0:T(8,128)(2,1)}, bf16[784,128]{1,0:T(8,128)(2,1)S(1)}, u32[]{:S(2)}, u32[]{:S(2)}) collective-permute-start(bf16[784,128]{1,0:T(8,128)(2,1)} %get-tuple-element.66), channel_id=1, source_target_pairs={{0,1},{1,2},{2,3},{3,4},{4,5},{5,6},{6,7},{7,0},{8,9},{9,10},{10,1... | collective-permute-start | bytes 602120 | tf_op jit(solution)/shard_map/ppermute | solution.py:597
  17.4 18.3 %collective-permute-start.1 = (bf16[784,128]{1,0:T(8,128)(2,1)}, bf16[784,128]{1,0:T(8,128)(2,1)S(1)}, u32[]{:S(2)}, u32[]{:S(2)}) collective-permute-start(bf16[784,128]{1,0:T(8,128)(2,1)} %get-tuple-element.73), channel_id=1, source_target_pairs={{0,2},{1,3},{2,4},{3,5},{4,6},{5,7},{6,0},{7,1},{8,10},{9,11},{10,... | collective-permute-start | bytes 602120 | tf_op jit(solution)/shard_map/ppermute | solution.py:597
  20.1 16.4 %collective-permute-start.2 = (bf16[784,128]{1,0:T(8,128)(2,1)}, bf16[784,128]{1,0:T(8,128)(2,1)S(1)}, u32[]{:S(2)}, u32[]{:S(2)}) collective-permute-start(bf16[784,128]{1,0:T(8,128)(2,1)} %get-tuple-element.74), channel_id=1, source_target_pairs={{0,3},{1,4},{2,5},{3,6},{4,7},{5,0},{6,1},{7,2},{8,11},{9,12},{10,... | collective-permute-start | bytes 602120 | tf_op jit(solution)/shard_map/ppermute | solution.py:597
  21.7 17.1 %collective-permute-start.3 = (bf16[784,128]{1,0:T(8,128)(2,1)}, bf16[784,128]{1,0:T(8,128)(2,1)S(1)}, u32[]{:S(2)}, u32[]{:S(2)}) collective-permute-start(bf16[784,128]{1,0:T(8,128)(2,1)} %get-tuple-element.75), channel_id=1, source_target_pairs={{0,4},{1,5},{2,6},{3,7},{4,0},{5,1},{6,2},{7,3},{8,12},{9,13},{10,... | collective-permute-start | bytes 602120 | tf_op jit(solution)/shard_map/ppermute | solution.py:597
  23.0 15.7 %collective-permute-start.4 = (bf16[784,128]{1,0:T(8,128)(2,1)}, bf16[784,128]{1,0:T(8,128)(2,1)S(1)}, u32[]{:S(2)}, u32[]{:S(2)}) collective-permute-start(bf16[784,128]{1,0:T(8,128)(2,1)} %get-tuple-element.76), channel_id=1, source_target_pairs={{0,5},{1,6},{2,7},{3,0},{4,1},{5,2},{6,3},{7,4},{8,13},{9,14},{10,... | collective-permute-start | bytes 602120 | tf_op jit(solution)/shard_map/ppermute | solution.py:597
  27.9 17.3 %collective-permute-start.5 = (bf16[784,128]{1,0:T(8,128)(2,1)}, bf16[784,128]{1,0:T(8,128)(2,1)S(1)}, u32[]{:S(2)}, u32[]{:S(2)}) collective-permute-start(bf16[784,128]{1,0:T(8,128)(2,1)} %get-tuple-element.81), channel_id=1, source_target_pairs={{0,6},{1,7},{2,0},{3,1},{4,2},{5,3},{6,4},{7,5},{8,14},{9,15},{10,... | collective-permute-start | bytes 602120 | tf_op jit(solution)/shard_map/ppermute | solution.py:597
  30.7 5.0 %copy-start.13 = (bf16[784,128]{1,0:T(8,128)(2,1)S(1)}, bf16[784,128]{1,0:T(8,128)(2,1)}, u32[]{:S(2)}) copy-start(bf16[784,128]{1,0:T(8,128)(2,1)} %get-tuple-element.82) | copy-start | bytes 602116
  30.7 5.8 %copy-start.3 = (bf16[2,128,768]{2,1,0:T(8,128)(2,1)S(1)}, bf16[2,128,768]{2,1,0:T(8,128)(2,1)}, u32[]{:S(2)}) copy-start(bf16[2,128,768]{2,1,0:T(8,128)(2,1)} %g_ref.1) | copy-start | bytes 1179652
  35.8 9.4 %collective-permute-start.6 = (bf16[784,128]{1,0:T(8,128)(2,1)S(1)}, bf16[784,128]{1,0:T(8,128)(2,1)S(1)}, u32[]{:S(2)}, u32[]{:S(2)}) collective-permute-start(bf16[784,128]{1,0:T(8,128)(2,1)S(1)} %copy-done.13), channel_id=1, source_target_pairs={{0,7},{1,0},{2,1},{3,2},{4,3},{5,4},{6,5},{7,6},{8,15},{9,8},{10,9... | collective-permute-start | bytes 602120 | tf_op jit(solution)/shard_map/ppermute | solution.py:597
  36.5 24.2 %collective-permute-start.8 = (bf16[256,768]{1,0:T(8,128)(2,1)S(1)}, bf16[256,768]{1,0:T(8,128)(2,1)S(1)}, u32[]{:S(2)}, u32[]{:S(2)}) collective-permute-start(bf16[256,768]{1,0:T(8,128)(2,1)S(1)} %bitcast.29), channel_id=1, source_target_pairs={{0,8},{8,0},{16,24},{24,16},{32,40},{40,32},{48,56},{56,48},{64,72... | collective-permute-start | bytes 1179656 | tf_op jit(solution)/shard_map/ppermute | solution.py:563
  39.3 5.8 %copy-start = (bf16[16,32,768]{2,1,0:T(8,128)(2,1)}, bf16[16,32,768]{2,1,0:T(8,128)(2,1)S(1)}, u32[]{:S(2)}) copy-start(bf16[16,32,768]{2,1,0:T(8,128)(2,1)S(1)} %all-to-all-done.refs_0_.rx_ref) | copy-start | bytes 2359300
  48.8 22.2 %all-to-all-start.1 = ((bf16[16,32,768]{2,1,0:T(8,128)(2,1)}), bf16[16,32,768]{2,1,0:T(8,128)(2,1)S(1)}, u32[]{:S(2)}, u32[]{:S(2)}) async-start(bf16[16,32,768]{2,1,0:T(8,128)(2,1)} %get-tuple-element.83), calls=%async_computation.1 | async-start | bytes 1572864 | tf_op jit(solution)/shard_map/all_to_all | solution.py:559
  60.2 1.8 %collective-permute-start.7 = (bf16[512,256]{1,0:T(8,128)(2,1)}, bf16[512,256]{1,0:T(8,128)(2,1)S(1)}, u32[]{:S(2)}, u32[]{:S(2)}) collective-permute-start(bf16[512,256]{1,0:T(8,128)(2,1)} %get-tuple-element.86), channel_id=1, source_target_pairs={{0,8},{8,0},{16,24},{24,16},{32,40},{40,32},{48,56},{56,48},{64,72... | collective-permute-start | bytes 786440 | tf_op jit(solution)/shard_map/ppermute | solution.py:563
  60.6 1.9 %collective-permute-start.9 = (bf16[512,256]{1,0:T(8,128)(2,1)}, bf16[512,256]{1,0:T(8,128)(2,1)}, u32[]{:S(2)}, u32[]{:S(2)}) collective-permute-start(bf16[512,256]{1,0:T(8,128)(2,1)} %get-tuple-element.87), channel_id=1, source_target_pairs={{0,8},{8,0},{16,24},{24,16},{32,40},{40,32},{48,56},{56,48},{64,72... | collective-permute-start | bytes 786440 | tf_op jit(solution)/shard_map/ppermute | solution.py:563
  60.7 14.4 %copy-start.4 = (bf16[256,768]{1,0:T(8,128)(2,1)}, bf16[256,768]{1,0:T(8,128)(2,1)S(1)}, u32[]{:S(2)}) copy-start(bf16[256,768]{1,0:T(8,128)(2,1)S(1)} %collective-permute-done.8.gr_ref) | copy-start | bytes 1179652
  62.0 13.2 %copy-start.1 = (bf16[512,256]{1,0:T(8,128)(2,1)}, bf16[512,256]{1,0:T(8,128)(2,1)S(1)}, u32[]{:S(2)}) copy-start(bf16[512,256]{1,0:T(8,128)(2,1)S(1)} %collective-permute-done.7.xr_ref.refs_1_) | copy-start | bytes 786436
  75.1 26.0 %all-to-all-start.2 = ((bf16[8,784,128]{2,1,0:T(8,128)(2,1)}), bf16[8,784,128]{2,1,0:T(8,128)(2,1)S(1)}, u32[]{:S(2)}, u32[]{:S(2)}) async-start(bf16[8,784,128]{2,1,0:T(8,128)(2,1)} %get-tuple-element.94), calls=%async_computation.2 | async-start | bytes 3211264 | tf_op jit(solution)/shard_map/all_to_all | solution.py:559
  88.2 10.1 %collective-permute-start.10 = (bf16[896,256]{1,0:T(8,128)(2,1)}, bf16[896,256]{1,0:T(8,128)(2,1)S(1)}, u32[]{:S(2)}, u32[]{:S(2)}) collective-permute-start(bf16[896,256]{1,0:T(8,128)(2,1)} %get-tuple-element.95), channel_id=1, source_target_pairs={{0,8},{8,0},{16,24},{24,16},{32,40},{40,32},{48,56},{56,48},{64,72... | collective-permute-start | bytes 1376264 | tf_op jit(solution)/shard_map/ppermute | solution.py:563
  88.2 10.1 %collective-permute-start.11 = (bf16[256,768]{1,0:T(8,128)(2,1)}, bf16[256,768]{1,0:T(8,128)(2,1)S(1)}, u32[]{:S(2)}, u32[]{:S(2)}) collective-permute-start(bf16[256,768]{1,0:T(8,128)(2,1)} %get-tuple-element.110.dq_ref), channel_id=1, source_target_pairs={{0,8},{8,0},{16,24},{24,16},{32,40},{40,32},{48,56},{56,48},{64,72... | collective-permute-start | bytes 1179656 | tf_op jit(solution)/shard_map/ppermute | solution.py:563
  97.9 11.4 %collective-permute-start.13 = (bf16[256,2304]{1,0:T(8,128)(2,1)}, bf16[256,2304]{1,0:T(8,128)(2,1)}, u32[]{:S(2)}, u32[]{:S(2)}) collective-permute-start(bf16[256,2304]{1,0:T(8,128)(2,1)} %get-tuple-element.112.dc_ref), channel_id=1, source_target_pairs={{0,8},{8,0},{16,24},{24,16},{32,40},{40,32},{48,56},{56,48},{64,72... | collective-permute-start | bytes 3538952 | tf_op jit(solution)/shard_map/ppermute | solution.py:563
  98.2 7.2 %copy-start.5 = (bf16[256,768]{1,0:T(8,128)(2,1)}, bf16[256,768]{1,0:T(8,128)(2,1)S(1)}, u32[]{:S(2)}) copy-start(bf16[256,768]{1,0:T(8,128)(2,1)S(1)} %collective-permute-done.11.dqr_ref) | copy-start | bytes 1179652
  98.2 7.2 %copy-start.2 = (bf16[896,256]{1,0:T(8,128)(2,1)}, bf16[896,256]{1,0:T(8,128)(2,1)S(1)}, u32[]{:S(2)}) copy-start(bf16[896,256]{1,0:T(8,128)(2,1)S(1)} %collective-permute-done.10.nr_ref) | copy-start | bytes 1376260
  105.4 9.4 %collective-permute-start.12 = (bf16[256,1536]{1,0:T(8,128)(2,1)}, bf16[256,1536]{1,0:T(8,128)(2,1)S(1)}, u32[]{:S(2)}, u32[]{:S(2)}) collective-permute-start(bf16[256,1536]{1,0:T(8,128)(2,1)} %get-tuple-element.104.dkv_ref.refs_2_), channel_id=1, source_target_pairs={{0,8},{8,0},{16,24},{24,16},{32,40},{40,32},{48,56},{56,48},{64,72... | collective-permute-start | bytes 2359304 | tf_op jit(solution)/shard_map/ppermute | solution.py:563
  105.5 14.7 %all-to-all-start.3 = ((bf16[16,16,768]{2,1,0:T(8,128)(2,1)}), bf16[16,16,768]{2,1,0:T(8,128)(2,1)S(1)}, u32[]{:S(2)}, u32[]{:S(2)}) async-start(bf16[16,16,768]{2,1,0:T(8,128)(2,1)} %bitcast.7), calls=%async_computation.3 | async-start | bytes 786432 | tf_op jit(solution)/shard_map/all_to_all | solution.py:559
  118.6 10.2 %copy-start.7 = (f32[2,12,256]{2,1,0:T(8,128)S(1)}, f32[2,12,256]{2,1,0:T(8,128)}, u32[]{:S(2)}) copy-start(f32[2,12,256]{2,1,0:T(8,128)} %get-tuple-element.121) | copy-start | bytes 73732
  118.6 11.3 %copy-start.8 = (f32[2,24,128]{2,1,0:T(8,128)S(1)}, f32[2,24,128]{2,1,0:T(8,128)}, u32[]{:S(2)}) copy-start(f32[2,24,128]{2,1,0:T(8,128)} %get-tuple-element.120) | copy-start | bytes 73732
  120.2 43.3 %all-to-all-start.4 = ((bf16[64,8,2432]{2,1,0:T(8,128)(2,1)}), bf16[64,8,2432]{2,1,0:T(8,128)(2,1)S(1)}, u32[]{:S(2)}, u32[]{:S(2)}) async-start(bf16[64,8,2432]{2,1,0:T(8,128)(2,1)} %shard_map.149), calls=%async_computation.4 | async-start | bytes 4980736 | tf_op jit(solution)/shard_map/all_to_all | solution.py:559
  (1 other events, 4.8 us)

commit v5 on v4

--- a/solution.py
+++ b/solution.py
@@ -609,7 +609,7 @@
     qkv_c, col_out, probs_c = call(
         col_forward_kernel, 6.8,
         [((TOK, F), BF), ((TOK, D), BF), ((PAIRS, 2 * TOK, TOK), BF)],
-        after(rx, *states[:5]), w_qkv, wc, near=(0,), staged=True,
+        after(rx, states[0], states[1]), w_qkv, wc, near=(0,), staged=True,
     )
     row_out, out_swap, entering = call(
         row_join_kernel, 5.0,

time: 165 us -> 163 us (0.988)
  starting transfers between devices: 45.1 us -> 42.4 us
    all_to_all x5, starting transfers between devices: 32.2 us -> 29.5 us  [exchange(): return lax.all_to_all(x, axis, 0, 0, tiled=True, axis_index_groups=groups)]
    all_to_all x5, waiting for transfers between devices: 42.5 us -> 45.1 us  [exchange(): return lax.all_to_all(x, axis, 0, 0, tiled=True, axis_index_groups=groups)]
    ppermute x7, waiting for transfers between devices: 2.26 us -> 0.02 us  [per_device(): lax.ppermute(u, 'col', [(i, (i + n + 1) % 8) for i in range(8)])]
  transfers between devices with their start and end apart: 19 -> 19, of which waited for: 8 -> 7; matrix products, arithmetic and copies ran while one was open for 1% -> 1% of each run, Pallas kernels for 38% -> 38%
where the time goes in v5:
time: 163 us; the launch traced here: 162 us
  Pallas kernels  69.6 us (43%)
  waiting for transfers between devices  46.8 us (29%)
  starting transfers between devices  42.4 us (26%)
  local copies, waits for them, and re-layouts  2.27 us (1%)
    pallas_call x15, Pallas kernels, call(): pl.pallas_call(kernel, out_shape=[(pltpu.VMEM if n in keep else pltpu.HBM...  69.6 us
    all_to_all x5, waiting for transfers between devices, exchange(): return lax.all_to_all(x, axis, 0, 0, tiled=True, axis_index_groups=groups)  45.1 us
    all_to_all x5, starting transfers between devices, exchange(): return lax.all_to_all(x, axis, 0, 0, tiled=True, axis_index_groups=groups)  29.5 us
    ppermute x7, starting transfers between devices, per_device(): lax.ppermute(u, 'col', [(i, (i + n + 1) % 8) for i in range(8)])  11.5 us
  transfers between devices with their start and end apart: 19, of which 7 were waited for; matrix products, arithmetic and copies ran while one was open for 1% of the time, Pallas kernels for 38%

profile of v5, /device:TPU:0, one launch (start us, length us, event | category | flops | bytes accessed | tf_op | source)
XLA Modules:
  0.0 162.2 jit_solution(6351095578940705678)
XLA Ops:
  0.6 2.1 %shard_map.136 = bf16[16,32,768]{2,1,0:T(8,128)(2,1)} custom-call(bf16[2,128,768]{2,1,0:T(8,128)(2,1)} %x_ref.1, bf16[2,128,768]{2,1,0:T(8,128)(2,1)} %g_ref.1), custom_call_target="tpu_custom_call" | custom-call | flops 2200000000 | bytes 7200000 | tf_op jit(solution)/shard_map/pallas_call | solution.py:77
  2.7 8.3 %all-to-all-start = ((bf16[16,32,768]{2,1,0:T(8,128)(2,1)}), bf16[16,32,768]{2,1,0:T(8,128)(2,1)S(1)}, u32[]{:S(2)}, u32[]{:S(2)}) async-start(bf16[16,32,768]{2,1,0:T(8,128)(2,1)} %shard_map.136), calls=%async_computation | async-start | bytes 1572864 | tf_op jit(solution)/shard_map/all_to_all | solution.py:559
  11.1 4.8 %shard_map.137 = (f32[2,128,48]{2,1,0:T(8,128)}, f32[2,16,128]{2,1,0:T(8,128)}, bf16[256,1536]{1,0:T(8,128)(2,1)}, bf16[784,128]{1,0:T(8,128)(2,1)}, bf16[784,12...) custom-call(s32[1]{0:T(128)} %bitcast.1.refs_0_.place_ref, ...), custom_call_target="tpu_custom_call" | custom-call | flops 110000000 | bytes 360000 | tf_op jit(solution)/shard_map/pallas_call | solution.py:77
  15.8 1.6 collective-permute-start
  17.4 2.7 %collective-permute-start.1 = (bf16[784,128]{1,0:T(8,128)(2,1)}, bf16[784,128]{1,0:T(8,128)(2,1)S(1)}, u32[]{:S(2)}, u32[]{:S(2)}) collective-permute-start(bf16[784,128]{1,0:T(8,128)(2,1)} %get-tuple-element.73), channel_id=1, source_target_pairs={{0,2},{1,3},{2,4},{3,5},{4,6},{5,7},{6,0},{7,1},{8,10},{9,11},{10,... | collective-permute-start | bytes 602120 | tf_op jit(solution)/shard_map/ppermute | solution.py:597
  20.1 1.6 collective-permute-start.2
  21.7 1.3 collective-permute-start.3
  24.3 3.5 %shard_map.138 = (bf16[12,256,128]{2,1,0:T(8,128)(2,1)}, bf16[6,512,256]{2,1,0:T(8,128)(2,1)}) custom-call(bf16[2,2,12,128]{3,2,1,0:T(8,128)(2,1)S(1)} %bitcast.22, bf16[2,12,256]{2,1,0:T(8,128)(2,1)S(1)} %reshape.63.refs_1_, s32[2,128]{1,0:T(2,128)S(1)} %constant_dynamic-slice_fusion.refs_2_, s32[1,256]{1,0:T(1,128)S(1)} %reshape.56.refs_3_, ...), custom_call_target="tpu_custom_call" | custom-call | flops 110000000 | bytes 360000 | tf_op jit(solution)/shard_map/pallas_call | solution.py:77
  27.8 2.8 %collective-permute-start.5 = (bf16[784,128]{1,0:T(8,128)(2,1)}, bf16[784,128]{1,0:T(8,128)(2,1)S(1)}, u32[]{:S(2)}, u32[]{:S(2)}) collective-permute-start(bf16[784,128]{1,0:T(8,128)(2,1)} %get-tuple-element.81), channel_id=1, source_target_pairs={{0,6},{1,7},{2,0},{3,1},{4,2},{5,3},{6,4},{7,5},{8,14},{9,15},{10,... | collective-permute-start | bytes 602120 | tf_op jit(solution)/shard_map/ppermute | solution.py:597
  30.7 5.0 %shard_map.139 = (bf16[256,768]{1,0:T(8,128)(2,1)}, f32[256,768]{1,0:T(8,128)}, bf16[12,256,128]{2,1,0:T(8,128)(2,1)}) custom-call(bf16[256,768]{1,0:T(8,128)(2,1)} %bitcast.24, bf16[768,2304]{1,0:T(8,128)(2,1)} %w_ref.3, bf16[256,1536]{1,0:T(8,128)(2,1)} %get-tuple-element.67.refs_2_.kv_ref.refs_1_, bf16[12,256,128]{2,1,0:T(8,128)(2,1)} %get-tuple-element.69.refs_3_.wr_ref), custom_call_target="tpu_custom_call" | custom-call | flops 110000000 | bytes 360000 | tf_op jit(solution)/shard_map/pallas_call | solution.py:77
  36.5 2.8 %all-to-all-done.refs_0_.rx_ref = bf16[16,32,768]{2,1,0:T(8,128)(2,1)S(1)} async-done(((bf16[16,32,768]{2,1,0:T(8,128)(2,1)}), bf16[16,32,768]{2,1,0:T(8,128)(2,1)S(1)}, u32[]{:S(2)}, u32[]{:S(2)}) %all-to-all-start) | async-done | bytes 786464 | tf_op jit(solution)/shard_map/all_to_all | solution.py:559
  39.3 5.9 %shard_map.140 = (bf16[256,2304]{1,0:T(8,128)(2,1)}, bf16[256,768]{1,0:T(8,128)(2,1)}, bf16[6,512,256]{2,1,0:T(8,128)(2,1)}) custom-call(bf16[16,32,768]{2,1,0:T(8,128)(2,1)S(1)} %all-to-all-done.refs_0_.rx_ref, bf16[768,2304]{1,0:T(8,128)(2,1)} %w_ref.3, bf16[6,512,256]{2,1,0:T(8,128)(2,1)} %get-tuple-element.75.refs_2_.wc_ref), custom_call_target="tpu_custom_call" | custom-call | flops 7480000000 | bytes 24480000 | tf_op jit(solution)/shard_map/pallas_call | solution.py:77
  45.3 3.6 %shard_map.141 = (bf16[256,768]{1,0:T(8,128)(2,1)}, bf16[16,32,768]{2,1,0:T(8,128)(2,1)}, bf16[2,768,128]{2,1,0:T(8,128)(2,1)}) custom-call(s32[1]{0:T(128)} %bitcast.1.refs_0_.place_ref, bf16[256,768]{1,0:T(8,128)(2,1)} %get-tuple-element.70.refs_1_.q_ref, f32[2,128,48]{2,1,0:T(8,128)} %get-tuple-element.71.refs_2_.fac_ref.refs_4_, ...), custom_call_target="tpu_custom_call" | custom-call | flops 5500000256 | bytes 18000000 | tf_op jit(solution)/shard_map/pallas_call | solution.py:77
  48.9 5.1 %all-to-all-start.1 = ((bf16[16,32,768]{2,1,0:T(8,128)(2,1)}), bf16[16,32,768]{2,1,0:T(8,128)(2,1)S(1)}, u32[]{:S(2)}, u32[]{:S(2)}) async-start(bf16[16,32,768]{2,1,0:T(8,128)(2,1)} %get-tuple-element.83), calls=%async_computation.1 | async-start | bytes 1572864 | tf_op jit(solution)/shard_map/all_to_all | solution.py:559
  54.0 4.3 %shard_map.142 = (bf16[256,768]{1,0:T(8,128)(2,1)}, bf16[256,768]{1,0:T(8,128)(2,1)}, bf16[512,256]{1,0:T(8,128)(2,1)}, bf16[512,256]{1,0:T(8,128)(2,1)}, bf16[5...) custom-call(s32[1]{0:T(128)} %bitcast.core_ref, bf16[256,768]{1,0:T(8,128)(2,1)} %bitcast.25, bf16[256,768]{1,0:T(8,128)(2,1)} %bitcast.27, ...), custom_call_target="tpu_custom_call" | custom-call | flops 5500000256 | bytes 18000000 | tf_op jit(solution)/shard_map/pallas_call | solution.py:77
  58.8 1.2 collective-permute-done.7.xr_ref.refs_1_
  60.5 8.7 %all-to-all-done.1.rx_ref = bf16[16,32,768]{2,1,0:T(8,128)(2,1)S(1)} async-done(((bf16[16,32,768]{2,1,0:T(8,128)(2,1)}), bf16[16,32,768]{2,1,0:T(8,128)(2,1)S(1)}, u32[]{:S(2)}, u32[]{:S(2)}) %all-to-all-start.1) | async-done | bytes 786464 | tf_op jit(solution)/shard_map/all_to_all | solution.py:559
  69.2 4.1 %shard_map.143 = (bf16[256,768]{1,0:T(8,128)(2,1)}, bf16[8,784,128]{2,1,0:T(8,128)(2,1)}) custom-call(s32[1]{0:T(128)} %bitcast.1.refs_0_.place_ref, bf16[16,32,768]{2,1,0:T(8,128)(2,1)S(1)} %all-to-all-done.1.rx_ref, bf16[256,768]{1,0:T(8,128)(2,1)} %get-tuple-element.89.row_ref, bf16[256,768]{1,0:T(8,128)(2,1)} %get-tuple-element.90.dn_ref, ...), custom_call_target="tpu_custom_call" | custom-call | flops 4950000128 | bytes 16200000 | tf_op jit(solution)/shard_map/pallas_call | solution.py:77
  73.3 3.6 %all-to-all-start.2 = ((bf16[8,784,128]{2,1,0:T(8,128)(2,1)}), bf16[8,784,128]{2,1,0:T(8,128)(2,1)S(1)}, u32[]{:S(2)}, u32[]{:S(2)}) async-start(bf16[8,784,128]{2,1,0:T(8,128)(2,1)} %get-tuple-element.94), calls=%async_computation.2 | async-start | bytes 3211264 | tf_op jit(solution)/shard_map/all_to_all | solution.py:559
  76.9 8.4 %shard_map.144 = (bf16[256,768]{1,0:T(8,128)(2,1)}, bf16[256,1536]{1,0:T(8,128)(2,1)}, f32[2,24,128]{2,1,0:T(8,128)}, bf16[896,256]{1,0:T(8,128)(2,1)}, bf16[896,256]{1,0:T(8,128)(2,1)}) custom-call(s32[1]{0:T(128)} %bitcast.core_ref, bf16[16,32,768]{2,1,0:T(8,128)(2,1)S(1)} %all-to-all-done.1.rx_ref, bf16[256,768]{1,0:T(8,128)(2,1)} %get-tuple-element.89.row_ref, ...), custom_call_target="tpu_custom_call" | custom-call | flops 9790000128 | bytes 32040000 | tf_op jit(solution)/shard_map/pallas_call | solution.py:77
  85.8 9.3 %shard_map.145 = (bf16[256,2304]{1,0:T(8,128)(2,1)}, f32[2,12,256]{2,1,0:T(8,128)}, bf16[256,768]{1,0:T(8,128)(2,1)}) custom-call(bf16[16,32,768]{2,1,0:T(8,128)(2,1)S(1)} %all-to-all-done.1.rx_ref, bf16[256,768]{1,0:T(8,128)(2,1)} %get-tuple-element.77.refs_4_.col_ref, bf16[256,768]{1,0:T(8,128)(2,1)} %get-tuple-element.97.dn_ref, ...), custom_call_target="tpu_custom_call" | custom-call | flops 10670000128 | bytes 34920000 | tf_op jit(solution)/shard_map/pallas_call | solution.py:77
  95.4 3.2 %all-to-all-done.2.refs_3_ = bf16[8,784,128]{2,1,0:T(8,128)(2,1)S(1)} async-done(((bf16[8,784,128]{2,1,0:T(8,128)(2,1)}), bf16[8,784,128]{2,1,0:T(8,128)(2,1)S(1)}, u32[]{:S(2)}, u32[]{:S(2)}) %all-to-all-start.2) | async-done | bytes 1605664 | tf_op jit(solution)/shard_map/all_to_all | solution.py:559
  98.6 4.2 %shard_map.146 = (bf16[256,1536]{1,0:T(8,128)(2,1)}, f32[2,24,128]{2,1,0:T(8,128)}) custom-call(s32[1]{0:T(128)} %bitcast.1.refs_0_.place_ref, bf16[256,1536]{1,0:T(8,128)(2,1)} %get-tuple-element.67.refs_2_.kv_ref.refs_1_, bf16[2,768,128]{2,1,0:T(8,128)(2,1)} %get-tuple-element.84.s_ref.refs_2_, bf16[8,784,128]{2,1,0:T(8,128)(2,1)S(1)} %all-to-all-done.2.refs_3_, ...), custom_call_target="tpu_custom_call" | custom-call | flops 330000000 | bytes 1080000 | tf_op jit(solution)/shard_map/pallas_call | solution.py:77
  102.9 3.6 %all-to-all-start.3 = ((bf16[16,16,768]{2,1,0:T(8,128)(2,1)}), bf16[16,16,768]{2,1,0:T(8,128)(2,1)S(1)}, u32[]{:S(2)}, u32[]{:S(2)}) async-start(bf16[16,16,768]{2,1,0:T(8,128)(2,1)} %bitcast.7), calls=%async_computation.3 | async-start | bytes 786432 | tf_op jit(solution)/shard_map/all_to_all | solution.py:559
  106.5 5.5 %shard_map.148.refs_4_ = bf16[512,2432]{1,0:T(8,128)(2,1)S(1)} custom-call(bf16[512,256]{1,0:T(8,128)(2,1)} %get-tuple-element.106.xk_ref.refs_0_, bf16[512,256]{1,0:T(8,128)(2,1)} %copy-done.1, bf16[512,256]{1,0:T(8,128)(2,1)} %get-tuple-element.108.xck_ref, bf16[512,256]{1,0:T(8,128)(2,1)} %copy-done.6, bf16[256,768]{1,0:T(8,128)(2,1)} %get-tuple-element.110.dq_ref, ...), custom_call_target="tpu_custom_call" | custom-call | flops 330000000 | bytes 1080000 | tf_op jit(solution)/shard_map/pallas_call | solution.py:77
  112.0 3.7 %shard_map.149 = bf16[64,8,2432]{2,1,0:T(8,128)(2,1)} custom-call(bf16[512,256]{1,0:T(8,128)(2,1)} %get-tuple-element.106.xk_ref.refs_0_, bf16[512,256]{1,0:T(8,128)(2,1)} %copy-done.1, bf16[256,1536]{1,0:T(8,128)(2,1)} %get-tuple-element.104.dkv_ref.refs_2_, bf16[256,1536]{1,0:T(8,128)(2,1)S(1)} %collective-permute-done.12.refs_3_, ...), custom_call_target="tpu_custom_call" | custom-call | flops 330000000 | bytes 1080000 | tf_op jit(solution)/shard_map/pallas_call | solution.py:77
  115.8 1.6 all-to-all-done.3.rx_ref
  117.4 8.9 %all-to-all-start.4 = ((bf16[64,8,2432]{2,1,0:T(8,128)(2,1)}), bf16[64,8,2432]{2,1,0:T(8,128)(2,1)S(1)}, u32[]{:S(2)}, u32[]{:S(2)}) async-start(bf16[64,8,2432]{2,1,0:T(8,128)(2,1)} %shard_map.149), calls=%async_computation.4 | async-start | bytes 4980736 | tf_op jit(solution)/shard_map/all_to_all | solution.py:559
  126.7 0.7 copy.25
  128.0 4.2 %shard_map.147 = bf16[256,768]{1,0:T(8,128)(2,1)} custom-call(bf16[256,768]{1,0:T(8,128)(2,1)} %get-tuple-element.110.dq_ref, bf16[256,1536]{1,0:T(8,128)(2,1)} %get-tuple-element.104.dkv_ref.refs_2_, bf16[768,2304]{1,0:T(8,128)(2,1)} %w_ref.3, bf16[16,16,768]{2,1,0:T(8,128)(2,1)S(1)} %all-to-all-done.3.rx_ref), custom_call_target="tpu_custom_call" | custom-call | flops 4400000000 | bytes 14400000 | tf_op jit(solution)/shard_map/pallas_call | solution.py:77
  132.3 28.9 %all-to-all-done.4.rx_ref = bf16[64,8,2432]{2,1,0:T(8,128)(2,1)S(1)} async-done(((bf16[64,8,2432]{2,1,0:T(8,128)(2,1)}), bf16[64,8,2432]{2,1,0:T(8,128)(2,1)S(1)}, u32[]{:S(2)}, u32[]{:S(2)}) %all-to-all-start.4) | async-done | bytes 2490400 | tf_op jit(solution)/shard_map/all_to_all | solution.py:559
  161.1 1.0 shard_map.150
  (66 shorter events, 4.9 us)
Async XLA Ops:
  0.6 10.4 %copy-start.10 = (bf16[2,12,2,128]{3,2,1,0:T(2,128)(2,1)S(1)}, bf16[2,12,2,128]{3,2,1,0:T(2,128)(2,1)}, u32[]{:S(2)}) copy-start(bf16[2,12,2,128]{3,2,1,0:T(2,128)(2,1)} %param.14) | copy-start | bytes 36868
  2.7 8.3 %copy-start.11 = (s32[1024]{0:T(1024)S(1)}, s32[1024]{0:T(1024)}, u32[]{:S(2)}) copy-start(s32[1024]{0:T(1024)} %param.16) | copy-start | bytes 12292
  2.7 36.6 %all-to-all-start = ((bf16[16,32,768]{2,1,0:T(8,128)(2,1)}), bf16[16,32,768]{2,1,0:T(8,128)(2,1)S(1)}, u32[]{:S(2)}, u32[]{:S(2)}) async-start(bf16[16,32,768]{2,1,0:T(8,128)(2,1)} %shard_map.136), calls=%async_computation | async-start | bytes 1572864 | tf_op jit(solution)/shard_map/all_to_all | solution.py:559
  11.1 12.7 %copy-start.7 = (bf16[2,12,8,32]{3,2,1,0:T(8,128)(2,1)S(1)}, bf16[2,12,8,32]{3,2,1,0:T(8,128)(2,1)}, u32[]{:S(2)}) copy-start(bf16[2,12,8,32]{3,2,1,0:T(8,128)(2,1)} %param.15) | copy-start | bytes 36868
  11.1 13.1 %copy-start.13 = (s32[32]{0:T(128)S(1)}, s32[32]{0:T(128)}, u32[]{:S(2)}) copy-start(s32[32]{0:T(128)} %param.17) | copy-start | bytes 388
  15.8 12.0 %collective-permute-start = (bf16[784,128]{1,0:T(8,128)(2,1)}, bf16[784,128]{1,0:T(8,128)(2,1)S(1)}, u32[]{:S(2)}, u32[]{:S(2)}) collective-permute-start(bf16[784,128]{1,0:T(8,128)(2,1)} %get-tuple-element.66), channel_id=1, source_target_pairs={{0,1},{1,2},{2,3},{3,4},{4,5},{5,6},{6,7},{7,0},{8,9},{9,10},{10,1... | collective-permute-start | bytes 602120 | tf_op jit(solution)/shard_map/ppermute | solution.py:597
  17.4 18.3 %collective-permute-start.1 = (bf16[784,128]{1,0:T(8,128)(2,1)}, bf16[784,128]{1,0:T(8,128)(2,1)S(1)}, u32[]{:S(2)}, u32[]{:S(2)}) collective-permute-start(bf16[784,128]{1,0:T(8,128)(2,1)} %get-tuple-element.73), channel_id=1, source_target_pairs={{0,2},{1,3},{2,4},{3,5},{4,6},{5,7},{6,0},{7,1},{8,10},{9,11},{10,... | collective-permute-start | bytes 602120 | tf_op jit(solution)/shard_map/ppermute | solution.py:597
  20.1 25.0 %collective-permute-start.2 = (bf16[784,128]{1,0:T(8,128)(2,1)}, bf16[784,128]{1,0:T(8,128)(2,1)S(1)}, u32[]{:S(2)}, u32[]{:S(2)}) collective-permute-start(bf16[784,128]{1,0:T(8,128)(2,1)} %get-tuple-element.78), channel_id=1, source_target_pairs={{0,3},{1,4},{2,5},{3,6},{4,7},{5,0},{6,1},{7,2},{8,11},{9,12},{10,... | collective-permute-start | bytes 602120 | tf_op jit(solution)/shard_map/ppermute | solution.py:597
  21.7 23.6 %collective-permute-start.3 = (bf16[784,128]{1,0:T(8,128)(2,1)}, bf16[784,128]{1,0:T(8,128)(2,1)S(1)}, u32[]{:S(2)}, u32[]{:S(2)}) collective-permute-start(bf16[784,128]{1,0:T(8,128)(2,1)} %get-tuple-element.79), channel_id=1, source_target_pairs={{0,4},{1,5},{2,6},{3,7},{4,0},{5,1},{6,2},{7,3},{8,12},{9,13},{10,... | collective-permute-start | bytes 602120 | tf_op jit(solution)/shard_map/ppermute | solution.py:597
  23.0 22.3 %collective-permute-start.4 = (bf16[784,128]{1,0:T(8,128)(2,1)}, bf16[784,128]{1,0:T(8,128)(2,1)S(1)}, u32[]{:S(2)}, u32[]{:S(2)}) collective-permute-start(bf16[784,128]{1,0:T(8,128)(2,1)} %get-tuple-element.80), channel_id=1, source_target_pairs={{0,5},{1,6},{2,7},{3,0},{4,1},{5,2},{6,3},{7,4},{8,13},{9,14},{10,... | collective-permute-start | bytes 602120 | tf_op jit(solution)/shard_map/ppermute | solution.py:597
  27.8 17.5 %collective-permute-start.5 = (bf16[784,128]{1,0:T(8,128)(2,1)}, bf16[784,128]{1,0:T(8,128)(2,1)S(1)}, u32[]{:S(2)}, u32[]{:S(2)}) collective-permute-start(bf16[784,128]{1,0:T(8,128)(2,1)} %get-tuple-element.81), channel_id=1, source_target_pairs={{0,6},{1,7},{2,0},{3,1},{4,2},{5,3},{6,4},{7,5},{8,14},{9,15},{10,... | collective-permute-start | bytes 602120 | tf_op jit(solution)/shard_map/ppermute | solution.py:597
  35.7 9.6 %collective-permute-start.6 = (bf16[784,128]{1,0:T(8,128)(2,1)S(1)}, bf16[784,128]{1,0:T(8,128)(2,1)S(1)}, u32[]{:S(2)}, u32[]{:S(2)}) collective-permute-start(bf16[784,128]{1,0:T(8,128)(2,1)S(1)} %copy-done.14), channel_id=1, source_target_pairs={{0,7},{1,0},{2,1},{3,2},{4,3},{5,4},{6,5},{7,6},{8,15},{9,8},{10,9... | collective-permute-start | bytes 602120 | tf_op jit(solution)/shard_map/ppermute | solution.py:597
  39.3 5.9 %copy-start = (bf16[16,32,768]{2,1,0:T(8,128)(2,1)}, bf16[16,32,768]{2,1,0:T(8,128)(2,1)S(1)}, u32[]{:S(2)}) copy-start(bf16[16,32,768]{2,1,0:T(8,128)(2,1)S(1)} %all-to-all-done.refs_0_.rx_ref) | copy-start | bytes 2359300
  39.3 5.9 %copy-start.3 = (bf16[2,128,768]{2,1,0:T(8,128)(2,1)S(1)}, bf16[2,128,768]{2,1,0:T(8,128)(2,1)}, u32[]{:S(2)}) copy-start(bf16[2,128,768]{2,1,0:T(8,128)(2,1)} %g_ref.1) | copy-start | bytes 1179652
  45.2 13.6 %collective-permute-start.8 = (bf16[256,768]{1,0:T(8,128)(2,1)S(1)}, bf16[256,768]{1,0:T(8,128)(2,1)S(1)}, u32[]{:S(2)}, u32[]{:S(2)}) collective-permute-start(bf16[256,768]{1,0:T(8,128)(2,1)S(1)} %bitcast.29), channel_id=1, source_target_pairs={{0,8},{8,0},{16,24},{24,16},{32,40},{40,32},{48,56},{56,48},{64,72... | collective-permute-start | bytes 1179656 | tf_op jit(solution)/shard_map/ppermute | solution.py:563
  48.9 20.3 %all-to-all-start.1 = ((bf16[16,32,768]{2,1,0:T(8,128)(2,1)}), bf16[16,32,768]{2,1,0:T(8,128)(2,1)S(1)}, u32[]{:S(2)}, u32[]{:S(2)}) async-start(bf16[16,32,768]{2,1,0:T(8,128)(2,1)} %get-tuple-element.83), calls=%async_computation.1 | async-start | bytes 1572864 | tf_op jit(solution)/shard_map/all_to_all | solution.py:559
  58.3 1.8 %collective-permute-start.7 = (bf16[512,256]{1,0:T(8,128)(2,1)}, bf16[512,256]{1,0:T(8,128)(2,1)S(1)}, u32[]{:S(2)}, u32[]{:S(2)}) collective-permute-start(bf16[512,256]{1,0:T(8,128)(2,1)} %get-tuple-element.86), channel_id=1, source_target_pairs={{0,8},{8,0},{16,24},{24,16},{32,40},{40,32},{48,56},{56,48},{64,72... | collective-permute-start | bytes 786440 | tf_op jit(solution)/shard_map/ppermute | solution.py:563
  58.7 1.7 %collective-permute-start.9 = (bf16[512,256]{1,0:T(8,128)(2,1)}, bf16[512,256]{1,0:T(8,128)(2,1)S(1)}, u32[]{:S(2)}, u32[]{:S(2)}) collective-permute-start(bf16[512,256]{1,0:T(8,128)(2,1)} %get-tuple-element.87), channel_id=1, source_target_pairs={{0,8},{8,0},{16,24},{24,16},{32,40},{40,32},{48,56},{56,48},{64,72... | collective-permute-start | bytes 786440 | tf_op jit(solution)/shard_map/ppermute | solution.py:563
  58.8 14.4 %copy-start.4 = (bf16[256,768]{1,0:T(8,128)(2,1)}, bf16[256,768]{1,0:T(8,128)(2,1)S(1)}, u32[]{:S(2)}) copy-start(bf16[256,768]{1,0:T(8,128)(2,1)S(1)} %collective-permute-done.8.gr_ref) | copy-start | bytes 1179652
  60.1 13.2 %copy-start.1 = (bf16[512,256]{1,0:T(8,128)(2,1)}, bf16[512,256]{1,0:T(8,128)(2,1)S(1)}, u32[]{:S(2)}) copy-start(bf16[512,256]{1,0:T(8,128)(2,1)S(1)} %collective-permute-done.7.xr_ref.refs_1_) | copy-start | bytes 786436
  60.5 12.8 %copy-start.6 = (bf16[512,256]{1,0:T(8,128)(2,1)}, bf16[512,256]{1,0:T(8,128)(2,1)S(1)}, u32[]{:S(2)}) copy-start(bf16[512,256]{1,0:T(8,128)(2,1)S(1)} %collective-permute-done.9.xcr_ref) | copy-start | bytes 786436
  73.3 25.3 %all-to-all-start.2 = ((bf16[8,784,128]{2,1,0:T(8,128)(2,1)}), bf16[8,784,128]{2,1,0:T(8,128)(2,1)S(1)}, u32[]{:S(2)}, u32[]{:S(2)}) async-start(bf16[8,784,128]{2,1,0:T(8,128)(2,1)} %get-tuple-element.94), calls=%async_computation.2 | async-start | bytes 3211264 | tf_op jit(solution)/shard_map/all_to_all | solution.py:559
  85.3 10.1 %collective-permute-start.10 = (bf16[896,256]{1,0:T(8,128)(2,1)}, bf16[896,256]{1,0:T(8,128)(2,1)S(1)}, u32[]{:S(2)}, u32[]{:S(2)}) collective-permute-start(bf16[896,256]{1,0:T(8,128)(2,1)} %get-tuple-element.95), channel_id=1, source_target_pairs={{0,8},{8,0},{16,24},{24,16},{32,40},{40,32},{48,56},{56,48},{64,72... | collective-permute-start | bytes 1376264 | tf_op jit(solution)/shard_map/ppermute | solution.py:563
  85.3 10.1 %collective-permute-start.11 = (bf16[256,768]{1,0:T(8,128)(2,1)}, bf16[256,768]{1,0:T(8,128)(2,1)S(1)}, u32[]{:S(2)}, u32[]{:S(2)}) collective-permute-start(bf16[256,768]{1,0:T(8,128)(2,1)} %get-tuple-element.110.dq_ref), channel_id=1, source_target_pairs={{0,8},{8,0},{16,24},{24,16},{32,40},{40,32},{48,56},{56,48},{64,72... | collective-permute-start | bytes 1179656 | tf_op jit(solution)/shard_map/ppermute | solution.py:563
  95.1 11.4 %collective-permute-start.13 = (bf16[256,2304]{1,0:T(8,128)(2,1)}, bf16[256,2304]{1,0:T(8,128)(2,1)}, u32[]{:S(2)}, u32[]{:S(2)}) collective-permute-start(bf16[256,2304]{1,0:T(8,128)(2,1)} %get-tuple-element.112.dc_ref), channel_id=1, source_target_pairs={{0,8},{8,0},{16,24},{24,16},{32,40},{40,32},{48,56},{56,48},{64,72... | collective-permute-start | bytes 3538952 | tf_op jit(solution)/shard_map/ppermute | solution.py:563
  95.4 7.4 %copy-start.5 = (bf16[256,768]{1,0:T(8,128)(2,1)}, bf16[256,768]{1,0:T(8,128)(2,1)S(1)}, u32[]{:S(2)}) copy-start(bf16[256,768]{1,0:T(8,128)(2,1)S(1)} %collective-permute-done.11.dqr_ref) | copy-start | bytes 1179652
  95.4 7.4 %copy-start.2 = (bf16[896,256]{1,0:T(8,128)(2,1)}, bf16[896,256]{1,0:T(8,128)(2,1)S(1)}, u32[]{:S(2)}) copy-start(bf16[896,256]{1,0:T(8,128)(2,1)S(1)} %collective-permute-done.10.nr_ref) | copy-start | bytes 1376260
  102.8 9.2 %collective-permute-start.12 = (bf16[256,1536]{1,0:T(8,128)(2,1)}, bf16[256,1536]{1,0:T(8,128)(2,1)S(1)}, u32[]{:S(2)}, u32[]{:S(2)}) collective-permute-start(bf16[256,1536]{1,0:T(8,128)(2,1)} %get-tuple-element.104.dkv_ref.refs_2_), channel_id=1, source_target_pairs={{0,8},{8,0},{16,24},{24,16},{32,40},{40,32},{48,56},{56,48},{64,72... | collective-permute-start | bytes 2359304 | tf_op jit(solution)/shard_map/ppermute | solution.py:563
  102.9 14.5 %all-to-all-start.3 = ((bf16[16,16,768]{2,1,0:T(8,128)(2,1)}), bf16[16,16,768]{2,1,0:T(8,128)(2,1)S(1)}, u32[]{:S(2)}, u32[]{:S(2)}) async-start(bf16[16,16,768]{2,1,0:T(8,128)(2,1)} %bitcast.7), calls=%async_computation.3 | async-start | bytes 786432 | tf_op jit(solution)/shard_map/all_to_all | solution.py:559
  115.8 10.6 %copy-start.8 = (f32[2,12,256]{2,1,0:T(8,128)S(1)}, f32[2,12,256]{2,1,0:T(8,128)}, u32[]{:S(2)}) copy-start(f32[2,12,256]{2,1,0:T(8,128)} %get-tuple-element.121) | copy-start | bytes 73732
  115.8 11.6 %copy-start.9 = (f32[2,24,128]{2,1,0:T(8,128)S(1)}, f32[2,24,128]{2,1,0:T(8,128)}, u32[]{:S(2)}) copy-start(f32[2,24,128]{2,1,0:T(8,128)} %get-tuple-element.120) | copy-start | bytes 73732
  117.4 43.7 %all-to-all-start.4 = ((bf16[64,8,2432]{2,1,0:T(8,128)(2,1)}), bf16[64,8,2432]{2,1,0:T(8,128)(2,1)S(1)}, u32[]{:S(2)}, u32[]{:S(2)}) async-start(bf16[64,8,2432]{2,1,0:T(8,128)(2,1)} %shard_map.149), calls=%async_computation.4 | async-start | bytes 4980736 | tf_op jit(solution)/shard_map/all_to_all | solution.py:559
  (2 other events, 9.9 us)

commit v6 on v5

--- a/solution.py
+++ b/solution.py
@@ -508,25 +508,30 @@
         gd_ref[d] = gdp_ref[d] + nn(total.astype(BF), before)[: 2 * HEADS] + through
 
 
+def weight_out_kernel(nk_ref, nr_ref, g_ref, gr_ref, out_ref, gain_ref):
+    normed = jnp.concatenate([nk_ref[SPLIT:, :], nr_ref[SPLIT:, :]], axis=1)
+    gain_terms = jnp.concatenate([nk_ref[0:SPLIT, :], nr_ref[0:SPLIT, :]], axis=1)
+    for start in range(0, D, 256):
+        part = slice(start, start + 256)
+        out_ref[:, part] = nn(normed, jnp.concatenate([g_ref[:, part], gr_ref[:, part]], axis=0)).astype(BF)
+    gain_ref[...] = nn(gain_terms, jnp.ones((2 * TOK, 128), BF)).astype(BF)
+
+
 def weight_early_kernel(
-    xk_ref, xr_ref, xck_ref, xcr_ref, dq_ref, dqr_ref, dc_ref, dcr_ref, nk_ref, nr_ref, g_ref, gr_ref, out_ref
+    xk_ref, xr_ref, xck_ref, xcr_ref, dq_ref, dqr_ref, dc_ref, dcr_ref, ow_ref, gain_ref, out_ref
 ):
     x = jnp.concatenate([xk_ref[...], xr_ref[...]], axis=1)
     xc = jnp.concatenate([xck_ref[...], xcr_ref[...]], axis=1)
-    normed = jnp.concatenate([nk_ref[SPLIT:, :], nr_ref[SPLIT:, :]], axis=1)
-    gain_terms = jnp.concatenate([nk_ref[0:SPLIT, :], nr_ref[0:SPLIT, :]], axis=1)
     expand = place_thirds()
-    for start in range(0, D, 256):
-        part = slice(start, start + 256)
-        out_weight = nn(normed, jnp.concatenate([g_ref[:, part], gr_ref[:, part]], axis=0)).astype(BF)
-        for b in range(3):
-            cols = slice(b * D + start, b * D + start + 256)
-            total = nn(expand, out_weight[b * 128 : (b + 1) * 128])
-            total = total + nn(xc, jnp.concatenate([dc_ref[:, cols], dcr_ref[:, cols]], axis=0))
-            if b == 0:
-                total = total + nn(x, jnp.concatenate([dq_ref[:, cols], dqr_ref[:, cols]], axis=0))
-            out_ref[:, cols] = total.astype(BF)
-    out_ref[:, F:] = nn(gain_terms, jnp.ones((2 * TOK, 128), BF)).astype(BF)
+    for start in range(0, F, 256):
+        b, part = start // D, slice(start % D, start % D + 256)
+        cols = slice(start, start + 256)
+        total = nn(expand, ow_ref[b * 128 : (b + 1) * 128, part])
+        total = total + nn(xc, jnp.concatenate([dc_ref[:, cols], dcr_ref[:, cols]], axis=0))
+        if b == 0:
+            total = total + nn(x, jnp.concatenate([dq_ref[:, cols], dqr_ref[:, cols]], axis=0))
+        out_ref[:, cols] = total.astype(BF)
+    out_ref[:, F:] = gain_ref[...]
 
 
 def weight_late_kernel(xk_ref, xr_ref, dkv_ref, dkvr_ref, early_ref, out_ref):
@@ -643,7 +648,10 @@
         after(rx2, dm), col_out, dn_c, gain, qkv_c, wc, probs_c, w_qkv, near=(0, 3),
     )
     dqkv_c_far = swap(dqkv_c)
-    adj, n_far, dq_far, tok_c = lax.optimization_barrier((adj, n_far, dq_far, tok_c))
+    out_weight, gain_weight = call(
+        weight_out_kernel, 0.1, [((D // 2, D), BF), ((SPLIT, 128), BF)], n_keep, n_far, g, g_far
+    )
+    adj, out_weight, dq_far = lax.optimization_barrier((adj, out_weight, dq_far))
     rx3 = exchange(tok_c.reshape(16, 16, D), "row")
     dkv, gdr = call(
         row_finish_kernel, 0.3,
@@ -655,7 +663,7 @@
     (early,) = call(
         weight_early_kernel, 0.3,
         [((SPLIT, WIDE), BF)],
-        x_keep, x_far, xc_keep, xc_far, after(dq, dkv), dq_far, dqkv_c, dqkv_c_far, n_keep, n_far, g, g_far,
+        x_keep, x_far, xc_keep, xc_far, after(dq, dkv), dq_far, dqkv_c, dqkv_c_far, out_weight, gain_weight,
         keep=(0,),
     )
     (wg,) = call(

time: 163 us -> 164 us (level)
  waiting for transfers between devices: 46.8 us -> 44.4 us
  Pallas kernels: 69.6 us -> 71.9 us
    all_to_all x5, waiting for transfers between devices: 45.1 us -> 42.7 us  [exchange(): return lax.all_to_all(x, axis, 0, 0, tiled=True, axis_index_groups=groups)]
    pallas_call x15 -> x16, Pallas kernels: 69.6 us -> 71.9 us  [call(): pl.pallas_call(kernel, out_shape=[(pltpu.VMEM if n in keep else pltpu.HBM...]
  transfers between devices with their start and end apart: 19 -> 19, of which waited for: 7 -> 6; matrix products, arithmetic and copies ran while one was open for 1% -> 1% of each run, Pallas kernels for 38% -> 40%
where the time goes in v6:
time: 164 us; the launch traced here: 163 us
  Pallas kernels  71.9 us (44%)
  waiting for transfers between devices  44.4 us (27%)
  starting transfers between devices  42.9 us (26%)
  local copies, waits for them, and re-layouts  3.07 us (2%)
    pallas_call x16, Pallas kernels, call(): pl.pallas_call(kernel, out_shape=[(pltpu.VMEM if n in keep else pltpu.HBM...  71.9 us
    all_to_all x5, waiting for transfers between devices, exchange(): return lax.all_to_all(x, axis, 0, 0, tiled=True, axis_index_groups=groups)  42.7 us
    all_to_all x5, starting transfers between devices, exchange(): return lax.all_to_all(x, axis, 0, 0, tiled=True, axis_index_groups=groups)  29.7 us
    ppermute x7, starting transfers between devices, per_device(): lax.ppermute(u, 'col', [(i, (i + n + 1) % 8) for i in range(8)])  11.5 us
  transfers between devices with their start and end apart: 19, of which 6 were waited for; matrix products, arithmetic and copies ran while one was open for 1% of the time, Pallas kernels for 40%

profile of v6, /device:TPU:0, one launch (start us, length us, event | category | flops | bytes accessed | tf_op | source)
XLA Modules:
  0.0 163.3 jit_solution(7204726522851951297)
XLA Ops:
  0.6 2.1 %shard_map.136 = bf16[16,32,768]{2,1,0:T(8,128)(2,1)} custom-call(bf16[2,128,768]{2,1,0:T(8,128)(2,1)} %x_ref.1, bf16[2,128,768]{2,1,0:T(8,128)(2,1)} %g_ref.1), custom_call_target="tpu_custom_call" | custom-call | flops 2200000000 | bytes 7200000 | tf_op jit(solution)/shard_map/pallas_call | solution.py:77
  2.7 8.3 %all-to-all-start = ((bf16[16,32,768]{2,1,0:T(8,128)(2,1)}), bf16[16,32,768]{2,1,0:T(8,128)(2,1)S(1)}, u32[]{:S(2)}, u32[]{:S(2)}) async-start(bf16[16,32,768]{2,1,0:T(8,128)(2,1)} %shard_map.136), calls=%async_computation | async-start | bytes 1572864 | tf_op jit(solution)/shard_map/all_to_all | solution.py:564
  11.1 4.7 %shard_map.137 = (f32[2,128,48]{2,1,0:T(8,128)}, f32[2,16,128]{2,1,0:T(8,128)}, bf16[256,1536]{1,0:T(8,128)(2,1)}, bf16[784,128]{1,0:T(8,128)(2,1)}, bf16[784,12...) custom-call(s32[1]{0:T(128)} %bitcast.1.refs_0_.place_ref, ...), custom_call_target="tpu_custom_call" | custom-call | flops 110000000 | bytes 360000 | tf_op jit(solution)/shard_map/pallas_call | solution.py:77
  15.8 1.6 collective-permute-start
  17.4 2.7 %collective-permute-start.1 = (bf16[784,128]{1,0:T(8,128)(2,1)}, bf16[784,128]{1,0:T(8,128)(2,1)S(1)}, u32[]{:S(2)}, u32[]{:S(2)}) collective-permute-start(bf16[784,128]{1,0:T(8,128)(2,1)} %get-tuple-element.74), channel_id=1, source_target_pairs={{0,2},{1,3},{2,4},{3,5},{4,6},{5,7},{6,0},{7,1},{8,10},{9,11},{10,... | collective-permute-start | bytes 602120 | tf_op jit(solution)/shard_map/ppermute | solution.py:602
  20.1 1.6 collective-permute-start.2
  21.7 1.3 collective-permute-start.3
  24.3 3.5 %shard_map.138 = (bf16[12,256,128]{2,1,0:T(8,128)(2,1)}, bf16[6,512,256]{2,1,0:T(8,128)(2,1)}) custom-call(bf16[2,2,12,128]{3,2,1,0:T(8,128)(2,1)S(1)} %bitcast.22, bf16[2,12,256]{2,1,0:T(8,128)(2,1)S(1)} %reshape.63.refs_1_, s32[2,128]{1,0:T(2,128)S(1)} %constant_dynamic-slice_fusion.refs_2_, s32[1,256]{1,0:T(1,128)S(1)} %reshape.56.refs_3_, ...), custom_call_target="tpu_custom_call" | custom-call | flops 110000000 | bytes 360000 | tf_op jit(solution)/shard_map/pallas_call | solution.py:77
  27.8 2.9 %collective-permute-start.5 = (bf16[784,128]{1,0:T(8,128)(2,1)}, bf16[784,128]{1,0:T(8,128)(2,1)S(1)}, u32[]{:S(2)}, u32[]{:S(2)}) collective-permute-start(bf16[784,128]{1,0:T(8,128)(2,1)} %get-tuple-element.82), channel_id=1, source_target_pairs={{0,6},{1,7},{2,0},{3,1},{4,2},{5,3},{6,4},{7,5},{8,14},{9,15},{10,... | collective-permute-start | bytes 602120 | tf_op jit(solution)/shard_map/ppermute | solution.py:602
  30.7 5.0 %shard_map.139 = (bf16[256,768]{1,0:T(8,128)(2,1)}, f32[256,768]{1,0:T(8,128)}, bf16[12,256,128]{2,1,0:T(8,128)(2,1)}) custom-call(bf16[256,768]{1,0:T(8,128)(2,1)} %bitcast.24, bf16[768,2304]{1,0:T(8,128)(2,1)} %w_ref.3, bf16[256,1536]{1,0:T(8,128)(2,1)} %get-tuple-element.68.refs_2_.kv_ref.refs_1_, bf16[12,256,128]{2,1,0:T(8,128)(2,1)} %get-tuple-element.70.refs_3_.wr_ref), custom_call_target="tpu_custom_call" | custom-call | flops 110000000 | bytes 360000 | tf_op jit(solution)/shard_map/pallas_call | solution.py:77
  36.5 2.8 %all-to-all-done.refs_0_.rx_ref = bf16[16,32,768]{2,1,0:T(8,128)(2,1)S(1)} async-done(((bf16[16,32,768]{2,1,0:T(8,128)(2,1)}), bf16[16,32,768]{2,1,0:T(8,128)(2,1)S(1)}, u32[]{:S(2)}, u32[]{:S(2)}) %all-to-all-start) | async-done | bytes 786464 | tf_op jit(solution)/shard_map/all_to_all | solution.py:564
  39.3 5.9 %shard_map.140 = (bf16[256,2304]{1,0:T(8,128)(2,1)}, bf16[256,768]{1,0:T(8,128)(2,1)}, bf16[6,512,256]{2,1,0:T(8,128)(2,1)}) custom-call(bf16[16,32,768]{2,1,0:T(8,128)(2,1)S(1)} %all-to-all-done.refs_0_.rx_ref, bf16[768,2304]{1,0:T(8,128)(2,1)} %w_ref.3, bf16[6,512,256]{2,1,0:T(8,128)(2,1)} %get-tuple-element.76.refs_2_.wc_ref), custom_call_target="tpu_custom_call" | custom-call | flops 7480000000 | bytes 24480000 | tf_op jit(solution)/shard_map/pallas_call | solution.py:77
  45.3 3.6 %shard_map.141 = (bf16[256,768]{1,0:T(8,128)(2,1)}, bf16[16,32,768]{2,1,0:T(8,128)(2,1)}, bf16[2,768,128]{2,1,0:T(8,128)(2,1)}) custom-call(s32[1]{0:T(128)} %bitcast.1.refs_0_.place_ref, bf16[256,768]{1,0:T(8,128)(2,1)} %get-tuple-element.71.refs_1_.q_ref, f32[2,128,48]{2,1,0:T(8,128)} %get-tuple-element.72.refs_2_.fac_ref.refs_4_, ...), custom_call_target="tpu_custom_call" | custom-call | flops 5500000256 | bytes 18000000 | tf_op jit(solution)/shard_map/pallas_call | solution.py:77
  48.9 5.1 %all-to-all-start.1 = ((bf16[16,32,768]{2,1,0:T(8,128)(2,1)}), bf16[16,32,768]{2,1,0:T(8,128)(2,1)S(1)}, u32[]{:S(2)}, u32[]{:S(2)}) async-start(bf16[16,32,768]{2,1,0:T(8,128)(2,1)} %get-tuple-element.84), calls=%async_computation.1 | async-start | bytes 1572864 | tf_op jit(solution)/shard_map/all_to_all | solution.py:564
  54.0 4.3 %shard_map.142 = (bf16[256,768]{1,0:T(8,128)(2,1)}, bf16[256,768]{1,0:T(8,128)(2,1)}, bf16[512,256]{1,0:T(8,128)(2,1)}, bf16[512,256]{1,0:T(8,128)(2,1)}, bf16[5...) custom-call(s32[1]{0:T(128)} %bitcast.core_ref, bf16[256,768]{1,0:T(8,128)(2,1)} %bitcast.25, bf16[256,768]{1,0:T(8,128)(2,1)} %bitcast.27, ...), custom_call_target="tpu_custom_call" | custom-call | flops 5500000256 | bytes 18000000 | tf_op jit(solution)/shard_map/pallas_call | solution.py:77
  58.9 1.2 collective-permute-done.7.xr_ref.refs_1_
  60.5 8.7 %all-to-all-done.1.rx_ref = bf16[16,32,768]{2,1,0:T(8,128)(2,1)S(1)} async-done(((bf16[16,32,768]{2,1,0:T(8,128)(2,1)}), bf16[16,32,768]{2,1,0:T(8,128)(2,1)S(1)}, u32[]{:S(2)}, u32[]{:S(2)}) %all-to-all-start.1) | async-done | bytes 786464 | tf_op jit(solution)/shard_map/all_to_all | solution.py:564
  69.2 4.1 %shard_map.143 = (bf16[256,768]{1,0:T(8,128)(2,1)}, bf16[8,784,128]{2,1,0:T(8,128)(2,1)}) custom-call(s32[1]{0:T(128)} %bitcast.1.refs_0_.place_ref, bf16[16,32,768]{2,1,0:T(8,128)(2,1)S(1)} %all-to-all-done.1.rx_ref, bf16[256,768]{1,0:T(8,128)(2,1)} %get-tuple-element.90.row_ref, bf16[256,768]{1,0:T(8,128)(2,1)} %get-tuple-element.91.dn_ref, ...), custom_call_target="tpu_custom_call" | custom-call | flops 4950000128 | bytes 16200000 | tf_op jit(solution)/shard_map/pallas_call | solution.py:77
  73.3 3.6 %all-to-all-start.2 = ((bf16[8,784,128]{2,1,0:T(8,128)(2,1)}), bf16[8,784,128]{2,1,0:T(8,128)(2,1)S(1)}, u32[]{:S(2)}, u32[]{:S(2)}) async-start(bf16[8,784,128]{2,1,0:T(8,128)(2,1)} %get-tuple-element.95), calls=%async_computation.2 | async-start | bytes 3211264 | tf_op jit(solution)/shard_map/all_to_all | solution.py:564
  76.9 8.4 %shard_map.144 = (bf16[256,768]{1,0:T(8,128)(2,1)}, bf16[256,1536]{1,0:T(8,128)(2,1)}, f32[2,24,128]{2,1,0:T(8,128)}, bf16[896,256]{1,0:T(8,128)(2,1)}, bf16[896,256]{1,0:T(8,128)(2,1)}) custom-call(s32[1]{0:T(128)} %bitcast.core_ref, bf16[16,32,768]{2,1,0:T(8,128)(2,1)S(1)} %all-to-all-done.1.rx_ref, bf16[256,768]{1,0:T(8,128)(2,1)} %get-tuple-element.90.row_ref, ...), custom_call_target="tpu_custom_call" | custom-call | flops 9790000128 | bytes 32040000 | tf_op jit(solution)/shard_map/pallas_call | solution.py:77
  85.8 9.3 %shard_map.147 = (bf16[256,2304]{1,0:T(8,128)(2,1)}, f32[2,12,256]{2,1,0:T(8,128)}, bf16[256,768]{1,0:T(8,128)(2,1)}) custom-call(bf16[16,32,768]{2,1,0:T(8,128)(2,1)S(1)} %all-to-all-done.1.rx_ref, bf16[256,768]{1,0:T(8,128)(2,1)} %get-tuple-element.78.refs_4_.col_ref, bf16[256,768]{1,0:T(8,128)(2,1)} %get-tuple-element.105.dn_ref, ...), custom_call_target="tpu_custom_call" | custom-call | flops 10670000128 | bytes 34920000 | tf_op jit(solution)/shard_map/pallas_call | solution.py:77
  95.4 0.8 copy-done.2
  96.2 2.9 %shard_map.145 = (bf16[384,768]{1,0:T(8,128)(2,1)}, bf16[512,128]{1,0:T(8,128)(2,1)}) custom-call(bf16[896,256]{1,0:T(8,128)(2,1)} %get-tuple-element.96.nk_ref, bf16[896,256]{1,0:T(8,128)(2,1)} %copy-done.2, bf16[256,768]{1,0:T(8,128)(2,1)} %bitcast.28, bf16[256,768]{1,0:T(8,128)(2,1)} %copy-done.5), custom_call_target="tpu_custom_call" | custom-call | flops 110000000 | bytes 360000 | tf_op jit(solution)/shard_map/pallas_call | solution.py:77
  99.1 4.4 %shard_map.146 = (bf16[256,1536]{1,0:T(8,128)(2,1)}, f32[2,24,128]{2,1,0:T(8,128)}) custom-call(s32[1]{0:T(128)} %bitcast.1.refs_0_.place_ref, bf16[256,1536]{1,0:T(8,128)(2,1)} %get-tuple-element.68.refs_2_.kv_ref.refs_1_, bf16[2,768,128]{2,1,0:T(8,128)(2,1)} %get-tuple-element.85.s_ref.refs_2_, bf16[8,784,128]{2,1,0:T(8,128)(2,1)S(1)} %all-to-all-done.2.refs_3_, ...), custom_call_target="tpu_custom_call" | custom-call | flops 330000000 | bytes 1080000 | tf_op jit(solution)/shard_map/pallas_call | solution.py:77
  103.8 3.6 %all-to-all-start.3 = ((bf16[16,16,768]{2,1,0:T(8,128)(2,1)}), bf16[16,16,768]{2,1,0:T(8,128)(2,1)S(1)}, u32[]{:S(2)}, u32[]{:S(2)}) async-start(bf16[16,16,768]{2,1,0:T(8,128)(2,1)} %bitcast.7), calls=%async_computation.3 | async-start | bytes 786432 | tf_op jit(solution)/shard_map/all_to_all | solution.py:564
  107.3 4.8 %shard_map.149.refs_4_ = bf16[512,2432]{1,0:T(8,128)(2,1)S(1)} custom-call(bf16[512,256]{1,0:T(8,128)(2,1)} %get-tuple-element.109.xk_ref.refs_0_, bf16[512,256]{1,0:T(8,128)(2,1)} %copy-done.1, bf16[512,256]{1,0:T(8,128)(2,1)} %get-tuple-element.111.xck_ref, bf16[512,256]{1,0:T(8,128)(2,1)} %copy-done.6, bf16[256,768]{1,0:T(8,128)(2,1)} %get-tuple-element.113.dq_ref, ...), custom_call_target="tpu_custom_call" | custom-call | flops 330000000 | bytes 1080000 | tf_op jit(solution)/shard_map/pallas_call | solution.py:77
  112.1 3.7 %shard_map.150 = bf16[64,8,2432]{2,1,0:T(8,128)(2,1)} custom-call(bf16[512,256]{1,0:T(8,128)(2,1)} %get-tuple-element.109.xk_ref.refs_0_, bf16[512,256]{1,0:T(8,128)(2,1)} %copy-done.1, bf16[256,1536]{1,0:T(8,128)(2,1)} %get-tuple-element.103.dkv_ref.refs_2_, bf16[256,1536]{1,0:T(8,128)(2,1)S(1)} %collective-permute-done.12.refs_3_, ...), custom_call_target="tpu_custom_call" | custom-call | flops 330000000 | bytes 1080000 | tf_op jit(solution)/shard_map/pallas_call | solution.py:77
  115.9 2.3 %all-to-all-done.3.rx_ref = bf16[16,16,768]{2,1,0:T(8,128)(2,1)S(1)} async-done(((bf16[16,16,768]{2,1,0:T(8,128)(2,1)}), bf16[16,16,768]{2,1,0:T(8,128)(2,1)S(1)}, u32[]{:S(2)}, u32[]{:S(2)}) %all-to-all-start.3) | async-done | bytes 393248 | tf_op jit(solution)/shard_map/all_to_all | solution.py:564
  118.3 9.2 %all-to-all-start.4 = ((bf16[64,8,2432]{2,1,0:T(8,128)(2,1)}), bf16[64,8,2432]{2,1,0:T(8,128)(2,1)S(1)}, u32[]{:S(2)}, u32[]{:S(2)}) async-start(bf16[64,8,2432]{2,1,0:T(8,128)(2,1)} %shard_map.150), calls=%async_computation.4 | async-start | bytes 4980736 | tf_op jit(solution)/shard_map/all_to_all | solution.py:564
  129.2 4.2 %shard_map.148 = bf16[256,768]{1,0:T(8,128)(2,1)} custom-call(bf16[256,768]{1,0:T(8,128)(2,1)} %get-tuple-element.113.dq_ref, bf16[256,1536]{1,0:T(8,128)(2,1)} %get-tuple-element.103.dkv_ref.refs_2_, bf16[768,2304]{1,0:T(8,128)(2,1)} %w_ref.3, bf16[16,16,768]{2,1,0:T(8,128)(2,1)S(1)} %all-to-all-done.3.rx_ref), custom_call_target="tpu_custom_call" | custom-call | flops 4400000000 | bytes 14400000 | tf_op jit(solution)/shard_map/pallas_call | solution.py:77
  133.4 28.9 %all-to-all-done.4.rx_ref = bf16[64,8,2432]{2,1,0:T(8,128)(2,1)S(1)} async-done(((bf16[64,8,2432]{2,1,0:T(8,128)(2,1)}), bf16[64,8,2432]{2,1,0:T(8,128)(2,1)S(1)}, u32[]{:S(2)}, u32[]{:S(2)}) %all-to-all-start.4) | async-done | bytes 2490400 | tf_op jit(solution)/shard_map/all_to_all | solution.py:564
  162.3 1.0 shard_map.151
  (67 shorter events, 5.8 us)
Async XLA Ops:
  0.6 10.4 %copy-start.10 = (bf16[2,12,2,128]{3,2,1,0:T(2,128)(2,1)S(1)}, bf16[2,12,2,128]{3,2,1,0:T(2,128)(2,1)}, u32[]{:S(2)}) copy-start(bf16[2,12,2,128]{3,2,1,0:T(2,128)(2,1)} %param.14) | copy-start | bytes 36868
  2.7 8.3 %copy-start.11 = (s32[1024]{0:T(1024)S(1)}, s32[1024]{0:T(1024)}, u32[]{:S(2)}) copy-start(s32[1024]{0:T(1024)} %param.16) | copy-start | bytes 12292
  2.7 36.6 %all-to-all-start = ((bf16[16,32,768]{2,1,0:T(8,128)(2,1)}), bf16[16,32,768]{2,1,0:T(8,128)(2,1)S(1)}, u32[]{:S(2)}, u32[]{:S(2)}) async-start(bf16[16,32,768]{2,1,0:T(8,128)(2,1)} %shard_map.136), calls=%async_computation | async-start | bytes 1572864 | tf_op jit(solution)/shard_map/all_to_all | solution.py:564
  11.1 12.7 %copy-start.13 = (s32[32]{0:T(128)S(1)}, s32[32]{0:T(128)}, u32[]{:S(2)}) copy-start(s32[32]{0:T(128)} %param.17) | copy-start | bytes 388
  11.1 12.8 %copy-start.7 = (bf16[2,12,8,32]{3,2,1,0:T(8,128)(2,1)S(1)}, bf16[2,12,8,32]{3,2,1,0:T(8,128)(2,1)}, u32[]{:S(2)}) copy-start(bf16[2,12,8,32]{3,2,1,0:T(8,128)(2,1)} %param.15) | copy-start | bytes 36868
  15.8 12.0 %collective-permute-start = (bf16[784,128]{1,0:T(8,128)(2,1)}, bf16[784,128]{1,0:T(8,128)(2,1)S(1)}, u32[]{:S(2)}, u32[]{:S(2)}) collective-permute-start(bf16[784,128]{1,0:T(8,128)(2,1)} %get-tuple-element.67), channel_id=1, source_target_pairs={{0,1},{1,2},{2,3},{3,4},{4,5},{5,6},{6,7},{7,0},{8,9},{9,10},{10,1... | collective-permute-start | bytes 602120 | tf_op jit(solution)/shard_map/ppermute | solution.py:602
  17.4 18.3 %collective-permute-start.1 = (bf16[784,128]{1,0:T(8,128)(2,1)}, bf16[784,128]{1,0:T(8,128)(2,1)S(1)}, u32[]{:S(2)}, u32[]{:S(2)}) collective-permute-start(bf16[784,128]{1,0:T(8,128)(2,1)} %get-tuple-element.74), channel_id=1, source_target_pairs={{0,2},{1,3},{2,4},{3,5},{4,6},{5,7},{6,0},{7,1},{8,10},{9,11},{10,... | collective-permute-start | bytes 602120 | tf_op jit(solution)/shard_map/ppermute | solution.py:602
  20.1 25.1 %collective-permute-start.2 = (bf16[784,128]{1,0:T(8,128)(2,1)}, bf16[784,128]{1,0:T(8,128)(2,1)S(1)}, u32[]{:S(2)}, u32[]{:S(2)}) collective-permute-start(bf16[784,128]{1,0:T(8,128)(2,1)} %get-tuple-element.79), channel_id=1, source_target_pairs={{0,3},{1,4},{2,5},{3,6},{4,7},{5,0},{6,1},{7,2},{8,11},{9,12},{10,... | collective-permute-start | bytes 602120 | tf_op jit(solution)/shard_map/ppermute | solution.py:602
  21.7 23.6 %collective-permute-start.3 = (bf16[784,128]{1,0:T(8,128)(2,1)}, bf16[784,128]{1,0:T(8,128)(2,1)S(1)}, u32[]{:S(2)}, u32[]{:S(2)}) collective-permute-start(bf16[784,128]{1,0:T(8,128)(2,1)} %get-tuple-element.80), channel_id=1, source_target_pairs={{0,4},{1,5},{2,6},{3,7},{4,0},{5,1},{6,2},{7,3},{8,12},{9,13},{10,... | collective-permute-start | bytes 602120 | tf_op jit(solution)/shard_map/ppermute | solution.py:602
  23.0 22.3 %collective-permute-start.4 = (bf16[784,128]{1,0:T(8,128)(2,1)}, bf16[784,128]{1,0:T(8,128)(2,1)S(1)}, u32[]{:S(2)}, u32[]{:S(2)}) collective-permute-start(bf16[784,128]{1,0:T(8,128)(2,1)} %get-tuple-element.81), channel_id=1, source_target_pairs={{0,5},{1,6},{2,7},{3,0},{4,1},{5,2},{6,3},{7,4},{8,13},{9,14},{10,... | collective-permute-start | bytes 602120 | tf_op jit(solution)/shard_map/ppermute | solution.py:602
  27.8 17.5 %collective-permute-start.5 = (bf16[784,128]{1,0:T(8,128)(2,1)}, bf16[784,128]{1,0:T(8,128)(2,1)S(1)}, u32[]{:S(2)}, u32[]{:S(2)}) collective-permute-start(bf16[784,128]{1,0:T(8,128)(2,1)} %get-tuple-element.82), channel_id=1, source_target_pairs={{0,6},{1,7},{2,0},{3,1},{4,2},{5,3},{6,4},{7,5},{8,14},{9,15},{10,... | collective-permute-start | bytes 602120 | tf_op jit(solution)/shard_map/ppermute | solution.py:602
  30.7 5.0 %copy-start.14 = (bf16[784,128]{1,0:T(8,128)(2,1)S(1)}, bf16[784,128]{1,0:T(8,128)(2,1)}, u32[]{:S(2)}) copy-start(bf16[784,128]{1,0:T(8,128)(2,1)} %get-tuple-element.83) | copy-start | bytes 602116
  35.7 9.6 %collective-permute-start.6 = (bf16[784,128]{1,0:T(8,128)(2,1)S(1)}, bf16[784,128]{1,0:T(8,128)(2,1)S(1)}, u32[]{:S(2)}, u32[]{:S(2)}) collective-permute-start(bf16[784,128]{1,0:T(8,128)(2,1)S(1)} %copy-done.14), channel_id=1, source_target_pairs={{0,7},{1,0},{2,1},{3,2},{4,3},{5,4},{6,5},{7,6},{8,15},{9,8},{10,9... | collective-permute-start | bytes 602120 | tf_op jit(solution)/shard_map/ppermute | solution.py:602
  39.3 5.9 %copy-start = (bf16[16,32,768]{2,1,0:T(8,128)(2,1)}, bf16[16,32,768]{2,1,0:T(8,128)(2,1)S(1)}, u32[]{:S(2)}) copy-start(bf16[16,32,768]{2,1,0:T(8,128)(2,1)S(1)} %all-to-all-done.refs_0_.rx_ref) | copy-start | bytes 2359300
  39.3 5.9 %copy-start.4 = (bf16[2,128,768]{2,1,0:T(8,128)(2,1)S(1)}, bf16[2,128,768]{2,1,0:T(8,128)(2,1)}, u32[]{:S(2)}) copy-start(bf16[2,128,768]{2,1,0:T(8,128)(2,1)} %g_ref.1) | copy-start | bytes 1179652
  45.2 13.6 %collective-permute-start.8 = (bf16[256,768]{1,0:T(8,128)(2,1)S(1)}, bf16[256,768]{1,0:T(8,128)(2,1)S(1)}, u32[]{:S(2)}, u32[]{:S(2)}) collective-permute-start(bf16[256,768]{1,0:T(8,128)(2,1)S(1)} %bitcast.29), channel_id=1, source_target_pairs={{0,8},{8,0},{16,24},{24,16},{32,40},{40,32},{48,56},{56,48},{64,72... | collective-permute-start | bytes 1179656 | tf_op jit(solution)/shard_map/ppermute | solution.py:568
  48.9 20.3 %all-to-all-start.1 = ((bf16[16,32,768]{2,1,0:T(8,128)(2,1)}), bf16[16,32,768]{2,1,0:T(8,128)(2,1)S(1)}, u32[]{:S(2)}, u32[]{:S(2)}) async-start(bf16[16,32,768]{2,1,0:T(8,128)(2,1)} %get-tuple-element.84), calls=%async_computation.1 | async-start | bytes 1572864 | tf_op jit(solution)/shard_map/all_to_all | solution.py:564
  54.0 4.9 %copy-start.12 = (f32[768]{0:T(1024)S(1)}, f32[768]{0:T(1024)}, u32[]{:S(2)}) copy-start(f32[768]{0:T(1024)} %param.13) | copy-start | bytes 9220
  58.3 1.8 %collective-permute-start.7 = (bf16[512,256]{1,0:T(8,128)(2,1)}, bf16[512,256]{1,0:T(8,128)(2,1)S(1)}, u32[]{:S(2)}, u32[]{:S(2)}) collective-permute-start(bf16[512,256]{1,0:T(8,128)(2,1)} %get-tuple-element.87), channel_id=1, source_target_pairs={{0,8},{8,0},{16,24},{24,16},{32,40},{40,32},{48,56},{56,48},{64,72... | collective-permute-start | bytes 786440 | tf_op jit(solution)/shard_map/ppermute | solution.py:568
  58.7 1.7 %collective-permute-start.9 = (bf16[512,256]{1,0:T(8,128)(2,1)}, bf16[512,256]{1,0:T(8,128)(2,1)S(1)}, u32[]{:S(2)}, u32[]{:S(2)}) collective-permute-start(bf16[512,256]{1,0:T(8,128)(2,1)} %get-tuple-element.88), channel_id=1, source_target_pairs={{0,8},{8,0},{16,24},{24,16},{32,40},{40,32},{48,56},{56,48},{64,72... | collective-permute-start | bytes 786440 | tf_op jit(solution)/shard_map/ppermute | solution.py:568
  58.8 14.4 %copy-start.5 = (bf16[256,768]{1,0:T(8,128)(2,1)}, bf16[256,768]{1,0:T(8,128)(2,1)S(1)}, u32[]{:S(2)}) copy-start(bf16[256,768]{1,0:T(8,128)(2,1)S(1)} %collective-permute-done.8.gr_ref) | copy-start | bytes 1179652
  60.1 13.2 %copy-start.1 = (bf16[512,256]{1,0:T(8,128)(2,1)}, bf16[512,256]{1,0:T(8,128)(2,1)S(1)}, u32[]{:S(2)}) copy-start(bf16[512,256]{1,0:T(8,128)(2,1)S(1)} %collective-permute-done.7.xr_ref.refs_1_) | copy-start | bytes 786436
  60.5 12.8 %copy-start.6 = (bf16[512,256]{1,0:T(8,128)(2,1)}, bf16[512,256]{1,0:T(8,128)(2,1)S(1)}, u32[]{:S(2)}) copy-start(bf16[512,256]{1,0:T(8,128)(2,1)S(1)} %collective-permute-done.9.xcr_ref) | copy-start | bytes 786436
  73.3 25.8 %all-to-all-start.2 = ((bf16[8,784,128]{2,1,0:T(8,128)(2,1)}), bf16[8,784,128]{2,1,0:T(8,128)(2,1)S(1)}, u32[]{:S(2)}, u32[]{:S(2)}) async-start(bf16[8,784,128]{2,1,0:T(8,128)(2,1)} %get-tuple-element.95), calls=%async_computation.2 | async-start | bytes 3211264 | tf_op jit(solution)/shard_map/all_to_all | solution.py:564
  85.3 13.8 %collective-permute-start.11 = (bf16[256,768]{1,0:T(8,128)(2,1)}, bf16[256,768]{1,0:T(8,128)(2,1)S(1)}, u32[]{:S(2)}, u32[]{:S(2)}) collective-permute-start(bf16[256,768]{1,0:T(8,128)(2,1)} %get-tuple-element.113.dq_ref), channel_id=1, source_target_pairs={{0,8},{8,0},{16,24},{24,16},{32,40},{40,32},{48,56},{56,48},{64,72... | collective-permute-start | bytes 1179656 | tf_op jit(solution)/shard_map/ppermute | solution.py:568
  85.3 10.1 %collective-permute-start.10 = (bf16[896,256]{1,0:T(8,128)(2,1)}, bf16[896,256]{1,0:T(8,128)(2,1)S(1)}, u32[]{:S(2)}, u32[]{:S(2)}) collective-permute-start(bf16[896,256]{1,0:T(8,128)(2,1)} %get-tuple-element.97), channel_id=1, source_target_pairs={{0,8},{8,0},{16,24},{24,16},{32,40},{40,32},{48,56},{56,48},{64,72... | collective-permute-start | bytes 1376264 | tf_op jit(solution)/shard_map/ppermute | solution.py:568
  95.1 12.3 %collective-permute-start.13 = (bf16[256,2304]{1,0:T(8,128)(2,1)}, bf16[256,2304]{1,0:T(8,128)(2,1)}, u32[]{:S(2)}, u32[]{:S(2)}) collective-permute-start(bf16[256,2304]{1,0:T(8,128)(2,1)} %get-tuple-element.115.dc_ref), channel_id=1, source_target_pairs={{0,8},{8,0},{16,24},{24,16},{32,40},{40,32},{48,56},{56,48},{64,72... | collective-permute-start | bytes 3538952 | tf_op jit(solution)/shard_map/ppermute | solution.py:568
  103.5 8.6 %collective-permute-start.12 = (bf16[256,1536]{1,0:T(8,128)(2,1)}, bf16[256,1536]{1,0:T(8,128)(2,1)S(1)}, u32[]{:S(2)}, u32[]{:S(2)}) collective-permute-start(bf16[256,1536]{1,0:T(8,128)(2,1)} %get-tuple-element.103.dkv_ref.refs_2_), channel_id=1, source_target_pairs={{0,8},{8,0},{16,24},{24,16},{32,40},{40,32},{48,56},{56,48},{64,72... | collective-permute-start | bytes 2359304 | tf_op jit(solution)/shard_map/ppermute | solution.py:568
  103.8 14.5 %all-to-all-start.3 = ((bf16[16,16,768]{2,1,0:T(8,128)(2,1)}), bf16[16,16,768]{2,1,0:T(8,128)(2,1)S(1)}, u32[]{:S(2)}, u32[]{:S(2)}) async-start(bf16[16,16,768]{2,1,0:T(8,128)(2,1)} %bitcast.7), calls=%async_computation.3 | async-start | bytes 786432 | tf_op jit(solution)/shard_map/all_to_all | solution.py:564
  115.9 11.6 %copy-start.8 = (f32[2,12,256]{2,1,0:T(8,128)S(1)}, f32[2,12,256]{2,1,0:T(8,128)}, u32[]{:S(2)}) copy-start(f32[2,12,256]{2,1,0:T(8,128)} %get-tuple-element.123) | copy-start | bytes 73732
  115.9 12.6 %copy-start.9 = (f32[2,24,128]{2,1,0:T(8,128)S(1)}, f32[2,24,128]{2,1,0:T(8,128)}, u32[]{:S(2)}) copy-start(f32[2,24,128]{2,1,0:T(8,128)} %get-tuple-element.122) | copy-start | bytes 73732
  118.3 44.0 %all-to-all-start.4 = ((bf16[64,8,2432]{2,1,0:T(8,128)(2,1)}), bf16[64,8,2432]{2,1,0:T(8,128)(2,1)S(1)}, u32[]{:S(2)}, u32[]{:S(2)}) async-start(bf16[64,8,2432]{2,1,0:T(8,128)(2,1)} %shard_map.150), calls=%async_computation.4 | async-start | bytes 4980736 | tf_op jit(solution)/shard_map/all_to_all | solution.py:564
  (2 other events, 5.2 us)
